TPU v7x, 768 devices: a whole 4x8x12 slice. The times are simulated.
768 devices in a mesh: dp: 48 (over x, z), feat: 16 (over y, core).
Axes of the slice: x: 4, y: 8, z: 12, core: 2. Of those that a mesh axis runs over, the one named last changes fastest.
Arguments:
- activations: bfloat16 [12288, 8192], P('dp', 'feat'), may hold values from -6 to 6
- cotangent: bfloat16 [12288, 1024], P('dp'), may hold values from -0.053955078 to 0.053955078
- weight: float32 [8192, 1024], P('feat'), may hold values from -0.0625 to 0.0625
- stats_old: float32 [16, 48, 2, 256, 256], P('feat', 'dp'), as said below
- owners: int32 [32, 4], replicated, may hold values from 0 to 47, as said below
- next_acts: bfloat16 [12288, 8192], P('dp', 'feat'), may hold values from -6 to 6
Outputs:
- weight_new: float32 [8192, 1024], P('feat')
- stats_new: float32 [16, 48, 2, 256, 256], P('feat', 'dp')
- next_out: bfloat16 [12288, 1024], P('dp', 'feat')
Inputs may be any that keep to these rules, and one draw needn't show every extreme that they name: `owners`: blocks are grouped by the index of feat that holds their rows (8192 / (256 * 16) row blocks a group); in every group each dp index owns at most 2 blocks, and some dp index owns exactly 2. `stats_old`: every slot holds a symmetric positive definite matrix; slots that no block maps to are not read.
All inputs are finite; a program needn't handle non-finite values.
Results may differ from a plain program's by a relative error of at most 0.02.
Values may be sent and summed in bfloat16 or wider, within the bound.
No kernel may reach another device: no remote copies, remote signals or barrier semaphores. Data moves between devices by JAX's collectives and lax.ppermute only.
A program may use at most 128 MiB of HBM per device.

v0:
```python
import jax
import jax.numpy as jnp
from jax import lax
from jax.sharding import Mesh
from jax.sharding import PartitionSpec as P

ITERS = 6
DP = ("dp_0", "dp_1")


decay_rate = 0.9
step_rate = 0.01


def spread(x, axes, root):
    x = jnp.where(lax.axis_index(axes) == root, x, jnp.zeros_like(x))
    for axis in axes:
        x = lax.psum(x, axis)
    return x


def in_blocks(x, dim, devices):
    before, after = (x.shape[:dim], x.shape[dim + 1 :])
    return jnp.moveaxis(x.reshape(*before, devices, -1, *after), dim, 0)


def sum_at_owner(x, axis, dim):
    devices = lax.axis_size(axis)
    tiles = lax.all_to_all(in_blocks(x, dim, devices), axis, 0, 0, tiled=True)
    return jnp.sum(tiles.astype(jnp.float32), axis=0)


def newton_root(stats):
    width = stats.shape[0]
    identity = jnp.eye(width, dtype=jnp.float32)
    norm_value = jnp.sqrt(jnp.sum(stats * stats) + 1e-06)
    matrix = stats / norm_value
    iterate = identity
    for counter in range(ITERS):
        factor = (5.0 * identity - matrix) / 4.0
        factor_low = factor.astype(jnp.bfloat16)
        iterate = jnp.dot(
            iterate.astype(jnp.bfloat16), factor_low, preferred_element_type=jnp.float32
        )
        if counter + 1 < ITERS:
            square = jnp.dot(factor_low, factor_low, preferred_element_type=jnp.float32).astype(
                jnp.bfloat16
            )
            fourth = jnp.dot(square, square, preferred_element_type=jnp.float32).astype(
                jnp.bfloat16
            )
            matrix = jnp.dot(
                fourth, matrix.astype(jnp.bfloat16), preferred_element_type=jnp.float32
            )
    return iterate * norm_value ** (-0.25)


def update_stats(grad_block, old_stats):
    gram = (
        jnp.dot(grad_block, grad_block.T, preferred_element_type=jnp.float32) / grad_block.shape[0]
    )
    return decay_rate * old_stats + (1.0 - decay_rate) * gram


def block_at(matrix, block_id, col_blocks, width):
    row_start = block_id // col_blocks * width
    col_start = block_id % col_blocks * width
    return lax.dynamic_slice(matrix, (row_start, col_start), (width, width))


def as_blocks(matrix, row_blocks, col_blocks, width):
    return (
        matrix.reshape(row_blocks, width, col_blocks, width)
        .transpose(0, 2, 1, 3)
        .reshape(row_blocks * col_blocks, width, width)
    )


def body(activations, cotangent, weight, stats_old, owners, next_acts):
    width = stats_old.shape[-1]
    slots = stats_old.shape[2]
    rows_dev, columns = weight.shape
    row_blocks = rows_dev // width
    col_blocks = columns // width
    block_count = row_blocks * col_blocks
    partial_grad = jnp.einsum(
        "td,tc->dc", activations, cotangent, preferred_element_type=jnp.float32
    )
    summed = lax.psum(partial_grad, DP)
    grad_low = summed.astype(jnp.bfloat16)
    feat_index = lax.axis_index("feat")
    data_index = lax.axis_index(DP)
    own_list = lax.dynamic_slice_in_dim(owners, feat_index * row_blocks, row_blocks, 0).reshape(
        block_count
    )
    is_mine = (own_list == data_index).astype(jnp.int32)
    slot_of = jnp.cumsum(is_mine) - is_mine
    block_ids = jnp.arange(block_count, dtype=jnp.int32)
    slot_pick = jnp.clip(slot_of, 0, slots - 1)
    stats_list = []
    renewed_list = []
    chosen_list = []
    for position in range(slots):
        picked = (is_mine == 1) & (slot_of == position)
        alive = jnp.any(picked)
        chosen = jnp.sum(jnp.where(picked, block_ids, 0))
        grad_block = block_at(grad_low, chosen, col_blocks, width)
        renewed = update_stats(grad_block, stats_old[0, 0, position])
        stats_list.append(jnp.where(alive, renewed, 0.0))
        renewed_list.append(renewed)
        chosen_list.append(chosen)
    root_list = [newton_root(renewed) for renewed in renewed_list]
    new_list = []
    candidates = jnp.stack([root_matrix.astype(jnp.bfloat16) for root_matrix in root_list])
    for position in range(block_count):
        sending = lax.dynamic_index_in_dim(candidates, slot_pick[position], 0, keepdims=False)
        new_list.append(spread(sending, DP, own_list[position]))
    arrived_roots = jnp.stack(new_list)
    grad_blocks = as_blocks(grad_low, row_blocks, col_blocks, width)
    weight_blocks = as_blocks(weight, row_blocks, col_blocks, width)
    updates = jnp.einsum(
        "bij,bjk->bik", arrived_roots, grad_blocks, preferred_element_type=jnp.float32
    )
    new_blocks = weight_blocks - step_rate * updates
    weight_new = (
        new_blocks.reshape(row_blocks, col_blocks, width, width)
        .transpose(0, 2, 1, 3)
        .reshape(rows_dev, columns)
    )
    stats_out = jnp.stack(stats_list)[None, None]
    partial_next = jnp.dot(
        next_acts, weight_new.astype(jnp.bfloat16), preferred_element_type=jnp.float32
    )
    next_out = sum_at_owner(partial_next.astype(jnp.bfloat16), "feat", 1).astype(jnp.bfloat16)
    return (weight_new, stats_out, next_out)


def solution(mesh):
    torus = Mesh(mesh.devices.reshape(4, 12, mesh.shape["feat"]), ("dp_0", "dp_1", "feat"))
    placed = (
        P(DP, "feat"),
        P(DP, None),
        P("feat", None),
        P("feat", DP, None, None, None),
        P(),
        P(DP, "feat"),
    )
    return jax.shard_map(
        body,
        mesh=torus,
        in_specs=placed,
        out_specs=(P("feat", None), P("feat", DP, None, None, None), P(DP, "feat")),
        check_vma=False,
    )
```

profile of v0, /device:TPU:1, one launch (start us, length us, event | category | flops | bytes accessed | tf_op | source)
XLA Modules:
  0.0 521.0 jit_solution(8705509930525440829)
XLA Ops:
  7.2 0.8 constant_dynamic-slice_fusion
  8.5 0.5 broadcast.257
  9.0 0.7 reduce.8
  9.8 0.7 fusion.184
  10.4 0.6 select_reduce_fusion
  16.3 0.7 fusion.185
  17.0 0.7 fusion.186
  27.8 1.4 fusion.187
  29.2 205.7 %all-reduce.9 = bf16[512,1024]{1,0:T(8,128)(2,1)} all-reduce(f32[512,1024]{1,0:T(8,128)S(1)} %fusion.187), channel_id=1, replica_groups=mesh['dp_0'=4,'dp_1'=12,'feat'=16] {'dp_0','dp_1'}, use_global_device_ids=true, to_apply=%region_0.0 | all-reduce | flops 524288 | bytes 3145728 | tf_op jit(solution)/shard_map/psum | solution.py:89
  234.9 2.0 multiply_reduce_fusion.1
  237.6 0.7 select_bitcast_fusion.1
  238.2 0.4 convolution_convert_fusion.28
  239.2 0.4 convolution_convert_fusion.25
  239.7 0.9 multiply_reduce_fusion
  241.4 1.3 select_bitcast_fusion
  242.7 0.4 convolution_convert_fusion.13
  243.7 0.4 convolution_convert_fusion.10
  249.3 0.4 convolution_convert_fusion.22
  250.0 0.4 convolution_convert_fusion.19
  251.0 0.4 convolution_convert_fusion.16
  251.8 0.4 convolution_convert_fusion.7
  252.5 0.4 convolution_convert_fusion.4
  253.4 0.4 convolution_convert_fusion.1
  259.8 1.0 fusion.54
  260.8 0.9 fusion.33
  261.8 93.6 %all-reduce.8.cloned.1.call-done = (bf16[256,256]{1,0:T(8,128)(2,1)}, bf16[256,256]{1,0:T(8,128)(2,1)}, bf16[256,256]{1,0:T(8,128)(2,1)}, bf16[256,256]{1,0:T(8,...) async-done(((bf16[256,256]{1,0:T(8,128)(2,1)}, bf16[256,256]{1,0:T(8,128)(2,1)}, ...) | async-done | bytes 1048592 | tf_op jit(solution)/shard_map/psum | solution.py:18
  355.5 0.8 reshape.92
  356.3 1.1 copy.11
  357.5 3.2 reshape.87
  360.6 2.0 copy.9
  362.6 107.7 %all-reduce.6.cloned.1.call-done = (bf16[1,256,256]{2,1,0:T(8,128)(2,1)}, bf16[1,256,256]{2,1,0:T(8,128)(2,1)}, bf16[1,256,256]{2,1,0:T(8,128)(2,1)}, bf16[1,256...) async-done(((bf16[1,256,256]{2,1,0:T(8,128)(2,1)}, ...) | async-done | bytes 1048592 | tf_op jit(solution)/shard_map/psum | solution.py:18
  470.3 1.0 constant_dynamic-update-slice_fusion.7
  471.3 0.9 constant_dynamic-update-slice_fusion.6
  472.2 0.9 constant_dynamic-update-slice_fusion.5
  473.1 0.9 constant_dynamic-update-slice_fusion.4
  474.0 0.9 constant_dynamic-update-slice_fusion.3
  475.0 0.9 constant_dynamic-update-slice_fusion.2
  475.9 0.9 constant_dynamic-update-slice_fusion.1
  476.8 0.9 constant_dynamic-update-slice_fusion
  477.7 0.5 bitcast_subtract_fusion
  478.2 1.4 copy.12
  479.6 0.5 copy.14
  480.0 0.5 copy-done.5
  480.5 1.3 convolution_convert_fusion
  481.8 14.4 %all-to-all-start = ((bf16[16,256,64]{1,2,0:T(8,128)(2,1)}), bf16[16,256,64]{1,2,0:T(8,128)(2,1)S(1)}, u32[]{:S(2)}, u32[]{:S(2)}) async-start(bf16[16,256,64]{1,2,0:T(8,128)(2,1)} %bitcast.107), calls=%async_computation | async-start | bytes 1048576 | tf_op jit(solution)/shard_map/all_to_all | solution.py:29
  496.2 1.8 maximum_bitcast_fusion
  498.0 15.5 %all-to-all-done = bf16[16,256,64]{1,2,0:T(8,128)(2,1)S(1)} async-done(((bf16[16,256,64]{1,2,0:T(8,128)(2,1)}), bf16[16,256,64]{1,2,0:T(8,128)(2,1)S(1)}, u32[]{:S(2)}, u32[]{:S(2)}) %all-to-all-start) | async-done | bytes 524320 | tf_op jit(solution)/shard_map/all_to_all | solution.py:29
  513.5 0.7 reduce_sum.52
  (38 shorter events, 4.6 us)
Async XLA Ops:
  7.2 20.6 %copy-start = (bf16[256,1024]{1,0:T(8,128)(2,1)S(1)}, bf16[256,1024]{1,0:T(8,128)(2,1)}, u32[]{:S(2)}) copy-start(bf16[256,1024]{1,0:T(8,128)(2,1)} %param.7) | copy-start | bytes 1572868
  7.2 348.3 %all-reduce.8.cloned.1.call-start = ((), (), s32[]{:S(2)}) async-start(), calls=%async_computation.2 | async-start | bytes 2097152 | tf_op jit(solution)/shard_map/psum | solution.py:18
  29.2 205.7 %copy-start.4 = (f32[1,1,2,256,256]{4,3,2,1,0:T(8,128)S(1)}, f32[1,1,2,256,256]{4,3,2,1,0:T(8,128)}, u32[]{:S(2)}) copy-start(f32[1,1,2,256,256]{4,3,2,1,0:T(8,128)} %param.9) | copy-start | bytes 1572868
  234.9 4.8 copy-start.2
  261.8 208.5 %all-reduce.6.cloned.1.call-start = ((), (), s32[]{:S(2)}) async-start(), calls=%async_computation.1 | async-start | bytes 2097152 | tf_op jit(solution)/shard_map/psum | solution.py:18
  470.3 7.4 %copy-start.3 = (bf16[2,4,256,256]{3,2,1,0:T(8,128)(2,1)S(1)}, bf16[2,4,256,256]{3,2,1,0:T(8,128)(2,1)}, u32[]{:S(2)}) copy-start(bf16[2,4,256,256]{3,2,1,0:T(8,128)(2,1)} %copy.11) | copy-start | bytes 3145732
  479.5 1.0 copy-start.5
  480.0 17.9 %copy-start.1 = (f32[64,8,4,256]{3,1,2,0:T(8,128)}, f32[64,8,4,256]{3,1,2,0:T(8,128)S(1)}, u32[]{:S(2)}) copy-start(f32[64,8,4,256]{3,1,2,0:T(8,128)S(1)} %copy.14) | copy-start | bytes 6291460
  481.8 31.7 %all-to-all-start = ((bf16[16,256,64]{1,2,0:T(8,128)(2,1)}), bf16[16,256,64]{1,2,0:T(8,128)(2,1)S(1)}, u32[]{:S(2)}, u32[]{:S(2)}) async-start(bf16[16,256,64]{1,2,0:T(8,128)(2,1)} %bitcast.107), calls=%async_computation | async-start | bytes 1048576 | tf_op jit(solution)/shard_map/all_to_all | solution.py:29
Sparse Core Ops, SparseCore 0:
  261.9 93.5 all-reduce.7
  358.7 111.5 all-reduce.5
where the time goes:
time: 522 us; the launch traced here: 521 us
  waiting for transfers between devices  217 us (42%)
  blocking collectives  206 us (39%)
  between operations  41.2 us (8%)
  local copies, waits for them, and re-layouts  19.8 us (4%)
  starting transfers between devices  14.5 us (3%)
  matrix products  14.3 us (3%)
  other arithmetic  8.6 us (2%)
    psum x1, blocking collectives, body(): summed = lax.psum(partial_grad, DP)  206 us
    psum x2, waiting for transfers between devices, spread(): x = lax.psum(x, axis)  201 us
    all_to_all x1, waiting for transfers between devices, sum_at_owner(): tiles = lax.all_to_all(in_blocks(x, dim, devices), axis, 0, 0, tiled=True)  15.5 us
    all_to_all x1, starting transfers between devices, sum_at_owner(): tiles = lax.all_to_all(in_blocks(x, dim, devices), axis, 0, 0, tiled=True)  14.4 us
  transfers between devices with their start and end apart: 3, of which 3 were waited for; matrix products, arithmetic and copies ran while one was open for 2% of the time, Pallas kernels for 0%

commit v1 on v0

v1 whole, which is shorter than its diff:
```python
import functools

import jax
import jax.numpy as jnp
from jax import lax
from jax.experimental import pallas as pl
from jax.experimental.pallas import tpu as pltpu
from jax.sharding import Mesh
from jax.sharding import PartitionSpec as P

ITERS = 6
DP = ("x", "z")
BF = jnp.bfloat16
F32 = jnp.float32
decay_rate = 0.9
step_rate = 0.01

W = 256
H = W // 2
SENT = 2 * W + 2 * H + 32
VMEM = pltpu.CompilerParams(vmem_limit_bytes=48 * 1024 * 1024)


def place(rows):
    return pl.BlockSpec(memory_space=rows)


IN_VMEM = place(pltpu.VMEM)
IN_SMEM = place(pltpu.SMEM)


def dims(rows, cols):
    return (
        lax.broadcasted_iota(jnp.int32, (rows, cols), 0),
        lax.broadcasted_iota(jnp.int32, (rows, cols), 1),
    )


def mine_and_slot(owners, where, block, cols):
    me, base = where[0], where[1]
    slot = jnp.int32(0)
    for before in range(block):
        slot += (owners[base + before // cols, before % cols] == me).astype(jnp.int32)
    return owners[base + block // cols, block % cols] == me, slot


def grad_kernel(where, owners, acts, cot, stats, out):
    cols = out.shape[0]
    row, col = dims(H, H)
    for i in range(cols):
        out[i, : 2 * W, :] = lax.dot_general(
            acts[...], cot[:, i * W : (i + 1) * W], (((0,), (0,)), ((), ())), preferred_element_type=F32
        ).astype(BF)
        out[i, 2 * W :, :] = jnp.zeros((SENT - 2 * W, W), BF)
        for r in range(2):
            mine, slot = mine_and_slot(owners, where, r * cols + i, cols)

            @pl.when(mine)
            def _(i=i, r=r, slot=slot):
                old = stats[0, 0, jnp.minimum(slot, stats.shape[2] - 1)]
                upper, lower = old[:H, :H], old[H:, H:]
                start = 2 * W + r * H
                out[i, start : start + H, :H] = old[:H, H:].astype(BF)
                out[i, start : start + H, H:] = jnp.where(col >= row, upper, lower).astype(BF)
                diagonal = jnp.sum(jnp.where(row == col, lower, 0.0), axis=0, keepdims=True)
                start = 2 * W + 2 * H + r * 16
                out[i, start : start + 16, :H] = jnp.broadcast_to(diagonal, (16, H)).astype(BF)


def sum_x_kernel(tiles, out):
    total = tiles[0].astype(F32)
    for i in range(1, tiles.shape[0]):
        total += tiles[i].astype(F32)
    out[: total.shape[0], :] = total.astype(BF)
    rest = out.shape[0] - total.shape[0]
    if rest:
        out[total.shape[0] :, :] = jnp.zeros((rest, W), BF)


def sum_z_kernel(tiles, out):
    total = tiles[0].astype(F32)
    for i in range(1, tiles.shape[0]):
        total += tiles[i].astype(F32)
    total = total.astype(BF)
    for i in range(out.shape[0]):
        out[i] = total


def dot(a, b):
    return jnp.dot(a, b, preferred_element_type=F32)


def root_kernel(tile, out):
    row, col = dims(H, H)
    big_row, big_col = dims(W, W)
    identity = (big_row == big_col).astype(F32)
    grads, matrices, iterates, norms = [], [], [], []
    for r in range(2):
        grad = tile[r * W : (r + 1) * W, :]
        packed = tile[2 * W + r * H : 2 * W + (r + 1) * H, :].astype(F32)
        diagonal = tile[2 * W + 2 * H + r * 16 : 2 * W + 2 * H + (r + 1) * 16, :H][:1, :].astype(F32)
        flipped = packed.T
        both, both_t = packed[:, H:], flipped[H:, :]
        upper = jnp.where(col >= row, both, both_t)
        lower = jnp.where(col < row, both, jnp.where(col > row, both_t, jnp.broadcast_to(diagonal, (H, H))))
        old = jnp.concatenate(
            [
                jnp.concatenate([upper, packed[:, :H]], axis=1),
                jnp.concatenate([flipped[:H, :], lower], axis=1),
            ],
            axis=0,
        )
        gram = lax.dot_general(grad, grad, (((1,), (1,)), ((), ())), preferred_element_type=F32) / W
        renewed = decay_rate * old + (1.0 - decay_rate) * gram
        norm = jnp.sqrt(jnp.sum(renewed * renewed, axis=(0, 1), keepdims=True) + 1e-06)
        grads.append(grad)
        matrices.append(renewed / norm)
        norms.append(norm)
        iterates.append(None)
    for step in range(ITERS):
        for r in range(2):
            low = ((5.0 * identity - matrices[r]) / 4.0).astype(BF)
            if step == 0:
                iterates[r] = low.astype(F32)
            else:
                iterates[r] = dot(iterates[r].astype(BF), low)
            if step + 1 < ITERS:
                square = dot(low, low).astype(BF)
                fourth = dot(square, square).astype(BF)
                matrices[r] = dot(fourth, matrices[r].astype(BF))
    for r in range(2):
        scale = lax.rsqrt(jnp.sqrt(norms[r]))
        root = (iterates[r] * scale).astype(BF)
        update = dot(root, grads[r]).astype(BF)
        for i in range(out.shape[0]):
            out[i, r * W : (r + 1) * W, :] = update


def next_kernel(weight, update, acts, weight_new, out):
    new = weight[...] - step_rate * update[0].astype(F32)
    weight_new[...] = new
    out[...] = lax.dot_general(
        new.astype(BF), acts[...], (((0,), (1,)), ((), ())), preferred_element_type=F32
    ).astype(BF)


def stats_kernel(where, owners, grads, stats, out):
    cols = grads.shape[0]
    out[...] = jnp.zeros(out.shape, F32)
    for i in range(cols):
        for r in range(2):
            mine, slot = mine_and_slot(owners, where, r * cols + i, cols)

            @pl.when(mine)
            def _(i=i, r=r, slot=slot):
                at = jnp.minimum(slot, stats.shape[2] - 1)
                grad = grads[i, r * W : (r + 1) * W, :]
                gram = lax.dot_general(grad, grad, (((1,), (1,)), ((), ())), preferred_element_type=F32) / W
                out[0, 0, at] = decay_rate * stats[0, 0, at] + (1.0 - decay_rate) * gram


def call(kernel, out, *args, specs=None):
    return pl.pallas_call(
        kernel,
        out_shape=out,
        in_specs=specs or [IN_VMEM] * len(args),
        out_specs=jax.tree.map(lambda _: IN_VMEM, out),
        compiler_params=VMEM,
    )(*args)


def swap(x, axis):
    return lax.all_to_all(x, axis, 0, 0, tiled=True)


def body(activations, cotangent, weight, stats_old, owners, next_acts):
    n_x, n_z, n_feat = (lax.axis_size(a) for a in ("x", "z", "feat"))
    rows_dev, columns = weight.shape
    tokens = activations.shape[0]
    share = -(-SENT // (8 * n_z)) * 8
    where = jnp.stack([lax.axis_index("x") * n_z + lax.axis_index("z"), lax.axis_index("feat") * (rows_dev // W)])
    shape = jax.ShapeDtypeStruct
    sent = call(
        grad_kernel,
        shape((n_x, SENT, W), BF),
        where,
        owners,
        activations,
        cotangent,
        stats_old,
        specs=[IN_SMEM, IN_SMEM, IN_VMEM, IN_VMEM, IN_VMEM],
    )
    column = call(sum_x_kernel, shape((n_z * share, W), BF), swap(sent, "x"))
    mine = call(sum_z_kernel, shape((n_z, share, W), BF), swap(column.reshape(n_z, share, W), "z"))
    full = swap(mine, "z").reshape(n_z * share, W)
    grads = lax.all_gather(full[: 2 * W], "x", axis=0, tiled=False)
    updates = swap(call(root_kernel, shape((n_x, 2 * W, W), BF), full), "x")
    weight_new, partial_next = pl.pallas_call(
        next_kernel,
        grid=(n_x,),
        in_specs=[
            pl.BlockSpec((rows_dev, W), lambda i: (0, i)),
            pl.BlockSpec((1, rows_dev, W), lambda i: (i, 0, 0)),
            pl.BlockSpec((tokens, rows_dev), lambda i: (0, 0)),
        ],
        out_specs=[
            pl.BlockSpec((rows_dev, W), lambda i: (0, i)),
            pl.BlockSpec((W, tokens), lambda i: (i, 0)),
        ],
        out_shape=[shape((rows_dev, columns), F32), shape((columns, tokens), BF)],
        compiler_params=VMEM,
    )(weight, updates, next_acts)
    tiles = swap(partial_next.reshape(n_feat, columns // n_feat, tokens), "feat")
    next_out = jnp.sum(tiles.astype(F32), axis=0).astype(BF).T
    stats_new = call(
        stats_kernel,
        shape(stats_old.shape, F32),
        where,
        owners,
        grads,
        stats_old,
        specs=[IN_SMEM, IN_SMEM, IN_VMEM, IN_VMEM],
    )
    return (weight_new, stats_new, next_out)


def solution(mesh):
    torus = Mesh(mesh.devices.reshape(4, 12, mesh.shape["feat"]), ("x", "z", "feat"))
    return jax.shard_map(
        body,
        mesh=torus,
        in_specs=(
            P(DP, "feat"),
            P(DP, None),
            P("feat", None),
            P("feat", DP, None, None, None),
            P(),
            P(DP, "feat"),
        ),
        out_specs=(P("feat", None), P("feat", DP, None, None, None), P(DP, "feat")),
        check_vma=False,
    )
```

time: 522 us -> 160 us (0.31)
  the two profiles are of different devices: /device:TPU:1 before, /device:TPU:65 now
where the time goes in v1:
time: 160 us; the launch traced here: 159 us
  blocking collectives  84.9 us (53%)
  waiting for transfers between devices  27.9 us (17%)
  between operations  14.1 us (9%)
  starting transfers between devices  12.4 us (8%)
  Pallas kernels  11.8 us (7%)
  local copies, waits for them, and re-layouts  7.34 us (5%)
    all_to_all x3, blocking collectives, swap(): return lax.all_to_all(x, axis, 0, 0, tiled=True)  84.9 us
    all_to_all x2, waiting for transfers between devices, swap(): return lax.all_to_all(x, axis, 0, 0, tiled=True)  24.3 us
    all_to_all x2, starting transfers between devices, swap(): return lax.all_to_all(x, axis, 0, 0, tiled=True)  12.4 us
    pallas_call x5, Pallas kernels, call(): pl.pallas_call(kernel, out_shape=out, in_specs=specs or [IN_VMEM] * len(a...  9.52 us
    unnamed x15, local copies, waits for them, and re-layouts  6.62 us
    all_gather x1, waiting for transfers between devices, body(): grads = lax.all_gather(full[:2 * W], 'x', axis=0, tiled=False)  3.58 us
  transfers between devices with their start and end apart: 3, of which 3 were waited for; matrix products, arithmetic and copies ran while one was open for 0% of the time, Pallas kernels for 3%

profile of v1, /device:TPU:65, one launch (start us, length us, event | category | flops | bytes accessed | tf_op | source)
XLA Modules:
  0.0 159.2 jit_solution(16297124058391265544)
XLA Ops:
  7.2 0.8 copy.9.owners
  7.9 0.1 pad_add_fusion.where
  8.0 0.0 copy-start
  8.0 1.0 copy-done
  9.1 0.0 copy-start.4
  9.1 1.0 copy-done.4
  10.1 0.0 copy-start.5
  10.1 0.9 copy-done.5
  11.1 2.1 %shard_map.85 = bf16[4,800,256]{2,1,0:T(8,128)(2,1)S(1)} custom-call(s32[2]{0:T(128)S(1)} %pad_add_fusion.where, s32[32,4]{1,0:T(8,128)S(1)} %copy.9.owners, bf16[256,512]{1,0:T(8,128)(2,1)S(1)} %copy-done.5, bf16[256,1024]{1,0:T(8,128)(2,1)S(1)} %copy-done.4, f32[1,1,2,256,256]{4,3,2,1,0:T(8,128)S(1)} %copy-done), custom_call_target="tpu_custom_call" | custom-call | tf_op jit(solution)/shard_map/pallas_call | solution.py:163
  13.1 24.0 %all_to_all.25.tiles = bf16[4,800,256]{2,1,0:T(8,128)(2,1)S(1)} all-to-all(bf16[4,800,256]{2,1,0:T(8,128)(2,1)S(1)} %shard_map.85), channel_id=1, replica_groups=mesh['x'=4,'z'=12,'feat'=16] {'x'}, dimensions={0} | all-to-all | bytes 3276800 | tf_op jit(solution)/shard_map/all_to_all | solution.py:173
  37.2 0.2 shard_map.86
  37.4 36.0 %all_to_all.26.tiles = bf16[12,72,256]{2,1,0:T(8,128)(2,1)S(1)} all-to-all(bf16[12,72,256]{2,1,0:T(8,128)(2,1)S(1)} %bitcast.9), channel_id=1, replica_groups=mesh['x'=4,'z'=12,'feat'=16] {'z'}, dimensions={0} | all-to-all | bytes 884736 | tf_op jit(solution)/shard_map/all_to_all | solution.py:173
  73.4 0.1 shard_map.87
  73.4 24.8 %all_to_all.27 = bf16[12,72,256]{2,1,0:T(8,128)(2,1)S(1)} all-to-all(bf16[12,72,256]{2,1,0:T(8,128)(2,1)S(1)} %shard_map.87), channel_id=1, replica_groups=mesh['x'=4,'z'=12,'feat'=16] {'z'}, dimensions={0} | all-to-all | bytes 884736 | tf_op jit(solution)/shard_map/all_to_all | solution.py:173
  98.3 0.0 copy-start.6
  98.3 5.4 %shard_map.88 = bf16[4,512,256]{2,1,0:T(8,128)(2,1)} custom-call(bf16[864,256]{1,0:T(8,128)(2,1)S(1)} %bitcast.7), custom_call_target="tpu_custom_call" | custom-call | tf_op jit(solution)/shard_map/pallas_call | solution.py:163
  103.7 3.5 %all-to-all-start.3 = ((bf16[4,512,256]{2,1,0:T(8,128)(2,1)}), bf16[4,512,256]{2,1,0:T(8,128)(2,1)S(1)}, u32[]{:S(2)}, u32[]{:S(2)}) async-start(bf16[4,512,256]{2,1,0:T(8,128)(2,1)} %shard_map.88), calls=%async_computation.3 | async-start | bytes 2097152 | tf_op jit(solution)/shard_map/all_to_all | solution.py:173
  107.2 0.0 all-gather.3.cloned.1.call-start
  107.3 0.7 slice.4
  108.0 0.0 all-gather.3.cloned.1.call-update
  108.0 0.0 copy-start.1
  108.0 13.5 %all-to-all-done.3.update = bf16[4,512,256]{2,1,0:T(8,128)(2,1)S(1)} async-done(((bf16[4,512,256]{2,1,0:T(8,128)(2,1)}), bf16[4,512,256]{2,1,0:T(8,128)(2,1)S(1)}, u32[]{:S(2)}, u32[]{:S(2)}) %all-to-all-start.3) | async-done | bytes 1048608 | tf_op jit(solution)/shard_map/all_to_all | solution.py:173
  121.6 0.0 copy-done.6
  121.6 0.0 copy-start.2
  121.6 1.6 copy-done.2
  123.2 2.3 %shard_map.89 = (f32[512,1024]{1,0:T(8,128)}, bf16[1024,256]{1,0:T(8,128)(2,1)}) custom-call(f32[512,1024]{1,0:T(8,128)S(1)} %copy-done.2, bf16[4,512,256]{2,1,0:T(8,128)(2,1)S(1)} %all-to-all-done.3.update, bf16[256,512]{1,0:T(8,128)(2,1)S(1)} %copy-done.6), custom_call_target="tpu_custom_call" | custom-call | tf_op jit(solution)/shard_map/pallas_call | solution.py:198
  125.5 8.9 %all-to-all-start.4 = ((bf16[16,64,256]{2,1,0:T(8,128)(2,1)}), bf16[16,64,256]{2,1,0:T(8,128)(2,1)S(1)}, u32[]{:S(2)}, u32[]{:S(2)}) async-start(bf16[16,64,256]{2,1,0:T(8,128)(2,1)} %bitcast.5), calls=%async_computation.4 | async-start | bytes 1048576 | tf_op jit(solution)/shard_map/all_to_all | solution.py:173
  134.3 3.6 %all-gather.3.cloned.1.call-done = bf16[2048,256]{1,0:T(8,128)(2,1)} async-done(((bf16[512,256]{1,0:T(8,128)(2,1)}), bf16[2048,256]{1,0:T(8,128)(2,1)}) %all-gather.3.cloned.1.call-update) | async-done | bytes 1048592 | tf_op jit(solution)/shard_map/all_gather | solution.py:196
  137.9 0.0 copy-done.1
  137.9 0.0 copy-start.3
  137.9 1.2 copy-done.3
  139.2 1.7 %shard_map.90 = f32[1,1,2,256,256]{4,3,2,1,0:T(8,128)} custom-call(s32[2]{0:T(128)S(1)} %pad_add_fusion.where, s32[32,4]{1,0:T(8,128)S(1)} %copy.9.owners, bf16[4,512,256]{2,1,0:T(8,128)(2,1)S(1)} %bitcast.10, f32[1,1,2,256,256]{4,3,2,1,0:T(8,128)S(1)} %copy-done.1), custom_call_target="tpu_custom_call" | custom-call | tf_op jit(solution)/shard_map/pallas_call | solution.py:163
  140.9 10.8 %all-to-all-done.4 = bf16[16,64,256]{2,1,0:T(8,128)(2,1)S(1)} async-done(((bf16[16,64,256]{2,1,0:T(8,128)(2,1)}), bf16[16,64,256]{2,1,0:T(8,128)(2,1)S(1)}, u32[]{:S(2)}, u32[]{:S(2)}) %all-to-all-start.4) | async-done | bytes 524320 | tf_op jit(solution)/shard_map/all_to_all | solution.py:173
  151.7 0.7 reduce_sum.12
Async XLA Ops:
  8.0 1.0 copy-start
  9.1 1.0 copy-start.4
  10.1 0.9 copy-start.5
  98.3 23.3 %copy-start.6 = (bf16[256,512]{1,0:T(8,128)(2,1)S(1)}, bf16[256,512]{1,0:T(8,128)(2,1)}, u32[]{:S(2)}) copy-start(bf16[256,512]{1,0:T(8,128)(2,1)} %acts.3) | copy-start | bytes 786436
  103.7 17.9 %all-to-all-start.3 = ((bf16[4,512,256]{2,1,0:T(8,128)(2,1)}), bf16[4,512,256]{2,1,0:T(8,128)(2,1)S(1)}, u32[]{:S(2)}, u32[]{:S(2)}) async-start(bf16[4,512,256]{2,1,0:T(8,128)(2,1)} %shard_map.88), calls=%async_computation.3 | async-start | bytes 2097152 | tf_op jit(solution)/shard_map/all_to_all | solution.py:173
  107.2 30.7 %all-gather.3.cloned.1.call-start = ((), (), s32[]{:S(2)}) async-start(), calls=%async_computation.5 | async-start | bytes 1310720 | tf_op jit(solution)/shard_map/all_gather | solution.py:196
  108.0 29.9 %copy-start.1 = (f32[1,1,2,256,256]{4,3,2,1,0:T(8,128)S(1)}, f32[1,1,2,256,256]{4,3,2,1,0:T(8,128)}, u32[]{:S(2)}) copy-start(f32[1,1,2,256,256]{4,3,2,1,0:T(8,128)} %stats.3) | copy-start | bytes 1572868
  121.6 1.6 %copy-start.2 = (f32[512,1024]{1,0:T(8,128)S(1)}, f32[512,1024]{1,0:T(8,128)}, u32[]{:S(2)}) copy-start(f32[512,1024]{1,0:T(8,128)} %weight.1) | copy-start | bytes 6291460
  125.5 26.2 %all-to-all-start.4 = ((bf16[16,64,256]{2,1,0:T(8,128)(2,1)}), bf16[16,64,256]{2,1,0:T(8,128)(2,1)S(1)}, u32[]{:S(2)}, u32[]{:S(2)}) async-start(bf16[16,64,256]{2,1,0:T(8,128)(2,1)} %bitcast.5), calls=%async_computation.4 | async-start | bytes 1048576 | tf_op jit(solution)/shard_map/all_to_all | solution.py:173
  137.9 1.2 copy-start.3
Sparse Core Ops, SparseCore 0:
  111.0 26.8 all-gather.2

commit v2 on v1

v2 whole, which is shorter than its diff:
```python
import jax
import jax.numpy as jnp
from jax import lax
from jax.experimental import pallas as pl
from jax.experimental.pallas import tpu as pltpu
from jax.sharding import Mesh
from jax.sharding import PartitionSpec as P

ITERS = 6
DP = ("x", "zh", "zl")
BF = jnp.bfloat16
F32 = jnp.float32
decay_rate = 0.9
step_rate = 0.01

W = 256
H = W // 2
SENT = 2 * W + 2 * H + 32


def room(mib):
    return pltpu.CompilerParams(vmem_limit_bytes=mib * 1024 * 1024)


IN_VMEM = pl.BlockSpec(memory_space=pltpu.VMEM)
IN_SMEM = pl.BlockSpec(memory_space=pltpu.SMEM)


def dims(rows, cols):
    return (
        lax.broadcasted_iota(jnp.int32, (rows, cols), 0),
        lax.broadcasted_iota(jnp.int32, (rows, cols), 1),
    )


def mine_and_slot(owners, where, block, cols, count):
    me, base = where[0], where[1]
    mine = jnp.int32(0)
    slot = jnp.int32(0)
    for other in range(count):
        held = (owners[other % cols, base + other // cols] == me).astype(jnp.int32)
        slot += jnp.where(other < block, held, 0)
        mine += jnp.where(other == block, held, 0)
    return mine == 1, slot


def grad_kernel(where, owners, acts, cot, stats, out, turned):
    cols = pl.num_programs(0)
    i = pl.program_id(0)
    row, col = dims(H, H)

    @pl.when(i == 0)
    def _():
        turned[...] = acts[...].T

    out[0, : 2 * W, :] = jnp.dot(turned[...], cot[...], preferred_element_type=F32).astype(BF)
    out[0, 2 * W :, :] = jnp.zeros((SENT - 2 * W, W), BF)
    for r in range(2):
        mine, slot = mine_and_slot(owners, where, r * 4 + i, 4, 8)

        @pl.when(mine)
        def _(r=r, slot=slot):
            old = stats[0, 0, jnp.minimum(slot, stats.shape[2] - 1)]
            upper, lower = old[:H, :H], old[H:, H:]
            start = 2 * W + r * H
            out[0, start : start + H, :H] = old[:H, H:].astype(BF)
            out[0, start : start + H, H:] = jnp.where(col >= row, upper, lower).astype(BF)
            diagonal = jnp.sum(jnp.where(row == col, lower, 0.0), axis=0, keepdims=True)
            start = 2 * W + 2 * H + r * 16
            out[0, start : start + 16, :H] = jnp.broadcast_to(diagonal, (16, H)).astype(BF)


def sum_kernel(tiles, out):
    total = tiles[0].astype(F32)
    for i in range(1, tiles.shape[0]):
        total += tiles[i].astype(F32)
    total = total.astype(BF)
    for i in range(out.shape[0]):
        out[i] = total


def dot(a, b):
    return jnp.dot(a, b, preferred_element_type=F32)


def root_kernel(where, tile, weight, own, first, second, third, sent, out):
    row, col = dims(H, H)
    big_row, big_col = dims(W, W)
    identity = (big_row == big_col).astype(F32)
    grads, matrices, iterates, norms = [], [], [], []
    for r in range(2):
        grad = tile[r * W : (r + 1) * W, :]
        packed = tile[2 * W + r * H : 2 * W + (r + 1) * H, :].astype(F32)
        diagonal = tile[2 * W + 2 * H + r * 16 : 2 * W + 2 * H + (r + 1) * 16, :H][:1, :].astype(F32)
        flipped = packed.T
        both, both_t = packed[:, H:], flipped[H:, :]
        upper = jnp.where(col >= row, both, both_t)
        lower = jnp.where(col < row, both, jnp.where(col > row, both_t, jnp.broadcast_to(diagonal, (H, H))))
        old = jnp.concatenate(
            [
                jnp.concatenate([upper, packed[:, :H]], axis=1),
                jnp.concatenate([flipped[:H, :], lower], axis=1),
            ],
            axis=0,
        )
        gram = lax.dot_general(grad, grad, (((1,), (1,)), ((), ())), preferred_element_type=F32) / W
        renewed = decay_rate * old + (1.0 - decay_rate) * gram
        norm = jnp.sqrt(jnp.sum(renewed * renewed, axis=(0, 1), keepdims=True) + 1e-06)
        grads.append(grad)
        matrices.append(renewed / norm)
        norms.append(norm)
        iterates.append(None)
        sent[(2 + r) * W : (3 + r) * W, :] = grad
    for step in range(ITERS):
        for r in range(2):
            low = ((5.0 * identity - matrices[r]) / 4.0).astype(BF)
            if step == 0:
                iterates[r] = low.astype(F32)
            else:
                iterates[r] = dot(iterates[r].astype(BF), low)
            if step + 1 < ITERS:
                square = dot(low, low).astype(BF)
                fourth = dot(square, square).astype(BF)
                matrices[r] = dot(fourth, matrices[r].astype(BF))
    news = []
    for r in range(2):
        root = (iterates[r] * lax.rsqrt(jnp.sqrt(norms[r]))).astype(BF)
        update = dot(root, grads[r]).astype(BF)
        sent[r * W : (r + 1) * W, :] = update
        news.append((weight[r * W : (r + 1) * W, :] - step_rate * update.astype(F32)).astype(BF))
    new = jnp.concatenate(news, axis=0)
    for k, acts in enumerate((own, first, second, third)):
        part = lax.dot_general(new, acts[...], (((0,), (1,)), ((), ())), preferred_element_type=F32).astype(BF)
        plane = (where[2] + (4 - k)) % 4
        out[pl.ds(pl.multiple_of(plane * W, W), W), :] = part


def finish_kernel(where, owners, own, first, second, third, weight, stats, weight_new, stats_new):
    stats_new[...] = jnp.zeros(stats_new.shape, F32)
    for k, part in enumerate((own, first, second, third)):
        column = (where[2] + (4 - k)) % 4
        at = pl.ds(pl.multiple_of(column * W, W), W)
        weight_new[:, at] = weight[:, at] - step_rate * part[: 2 * W, :].astype(F32)
        for r in range(2):
            mine, slot = mine_and_slot(owners, where, r * 4 + column, 4, 8)

            @pl.when(mine)
            def _(r=r, slot=slot, part=part):
                place = jnp.minimum(slot, stats.shape[2] - 1)
                grad = part[(2 + r) * W : (3 + r) * W, :]
                gram = lax.dot_general(grad, grad, (((1,), (1,)), ((), ())), preferred_element_type=F32) / W
                stats_new[0, 0, place] = decay_rate * stats[0, 0, place] + (1.0 - decay_rate) * gram


def call(kernel, out, *args, specs=None):
    return pl.pallas_call(
        kernel,
        out_shape=out,
        in_specs=specs or [IN_VMEM] * len(args),
        out_specs=jax.tree.map(lambda _: IN_VMEM, out),
        compiler_params=room(32),
    )(*args)


def swap(x, axis):
    return lax.all_to_all(x, axis, 0, 0, tiled=True)


def turn(x, axis, by):
    n = lax.axis_size(axis)
    return lax.ppermute(x, axis, [(i, (i + by) % n) for i in range(n)])


def body(activations, cotangent, weight, stats_old, owners, next_acts):
    n_x, n_zh, n_zl, n_feat = (lax.axis_size(a) for a in ("x", "zh", "zl", "feat"))
    rows_dev, columns = weight.shape
    tokens = activations.shape[0]
    x_index = lax.axis_index("x")
    where = jnp.stack(
        [
            (x_index * n_zh + lax.axis_index("zh")) * n_zl + lax.axis_index("zl"),
            lax.axis_index("feat") * (rows_dev // W),
            x_index,
        ]
    )
    owners = owners.T
    shape = jax.ShapeDtypeStruct
    sent = pl.pallas_call(
        grad_kernel,
        grid_spec=pltpu.PrefetchScalarGridSpec(
            num_scalar_prefetch=2,
            grid=(n_x,),
            in_specs=[
                pl.BlockSpec(activations.shape, lambda i, *_: (0, 0)),
                pl.BlockSpec((tokens, W), lambda i, *_: (0, i)),
                pl.BlockSpec(stats_old.shape, lambda i, *_: (0, 0, 0, 0, 0)),
            ],
            out_specs=pl.BlockSpec((1, SENT, W), lambda i, *_: (i, 0, 0)),
            scratch_shapes=[pltpu.VMEM((rows_dev, tokens), BF)],
        ),
        out_shape=shape((n_x, SENT, W), BF),
        compiler_params=room(32),
    )(where, owners, activations, cotangent, stats_old)
    share = SENT // n_zl
    column = call(sum_kernel, shape((1, SENT, W), BF), swap(sent, "x"))
    column, next_acts = lax.optimization_barrier((column, next_acts))
    part = call(sum_kernel, shape((n_zh, share, W), BF), swap(column.reshape(n_zl, share, W), "zl"))
    mine = call(sum_kernel, shape((n_zl, share, W), BF), swap(part, "zh"))
    full = swap(mine, "zl").reshape(SENT, W)
    others = [next_acts] + [turn(next_acts, "x", k) for k in range(1, n_x)]
    moved, partial_next = pl.pallas_call(
        root_kernel,
        grid_spec=pltpu.PrefetchScalarGridSpec(
            num_scalar_prefetch=1,
            grid=(1,),
            in_specs=[
                pl.BlockSpec((SENT, W), lambda i, where: (0, 0)),
                pl.BlockSpec((rows_dev, W), lambda i, where: (0, where[2])),
                *[pl.BlockSpec((tokens, rows_dev), lambda i, where: (0, 0))] * n_x,
            ],
            out_specs=[
                pl.BlockSpec((4 * W, W), lambda i, where: (0, 0)),
                pl.BlockSpec((n_x * W, tokens), lambda i, where: (0, 0)),
            ],
        ),
        out_shape=[shape((4 * W, W), BF), shape((n_x * W, tokens), BF)],
        compiler_params=room(32),
    )(where, full, weight, *others)
    tiles = swap(partial_next.reshape(n_feat, columns // n_feat, tokens), "feat")
    parts = [moved] + [turn(moved, "x", k) for k in range(1, n_x)]
    weight_new, stats_new = call(
        finish_kernel,
        [shape(weight.shape, F32), shape(stats_old.shape, F32)],
        where,
        owners,
        *parts,
        weight,
        stats_old,
        specs=[IN_SMEM, IN_SMEM] + [IN_VMEM] * 6,
    )
    summed = jnp.sum(tiles.astype(F32), axis=0).astype(BF)
    each = n_feat // n_x
    pairs = [
        (x * n_feat + to * each + j, to * n_feat + x * each + j)
        for x in range(n_x)
        for to in range(n_x)
        for j in range(each)
    ]
    next_out = lax.ppermute(summed, ("x", "feat"), pairs).T
    return (weight_new, stats_new, next_out)


def solution(mesh):
    torus = Mesh(mesh.devices.reshape(4, 3, 4, mesh.shape["feat"]), ("x", "zh", "zl", "feat"))
    return jax.shard_map(
        body,
        mesh=torus,
        in_specs=(
            P(DP, "feat"),
            P(DP, None),
            P("feat", None),
            P("feat", DP, None, None, None),
            P(),
            P(DP, "feat"),
        ),
        out_specs=(P("feat", None), P("feat", DP, None, None, None), P(DP, "feat")),
        check_vma=False,
    )
```

time: 160 us -> 155 us (0.969)
  the two profiles are of different devices: /device:TPU:65 before, /device:TPU:1 now
where the time goes in v2:
time: 155 us; the launch traced here: 154 us
  blocking collectives  61.8 us (40%)
  starting transfers between devices  34.6 us (22%)
  waiting for transfers between devices  30.9 us (20%)
  local copies, waits for them, and re-layouts  13.5 us (9%)
  Pallas kernels  11.6 us (7%)
    all_to_all x3, blocking collectives, swap(): return lax.all_to_all(x, axis, 0, 0, tiled=True)  61.8 us
    ppermute x6, waiting for transfers between devices, turn(): return lax.ppermute(x, axis, [(i, (i + by) % n) for i in range(n)])  21.2 us
    all_to_all x2, starting transfers between devices, swap(): return lax.all_to_all(x, axis, 0, 0, tiled=True)  18.4 us
    ppermute x6, starting transfers between devices, turn(): return lax.ppermute(x, axis, [(i, (i + by) % n) for i in range(n)])  15.6 us
    unnamed x39, local copies, waits for them, and re-layouts  13.5 us
    all_to_all x2, waiting for transfers between devices, swap(): return lax.all_to_all(x, axis, 0, 0, tiled=True)  9.64 us
    pallas_call x1, Pallas kernels, body(): pl.pallas_call(root_kernel, grid_spec=pltpu.PrefetchScalarGridSpec(num_sc...  5.4 us
    pallas_call x4, Pallas kernels, call(): pl.pallas_call(kernel, out_shape=out, in_specs=specs or [IN_VMEM] * len(a...  4.31 us
  transfers between devices with their start and end apart: 9, of which 5 were waited for; matrix products, arithmetic and copies ran while one was open for 1% of the time, Pallas kernels for 2%

profile of v2, /device:TPU:1, one launch (start us, length us, event | category | flops | bytes accessed | tf_op | source)
XLA Modules:
  0.0 154.4 jit_solution(11008831181687980736)
XLA Ops:
  0.6 0.1 pad_add_fusion.where
  0.7 0.5 copy-done.16
  1.2 1.0 copy-done.1
  2.3 1.0 copy-done.4
  3.3 0.9 copy-done.5
  4.3 0.7 copy-done.14
  5.0 1.9 %shard_map.85 = bf16[4,800,256]{2,1,0:T(8,128)(2,1)S(1)} custom-call(s32[3]{0:T(128)S(1)} %pad_add_fusion.where, s32[4,32]{1,0:T(4,128)S(1)} %bitcast.11, bf16[256,512]{1,0:T(8,128)(2,1)S(1)} %copy-done.5, bf16[256,1024]{1,0:T(8,128)(2,1)S(1)} %copy-done.4, f32[1,1,2,256,256]{4,3,2,1,0:T(8,128)S(1)} %copy-done.1), custom_call_target="tpu_custom_call" | custom-call | tf_op jit(solution)/shard_map/pallas_call | solution.py:188
  6.9 17.6 %all_to_all.25.tiles = bf16[4,800,256]{2,1,0:T(8,128)(2,1)S(1)} all-to-all(bf16[4,800,256]{2,1,0:T(8,128)(2,1)S(1)} %shard_map.85), channel_id=1, replica_groups=mesh['x'=4,'zh'=3,'zl'=4,'feat'=16] {'x'}, dimensions={0} | all-to-all | bytes 3276800 | tf_op jit(solution)/shard_map/all_to_all | solution.py:166
  24.4 0.2 shard_map.86
  24.6 0.0 copy-start.6
  24.6 0.0 copy-start
  24.7 24.0 %all_to_all.26.tiles = bf16[4,200,256]{2,1,0:T(8,128)(2,1)S(1)} all-to-all(bf16[4,200,256]{2,1,0:T(8,128)(2,1)S(1)} %bitcast.9), channel_id=1, replica_groups=mesh['x'=4,'zh'=3,'zl'=4,'feat'=16] {'zl'}, dimensions={0} | all-to-all | bytes 819200 | tf_op jit(solution)/shard_map/all_to_all | solution.py:166
  48.6 0.1 shard_map.87
  48.7 20.3 %all_to_all.27.tiles = bf16[3,200,256]{2,1,0:T(8,128)(2,1)S(1)} all-to-all(bf16[3,200,256]{2,1,0:T(8,128)(2,1)S(1)} %shard_map.87), channel_id=1, replica_groups=mesh['x'=4,'zh'=3,'zl'=4,'feat'=16] {'zh'}, dimensions={0} | all-to-all | bytes 614400 | tf_op jit(solution)/shard_map/all_to_all | solution.py:166
  69.0 0.8 shard_map.88
  69.8 9.7 %all-to-all-start.3 = ((bf16[4,200,256]{2,1,0:T(8,128)(2,1)}), bf16[4,200,256]{2,1,0:T(8,128)(2,1)S(1)}, u32[]{:S(2)}, u32[]{:S(2)}) async-start(bf16[4,200,256]{2,1,0:T(8,128)(2,1)} %shard_map.88), calls=%async_computation.3 | async-start | bytes 819200 | tf_op jit(solution)/shard_map/all_to_all | solution.py:166
  79.4 2.8 %collective-permute-start.2 = (bf16[256,512]{1,0:T(8,128)(2,1)S(1)}, bf16[256,512]{1,0:T(8,128)(2,1)S(1)}, u32[]{:S(2)}, u32[]{:S(2)}) collective-permute-start(bf16[256,512]{1,0:T(8,128)(2,1)S(1)} %copy-done.6), channel_id=1, source_target_pairs={{0,576},{192,0},{384,192},{576,384},{1,577},{193,1},{385,193},{577... | collective-permute-start | bytes 786440 | tf_op jit(solution)/shard_map/ppermute | solution.py:171
  82.2 3.1 %collective-permute-start.1 = (bf16[256,512]{1,0:T(8,128)(2,1)S(1)}, bf16[256,512]{1,0:T(8,128)(2,1)S(1)}, u32[]{:S(2)}, u32[]{:S(2)}) collective-permute-start(bf16[256,512]{1,0:T(8,128)(2,1)S(1)} %copy-done.6), channel_id=1, source_target_pairs={{0,384},{192,576},{384,0},{576,192},{1,385},{193,577},{385,1},{577... | collective-permute-start | bytes 786440 | tf_op jit(solution)/shard_map/ppermute | solution.py:171
  85.3 1.9 %collective-permute-start = (bf16[256,512]{1,0:T(8,128)(2,1)S(1)}, bf16[256,512]{1,0:T(8,128)(2,1)S(1)}, u32[]{:S(2)}, u32[]{:S(2)}) collective-permute-start(bf16[256,512]{1,0:T(8,128)(2,1)S(1)} %copy-done.6), channel_id=1, source_target_pairs={{0,192},{192,384},{384,576},{576,0},{1,193},{193,385},{385,577},{5... | collective-permute-start | bytes 786440 | tf_op jit(solution)/shard_map/ppermute | solution.py:171
  87.3 0.2 collective-permute-done.2.third
  87.5 0.7 copy-done.8
  88.2 3.3 %collective-permute-done.1.second = bf16[256,512]{1,0:T(8,128)(2,1)S(1)} collective-permute-done((bf16[256,512]{1,0:T(8,128)(2,1)S(1)}, bf16[256,512]{1,0:T(8,128)(2,1)S(1)}, u32[]{:S(2)}, u32[]{:S(2)}) %collective-permute-start.1) | collective-permute-done | bytes 262176 | tf_op jit(solution)/shard_map/ppermute | solution.py:171
  91.5 0.7 copy-done.10
  92.2 6.2 %collective-permute-done.first = bf16[256,512]{1,0:T(8,128)(2,1)S(1)} collective-permute-done((bf16[256,512]{1,0:T(8,128)(2,1)S(1)}, bf16[256,512]{1,0:T(8,128)(2,1)S(1)}, u32[]{:S(2)}, u32[]{:S(2)}) %collective-permute-start) | collective-permute-done | bytes 262176 | tf_op jit(solution)/shard_map/ppermute | solution.py:171
  98.4 0.7 copy-done.12
  99.1 0.0 all-to-all-done.3
  99.1 0.9 copy-done.7
  100.0 0.9 copy-done.9
  101.0 0.9 copy-done.11
  101.9 0.9 copy-done.13
  102.9 0.7 copy-done.17
  103.5 5.4 %shard_map.89 = (bf16[1024,256]{1,0:T(8,128)(2,1)S(1)}, bf16[1024,256]{1,0:T(8,128)(2,1)S(1)}) custom-call(s32[3]{0:T(128)S(1)} %copy-done.17, bf16[800,256]{1,0:T(8,128)(2,1)S(1)} %bitcast.8, f32[512,1024]{1,0:T(8,128)S(1)} %copy-done, bf16[256,512]{1,0:T(8,128)(2,1)S(1)} %copy-done.7, bf16[256,512]{1,0:T(8,128)(2,1)S(1)} %copy-done.13, ...), custom_call_target="tpu_custom_call" | custom-call | tf_op jit(solution)/shard_map/pallas_call | solution.py:211
  108.9 0.0 copy-start.3
  108.9 0.8 copy-done.3
  109.7 8.7 %all-to-all-start.4 = ((bf16[16,64,256]{2,1,0:T(8,128)(2,1)}), bf16[16,64,256]{2,1,0:T(8,128)(2,1)}, u32[]{:S(2)}, u32[]{:S(2)}) async-start(bf16[16,64,256]{2,1,0:T(8,128)(2,1)} %bitcast.10), calls=%async_computation.4 | async-start | bytes 1048576 | tf_op jit(solution)/shard_map/all_to_all | solution.py:166
  118.5 2.2 %collective-permute-start.5 = (bf16[1024,256]{1,0:T(8,128)(2,1)S(1)}, bf16[1024,256]{1,0:T(8,128)(2,1)}, u32[]{:S(2)}, u32[]{:S(2)}) collective-permute-start(bf16[1024,256]{1,0:T(8,128)(2,1)S(1)} %get-tuple-element.11.own), channel_id=1, source_target_pairs={{0,576},{192,0},{384,192},{576,384},{1,577},{193,1},{385,193},{577... | collective-permute-start | bytes 1572872 | tf_op jit(solution)/shard_map/ppermute | solution.py:171
  120.6 3.1 %collective-permute-start.4 = (bf16[1024,256]{1,0:T(8,128)(2,1)S(1)}, bf16[1024,256]{1,0:T(8,128)(2,1)}, u32[]{:S(2)}, u32[]{:S(2)}) collective-permute-start(bf16[1024,256]{1,0:T(8,128)(2,1)S(1)} %get-tuple-element.11.own), channel_id=1, source_target_pairs={{0,384},{192,576},{384,0},{576,192},{1,385},{193,577},{385,1},{577... | collective-permute-start | bytes 1572872 | tf_op jit(solution)/shard_map/ppermute | solution.py:171
  123.7 2.5 %collective-permute-start.3 = (bf16[1024,256]{1,0:T(8,128)(2,1)S(1)}, bf16[1024,256]{1,0:T(8,128)(2,1)}, u32[]{:S(2)}, u32[]{:S(2)}) collective-permute-start(bf16[1024,256]{1,0:T(8,128)(2,1)S(1)} %get-tuple-element.11.own), channel_id=1, source_target_pairs={{0,192},{192,384},{384,576},{576,0},{1,193},{193,385},{385,577},{5... | collective-permute-start | bytes 1572872 | tf_op jit(solution)/shard_map/ppermute | solution.py:171
  126.2 9.6 %all-to-all-done.4 = bf16[16,64,256]{2,1,0:T(8,128)(2,1)} async-done(((bf16[16,64,256]{2,1,0:T(8,128)(2,1)}), bf16[16,64,256]{2,1,0:T(8,128)(2,1)}, u32[]{:S(2)}, u32[]{:S(2)}) %all-to-all-start.4) | async-done | bytes 524320 | tf_op jit(solution)/shard_map/all_to_all | solution.py:166
  135.9 1.1 reduce_sum.12
  137.0 0.7 collective-permute-start.6
  137.7 0.0 collective-permute-done.5.third
  137.7 0.0 collective-permute-done.4.second
  137.7 11.5 %collective-permute-done.3.first = bf16[1024,256]{1,0:T(8,128)(2,1)} collective-permute-done((bf16[1024,256]{1,0:T(8,128)(2,1)S(1)}, bf16[1024,256]{1,0:T(8,128)(2,1)}, u32[]{:S(2)}, u32[]{:S(2)}) %collective-permute-start.3) | collective-permute-done | bytes 524320 | tf_op jit(solution)/shard_map/ppermute | solution.py:171
  149.2 0.7 copy-done.15
  149.9 0.7 copy-done.18
  150.6 3.3 %shard_map.90 = (f32[512,1024]{1,0:T(8,128)}, f32[1,1,2,256,256]{4,3,2,1,0:T(8,128)}) custom-call(s32[3]{0:T(128)S(1)} %copy-done.18, s32[4,32]{1,0:T(4,128)S(1)} %bitcast.12, bf16[1024,256]{1,0:T(8,128)(2,1)S(1)} %get-tuple-element.11.own, bf16[1024,256]{1,0:T(8,128)(2,1)} %collective-permute-done.3.first, bf16[1024,256]{1,0:T(8,128)(2,1)} %collective-permute-done.4.second, ...), custom_call_target="tpu_custom_call" | custom-call | tf_op jit(solution)/shard_map/pallas_call | solution.py:156
  153.8 0.6 copy.10
  (20 shorter events, 0.0 us)
Async XLA Ops:
  0.7 0.5 copy-start.16
  1.2 1.0 copy-start.1
  2.3 1.0 copy-start.4
  3.3 0.9 copy-start.5
  4.3 0.7 copy-start.14
  24.6 54.8 %copy-start.6 = (bf16[256,512]{1,0:T(8,128)(2,1)S(1)}, bf16[256,512]{1,0:T(8,128)(2,1)}, u32[]{:S(2)}) copy-start(bf16[256,512]{1,0:T(8,128)(2,1)} %own) | copy-start | bytes 786436
  24.6 74.4 %copy-start = (f32[512,1024]{1,0:T(8,128)S(1)}, f32[512,1024]{1,0:T(8,128)}, u32[]{:S(2)}) copy-start(f32[512,1024]{1,0:T(8,128)} %weight.3) | copy-start | bytes 6291460
  69.8 29.3 %all-to-all-start.3 = ((bf16[4,200,256]{2,1,0:T(8,128)(2,1)}), bf16[4,200,256]{2,1,0:T(8,128)(2,1)S(1)}, u32[]{:S(2)}, u32[]{:S(2)}) async-start(bf16[4,200,256]{2,1,0:T(8,128)(2,1)} %shard_map.88), calls=%async_computation.3 | async-start | bytes 819200 | tf_op jit(solution)/shard_map/all_to_all | solution.py:166
  79.4 8.0 %collective-permute-start.2 = (bf16[256,512]{1,0:T(8,128)(2,1)S(1)}, bf16[256,512]{1,0:T(8,128)(2,1)S(1)}, u32[]{:S(2)}, u32[]{:S(2)}) collective-permute-start(bf16[256,512]{1,0:T(8,128)(2,1)S(1)} %copy-done.6), channel_id=1, source_target_pairs={{0,576},{192,0},{384,192},{576,384},{1,577},{193,1},{385,193},{577... | collective-permute-start | bytes 786440 | tf_op jit(solution)/shard_map/ppermute | solution.py:171
  82.2 9.3 %collective-permute-start.1 = (bf16[256,512]{1,0:T(8,128)(2,1)S(1)}, bf16[256,512]{1,0:T(8,128)(2,1)S(1)}, u32[]{:S(2)}, u32[]{:S(2)}) collective-permute-start(bf16[256,512]{1,0:T(8,128)(2,1)S(1)} %copy-done.6), channel_id=1, source_target_pairs={{0,384},{192,576},{384,0},{576,192},{1,385},{193,577},{385,1},{577... | collective-permute-start | bytes 786440 | tf_op jit(solution)/shard_map/ppermute | solution.py:171
  85.3 13.0 %collective-permute-start = (bf16[256,512]{1,0:T(8,128)(2,1)S(1)}, bf16[256,512]{1,0:T(8,128)(2,1)S(1)}, u32[]{:S(2)}, u32[]{:S(2)}) collective-permute-start(bf16[256,512]{1,0:T(8,128)(2,1)S(1)} %copy-done.6), channel_id=1, source_target_pairs={{0,192},{192,384},{384,576},{576,0},{1,193},{193,385},{385,577},{5... | collective-permute-start | bytes 786440 | tf_op jit(solution)/shard_map/ppermute | solution.py:171
  87.5 0.7 copy-start.8
  91.5 0.7 copy-start.10
  98.4 0.7 copy-start.12
  99.1 1.0 copy-start.7
  100.0 0.9 copy-start.9
  101.0 0.9 copy-start.11
  101.9 0.9 copy-start.13
  102.9 0.7 copy-start.17
  103.5 45.7 %copy-start.2 = (f32[1,1,2,256,256]{4,3,2,1,0:T(8,128)S(1)}, f32[1,1,2,256,256]{4,3,2,1,0:T(8,128)}, u32[]{:S(2)}) copy-start(f32[1,1,2,256,256]{4,3,2,1,0:T(8,128)} %stats.3) | copy-start | bytes 1572868
  108.9 0.8 copy-start.3
  109.7 26.1 %all-to-all-start.4 = ((bf16[16,64,256]{2,1,0:T(8,128)(2,1)}), bf16[16,64,256]{2,1,0:T(8,128)(2,1)}, u32[]{:S(2)}, u32[]{:S(2)}) async-start(bf16[16,64,256]{2,1,0:T(8,128)(2,1)} %bitcast.10), calls=%async_computation.4 | async-start | bytes 1048576 | tf_op jit(solution)/shard_map/all_to_all | solution.py:166
  118.5 19.2 %collective-permute-start.5 = (bf16[1024,256]{1,0:T(8,128)(2,1)S(1)}, bf16[1024,256]{1,0:T(8,128)(2,1)}, u32[]{:S(2)}, u32[]{:S(2)}) collective-permute-start(bf16[1024,256]{1,0:T(8,128)(2,1)S(1)} %get-tuple-element.11.own), channel_id=1, source_target_pairs={{0,576},{192,0},{384,192},{576,384},{1,577},{193,1},{385,193},{577... | collective-permute-start | bytes 1572872 | tf_op jit(solution)/shard_map/ppermute | solution.py:171
  120.6 17.0 %collective-permute-start.4 = (bf16[1024,256]{1,0:T(8,128)(2,1)S(1)}, bf16[1024,256]{1,0:T(8,128)(2,1)}, u32[]{:S(2)}, u32[]{:S(2)}) collective-permute-start(bf16[1024,256]{1,0:T(8,128)(2,1)S(1)} %get-tuple-element.11.own), channel_id=1, source_target_pairs={{0,384},{192,576},{384,0},{576,192},{1,385},{193,577},{385,1},{577... | collective-permute-start | bytes 1572872 | tf_op jit(solution)/shard_map/ppermute | solution.py:171
  123.7 25.5 %collective-permute-start.3 = (bf16[1024,256]{1,0:T(8,128)(2,1)S(1)}, bf16[1024,256]{1,0:T(8,128)(2,1)}, u32[]{:S(2)}, u32[]{:S(2)}) collective-permute-start(bf16[1024,256]{1,0:T(8,128)(2,1)S(1)} %get-tuple-element.11.own), channel_id=1, source_target_pairs={{0,192},{192,384},{384,576},{576,0},{1,193},{193,385},{385,577},{5... | collective-permute-start | bytes 1572872 | tf_op jit(solution)/shard_map/ppermute | solution.py:171
  137.0 16.8 %collective-permute-start.6 = (bf16[64,256]{1,0:T(8,128)(2,1)S(1)}, bf16[64,256]{1,0:T(8,128)(2,1)S(1)}, u32[]{:S(2)}, u32[]{:S(2)}) collective-permute-start(bf16[64,256]{1,0:T(8,128)(2,1)S(1)} %reduce_sum.12), channel_id=1, source_target_pairs={{0,0},{1,1},{2,2},{3,3},{4,192},{5,193},{6,194},{7,195},{8,384},{9... | collective-permute-start | bytes 98312 | tf_op jit(solution)/shard_map/ppermute | solution.py:249
  149.2 0.7 copy-start.15
  149.9 0.7 copy-start.18

commit v3 on v2

v3 whole, which is shorter than its diff:
```python
import jax
import jax.numpy as jnp
from jax import lax
from jax.experimental import pallas as pl
from jax.experimental.pallas import tpu as pltpu
from jax.sharding import Mesh
from jax.sharding import PartitionSpec as P

ITERS = 6
DP = ("x", "zh", "zl")
BF = jnp.bfloat16
F32 = jnp.float32
decay_rate = 0.9
step_rate = 0.01

W = 256
H = W // 2
PACK = H + 16
EACH = W + PACK
SENT = 2 * EACH


def room(mib):
    return pltpu.CompilerParams(vmem_limit_bytes=mib * 1024 * 1024)


IN_VMEM = pl.BlockSpec(memory_space=pltpu.VMEM)
IN_HBM = pl.BlockSpec(memory_space=pltpu.HBM)


def dims(rows, cols):
    return (
        lax.broadcasted_iota(jnp.int32, (rows, cols), 0),
        lax.broadcasted_iota(jnp.int32, (rows, cols), 1),
    )


def start_copies(pairs, sems):
    copies = [pltpu.make_async_copy(a, b, sems.at[i]) for i, (a, b) in enumerate(pairs)]
    for copy in copies:
        copy.start()
    return copies


def wide(start):
    return pl.ds(pl.multiple_of(start * W, W), W)


def mine_and_slot(owners, block):
    me = (lax.axis_index("x") * 3 + lax.axis_index("zh")) * 4 + lax.axis_index("zl")
    base = lax.axis_index("feat") * 2
    mine = jnp.int32(0)
    slot = jnp.int32(0)
    for other in range(8):
        held = (owners[other % 4, base + other // 4] == me).astype(jnp.int32)
        slot += jnp.where(other < block, held, 0)
        mine += jnp.where(other == block, held, 0)
    return mine == 1, slot


def pack(old, out, start):
    row, col = dims(H, H)
    upper, lower = old[:H, :H], old[H:, H:]
    out[start : start + H, :H] = old[:H, H:].astype(BF)
    out[start : start + H, H:] = jnp.where(col >= row, upper, lower).astype(BF)
    diagonal = jnp.sum(jnp.where(row == col, lower, 0.0), axis=0, keepdims=True)
    out[start + H : start + PACK, :H] = jnp.broadcast_to(diagonal, (PACK - H, H)).astype(BF)
    out[start + H : start + PACK, H:] = jnp.zeros((PACK - H, H), BF)


def unpack(tile, start):
    row, col = dims(H, H)
    packed = tile[start : start + H, :].astype(F32)
    diagonal = tile[start + H : start + PACK, :H][:1, :].astype(F32)
    flipped = packed.T
    both, both_t = packed[:, H:], flipped[H:, :]
    upper = jnp.where(col >= row, both, both_t)
    lower = jnp.where(col < row, both, jnp.where(col > row, both_t, jnp.broadcast_to(diagonal, (H, H))))
    return jnp.concatenate(
        [
            jnp.concatenate([upper, packed[:, :H]], axis=1),
            jnp.concatenate([flipped[:H, :], lower], axis=1),
        ],
        axis=0,
    )


def grad_kernel(owners_in, acts_in, cot_in, stats_in, out, owners, acts, cot, stats, turned, sems):
    copies = start_copies(
        [(acts_in, acts), (owners_in, owners)]
        + [(cot_in.at[:, i * W : (i + 1) * W], cot.at[:, i * W : (i + 1) * W]) for i in range(4)]
        + [(stats_in.at[0, 0, k], stats.at[k]) for k in range(2)],
        sems,
    )
    for r in range(2):
        for i in range(4):
            out[i, r * EACH + W : (r + 1) * EACH, :] = jnp.zeros((PACK, W), BF)
    copies[0].wait()
    turned[...] = acts[...].T
    for i in range(4):
        copies[2 + i].wait()
        part = jnp.dot(turned[...], cot[:, i * W : (i + 1) * W], preferred_element_type=F32).astype(BF)
        for r in range(2):
            out[i, r * EACH : r * EACH + W, :] = part[r * W : (r + 1) * W, :]
    for at in (1, 6, 7):
        copies[at].wait()
    for r in range(2):
        for i in range(4):
            mine, slot = mine_and_slot(owners, r * 4 + i)

            @pl.when(mine)
            def _(i=i, r=r, slot=slot):
                pack(stats[jnp.minimum(slot, 1)], out.at[i], r * EACH + W)


def sum_kernel(tiles, out):
    total = tiles[0].astype(F32)
    for i in range(1, tiles.shape[0]):
        total += tiles[i].astype(F32)
    total = total.astype(BF)
    for i in range(out.shape[0]):
        out[i] = total


def dot(a, b):
    return jnp.dot(a, b, preferred_element_type=F32)


def root_kernel(tile, weight_in, own, first, second, third, sent, out, weight, acts, sems):
    x = lax.axis_index("x")
    copies = start_copies(
        [(weight_in.at[:, wide(x)], weight)]
        + [(part, acts.at[k]) for k, part in enumerate((own, first, second, third))],
        sems,
    )
    big_row, big_col = dims(W, W)
    identity = (big_row == big_col).astype(F32)
    grads, matrices, iterates, norms = [], [], [], []
    for r in range(2):
        grad = tile[r * EACH : r * EACH + W, :]
        old = unpack(tile, r * EACH + W)
        gram = lax.dot_general(grad, grad, (((1,), (1,)), ((), ())), preferred_element_type=F32) / W
        pack(gram, sent, r * EACH + W)
        renewed = decay_rate * old + (1.0 - decay_rate) * gram
        norm = jnp.sqrt(jnp.sum(renewed * renewed, axis=(0, 1), keepdims=True) + 1e-06)
        grads.append(grad)
        matrices.append(renewed / norm)
        norms.append(norm)
        iterates.append(None)
    for step in range(ITERS):
        for r in range(2):
            low = ((5.0 * identity - matrices[r]) / 4.0).astype(BF)
            if step == 0:
                iterates[r] = low.astype(F32)
            else:
                iterates[r] = dot(iterates[r].astype(BF), low)
            if step + 1 < ITERS:
                square = dot(low, low).astype(BF)
                fourth = dot(square, square).astype(BF)
                matrices[r] = dot(fourth, matrices[r].astype(BF))
    for copy in copies:
        copy.wait()
    news = []
    for r in range(2):
        root = (iterates[r] * lax.rsqrt(jnp.sqrt(norms[r]))).astype(BF)
        update = dot(root, grads[r]).astype(BF)
        sent[r * EACH : r * EACH + W, :] = update
        news.append((weight[r * W : (r + 1) * W, :] - step_rate * update.astype(F32)).astype(BF))
    new = jnp.concatenate(news, axis=0)
    for k in range(4):
        part = lax.dot_general(new, acts[k], (((0,), (1,)), ((), ())), preferred_element_type=F32).astype(BF)
        out[wide((x + (4 - k)) % 4), :] = part


def renew(owners, block, packed, start, stats, stats_new):
    mine, slot = mine_and_slot(owners, block)

    @pl.when(mine)
    def _():
        at = jnp.minimum(slot, 1)
        stats_new[at] = decay_rate * stats[at] + (1.0 - decay_rate) * unpack(packed, start)


def finish_kernel(
    owners_in, own, first, second_top, second_low, third, weight_in, stats_in,
    weight_out, stats_out, owners, weight, stats, new, stats_new, sems, out_sems
):
    x = lax.axis_index("x")
    columns = [(x + (4 - k)) % 4 for k in range(4)]
    copies = start_copies(
        [(owners_in, owners)]
        + [(stats_in.at[0, 0, k], stats.at[k]) for k in range(2)]
        + [(weight_in.at[:, wide(c)], weight.at[k]) for k, c in enumerate(columns)],
        sems,
    )
    halves = [[(own, 0), (own, EACH)], [(first, 0), (first, EACH)], [(second_top, 0), (second_low, 0)], [(third, 0), (third, EACH)]]
    sends = []
    for k in range(4):
        copies[3 + k].wait()
        for r, (part, start) in enumerate(halves[k]):
            rows = slice(r * W, (r + 1) * W)
            new[k, rows, :] = weight[k, rows, :] - step_rate * part[start : start + W, :].astype(F32)
        send = pltpu.make_async_copy(new.at[k], weight_out.at[:, wide(columns[k])], out_sems.at[k])
        send.start()
        sends.append(send)
    for at in range(3):
        copies[at].wait()
    stats_new[...] = jnp.zeros(stats_new.shape, F32)
    for k in range(4):
        for r, (part, start) in enumerate(halves[k]):
            renew(owners, r * 4 + columns[k], part, start + W, stats, stats_new)
    send = pltpu.make_async_copy(stats_new, stats_out.at[0, 0], out_sems.at[4])
    send.start()
    sends.append(send)
    for send in sends:
        send.wait()


def call(kernel, out, *args, specs=None, out_specs=None, scratch=(), mib=32):
    return pl.pallas_call(
        kernel,
        out_shape=out,
        in_specs=specs or [IN_VMEM] * len(args),
        out_specs=out_specs or jax.tree.map(lambda _: IN_VMEM, out),
        scratch_shapes=list(scratch),
        compiler_params=room(mib),
    )(*args)


def swap(x, axis):
    return lax.all_to_all(x, axis, 0, 0, tiled=True)


def turn(x, axis, by):
    n = lax.axis_size(axis)
    return lax.ppermute(x, axis, [(i, (i + by) % n) for i in range(n)])


def body(activations, cotangent, weight, stats_old, owners, next_acts):
    n_x, n_zh, n_zl, n_feat = (lax.axis_size(a) for a in ("x", "zh", "zl", "feat"))
    rows_dev, columns = weight.shape
    tokens = activations.shape[0]
    owners = owners.T
    shape = jax.ShapeDtypeStruct
    dma = pltpu.SemaphoreType.DMA
    sent = call(
        grad_kernel,
        shape((n_x, SENT, W), BF),
        owners,
        activations,
        cotangent,
        stats_old,
        specs=[IN_HBM] * 4,
        scratch=[
            pltpu.SMEM(owners.shape, jnp.int32),
            pltpu.VMEM((tokens, rows_dev), BF),
            pltpu.VMEM((tokens, columns), BF),
            pltpu.VMEM((2, W, W), F32),
            pltpu.VMEM((rows_dev, tokens), BF),
            dma((8,)),
        ],
        mib=60,
    )
    share = SENT // n_zl
    column = call(sum_kernel, shape((1, SENT, W), BF), swap(sent, "x"))
    column, acts = lax.optimization_barrier((column, next_acts))
    acts_1, acts_3 = turn(acts, "x", 1), turn(acts, "x", 3)
    tiles = swap(column.reshape(n_zl, share, W), "zl")
    tiles, acts, acts_1, acts_3 = lax.optimization_barrier((tiles, next_acts, acts_1, acts_3))
    part = call(sum_kernel, shape((n_zh, share, W), BF), tiles)
    part, acts = lax.optimization_barrier((part, acts))
    acts_2 = turn(acts, "x", 2)
    tiles = swap(part, "zh")
    tiles, acts_2 = lax.optimization_barrier((tiles, acts_2))
    mine = call(sum_kernel, shape((n_zl, share, W), BF), tiles)
    full = swap(mine, "zl").reshape(SENT, W)
    moved, partial_next = call(
        root_kernel,
        [shape((SENT, W), BF), shape((n_x * W, tokens), BF)],
        full,
        weight,
        next_acts,
        acts_1,
        acts_2,
        acts_3,
        specs=[IN_VMEM] + [IN_HBM] * 5,
        scratch=[pltpu.VMEM((rows_dev, W), F32), pltpu.VMEM((n_x, tokens, rows_dev), BF), dma((5,))],
    )
    tiles = swap(partial_next.reshape(n_feat, columns // n_feat, tokens), "feat")
    moved_1, moved_3 = turn(moved, "x", 1), turn(moved, "x", 3)
    moved_2 = turn(moved_1[:EACH], "x", 1), turn(moved_3[EACH:], "x", 3)
    weight_new, stats_new = call(
        finish_kernel,
        [shape(weight.shape, F32), shape(stats_old.shape, F32)],
        owners,
        moved,
        moved_1,
        *moved_2,
        moved_3,
        weight,
        stats_old,
        specs=[IN_HBM] + [IN_VMEM] * 5 + [IN_HBM] * 2,
        out_specs=[IN_HBM, IN_HBM],
        scratch=[
            pltpu.SMEM(owners.shape, jnp.int32),
            pltpu.VMEM((n_x, rows_dev, W), F32),
            pltpu.VMEM((2, W, W), F32),
            pltpu.VMEM((n_x, rows_dev, W), F32),
            pltpu.VMEM((2, W, W), F32),
            dma((7,)),
            dma((5,)),
        ],
    )
    summed = jnp.sum(tiles.astype(F32), axis=0).astype(BF)
    each = n_feat // n_x
    pairs = [
        (x * n_feat + to * each + j, to * n_feat + x * each + j)
        for x in range(n_x)
        for to in range(n_x)
        for j in range(each)
    ]
    next_out = lax.ppermute(summed, ("x", "feat"), pairs).T
    return (weight_new, stats_new, next_out)


def solution(mesh):
    torus = Mesh(mesh.devices.reshape(4, 3, 4, mesh.shape["feat"]), ("x", "zh", "zl", "feat"))
    return jax.shard_map(
        body,
        mesh=torus,
        in_specs=(
            P(DP, "feat"),
            P(DP, None),
            P("feat", None),
            P("feat", DP, None, None, None),
            P(),
            P(DP, "feat"),
        ),
        out_specs=(P("feat", None), P("feat", DP, None, None, None), P(DP, "feat")),
        check_vma=False,
    )
```

time: 155 us -> 138 us (0.89)
  the two profiles are of different devices: /device:TPU:1 before, /device:TPU:22 now
where the time goes in v3:
time: 138 us; the launch traced here: 137 us
  starting transfers between devices  57.3 us (42%)
  blocking collectives  35.7 us (26%)
  waiting for transfers between devices  25.6 us (19%)
  Pallas kernels  14.6 us (11%)
  local copies, waits for them, and re-layouts  2.03 us (1%)
    all_to_all x2, blocking collectives, swap(): return lax.all_to_all(x, axis, 0, 0, tiled=True)  35.7 us
    ppermute x7, starting transfers between devices, turn(): return lax.ppermute(x, axis, [(i, (i + by) % n) for i in range(n)])  26.3 us
    all_to_all x3, starting transfers between devices, swap(): return lax.all_to_all(x, axis, 0, 0, tiled=True)  26.1 us
    ppermute x7, waiting for transfers between devices, turn(): return lax.ppermute(x, axis, [(i, (i + by) % n) for i in range(n)])  17 us
    pallas_call x6, Pallas kernels, call(): pl.pallas_call(kernel, out_shape=out, in_specs=specs or [IN_VMEM] * len(a...  14.6 us
    ppermute x1, starting transfers between devices, body(): next_out = lax.ppermute(summed, ('x', 'feat'), pairs).T  4.89 us
    all_to_all x3, waiting for transfers between devices, swap(): return lax.all_to_all(x, axis, 0, 0, tiled=True)  4.63 us
    ppermute x1, waiting for transfers between devices, body(): next_out = lax.ppermute(summed, ('x', 'feat'), pairs).T  4 us
  transfers between devices with their start and end apart: 11, of which 6 were waited for; matrix products, arithmetic and copies ran while one was open for 2% of the time, Pallas kernels for 2%

profile of v3, /device:TPU:22, one launch (start us, length us, event | category | flops | bytes accessed | tf_op | source)
XLA Modules:
  0.0 137.2 jit_solution(5184900275745289939)
XLA Ops:
  0.6 3.6 %shard_map.85 = bf16[4,800,256]{2,1,0:T(8,128)(2,1)} custom-call(s32[4,32]{1,0:T(4,128)} %bitcast.6, bf16[256,512]{1,0:T(8,128)(2,1)} %acts_in.1, bf16[256,1024]{1,0:T(8,128)(2,1)} %cot_in.1, f32[1,1,2,256,256]{4,3,2,1,0:T(8,128)} %stats_in.3), custom_call_target="tpu_custom_call" | custom-call | tf_op jit(solution)/shard_map/pallas_call | solution.py:220
  4.3 24.1 %all_to_all.25.tiles = bf16[4,800,256]{2,1,0:T(8,128)(2,1)S(1)} all-to-all(bf16[4,800,256]{2,1,0:T(8,128)(2,1)} %shard_map.85), channel_id=1, replica_groups=mesh['x'=4,'zh'=3,'zl'=4,'feat'=16] {'x'}, dimensions={0} | all-to-all | bytes 3276800 | tf_op jit(solution)/shard_map/all_to_all | solution.py:231
  28.3 0.0 copy-start.2
  28.3 1.0 shard_map.86
  29.3 0.0 copy-start
  29.3 7.4 %all-to-all-start.1 = ((bf16[4,200,256]{2,1,0:T(8,128)(2,1)}), bf16[4,200,256]{2,1,0:T(8,128)(2,1)S(1)}, u32[]{:S(2)}, u32[]{:S(2)}) async-start(bf16[4,200,256]{2,1,0:T(8,128)(2,1)} %bitcast.1), calls=%async_computation.1 | async-start | bytes 819200 | tf_op jit(solution)/shard_map/all_to_all | solution.py:231
  36.7 0.0 copy-done.2
  36.7 2.3 %collective-permute-start.1 = (bf16[256,512]{1,0:T(8,128)(2,1)S(1)}, bf16[256,512]{1,0:T(8,128)(2,1)S(1)}, u32[]{:S(2)}, u32[]{:S(2)}) collective-permute-start(bf16[256,512]{1,0:T(8,128)(2,1)S(1)} %copy-done.2), channel_id=1, source_target_pairs={{0,576},{192,0},{384,192},{576,384},{1,577},{193,1},{385,193},{577... | collective-permute-start | bytes 786440 | tf_op jit(solution)/shard_map/ppermute | solution.py:236
  39.0 4.8 %collective-permute-start = (bf16[256,512]{1,0:T(8,128)(2,1)S(1)}, bf16[256,512]{1,0:T(8,128)(2,1)S(1)}, u32[]{:S(2)}, u32[]{:S(2)}) collective-permute-start(bf16[256,512]{1,0:T(8,128)(2,1)S(1)} %copy-done.2), channel_id=1, source_target_pairs={{0,192},{192,384},{384,576},{576,0},{1,193},{193,385},{385,577},{5... | collective-permute-start | bytes 786440 | tf_op jit(solution)/shard_map/ppermute | solution.py:236
  43.7 2.4 %collective-permute-done.1.third = bf16[256,512]{1,0:T(8,128)(2,1)S(1)} collective-permute-done((bf16[256,512]{1,0:T(8,128)(2,1)S(1)}, bf16[256,512]{1,0:T(8,128)(2,1)S(1)}, u32[]{:S(2)}, u32[]{:S(2)}) %collective-permute-start.1) | collective-permute-done | bytes 262176 | tf_op jit(solution)/shard_map/ppermute | solution.py:236
  46.2 1.5 %collective-permute-done.first = bf16[256,512]{1,0:T(8,128)(2,1)S(1)} collective-permute-done((bf16[256,512]{1,0:T(8,128)(2,1)S(1)}, bf16[256,512]{1,0:T(8,128)(2,1)S(1)}, u32[]{:S(2)}, u32[]{:S(2)}) %collective-permute-start) | collective-permute-done | bytes 262176 | tf_op jit(solution)/shard_map/ppermute | solution.py:236
  47.6 0.0 all-to-all-done.1.tiles
  47.6 0.8 shard_map.87
  48.4 11.3 %all-to-all-start.2 = ((bf16[3,200,256]{2,1,0:T(8,128)(2,1)}), bf16[3,200,256]{2,1,0:T(8,128)(2,1)S(1)}, u32[]{:S(2)}, u32[]{:S(2)}) async-start(bf16[3,200,256]{2,1,0:T(8,128)(2,1)} %shard_map.87), calls=%async_computation.2 | async-start | bytes 614400 | tf_op jit(solution)/shard_map/all_to_all | solution.py:231
  59.7 4.7 %collective-permute-start.2 = (bf16[256,512]{1,0:T(8,128)(2,1)S(1)}, bf16[256,512]{1,0:T(8,128)(2,1)S(1)}, u32[]{:S(2)}, u32[]{:S(2)}) collective-permute-start(bf16[256,512]{1,0:T(8,128)(2,1)S(1)} %copy-done.2), channel_id=1, source_target_pairs={{0,384},{192,576},{384,0},{576,192},{1,385},{193,577},{385,1},{577... | collective-permute-start | bytes 786440 | tf_op jit(solution)/shard_map/ppermute | solution.py:236
  64.3 5.1 %collective-permute-done.2.second = bf16[256,512]{1,0:T(8,128)(2,1)S(1)} collective-permute-done((bf16[256,512]{1,0:T(8,128)(2,1)S(1)}, bf16[256,512]{1,0:T(8,128)(2,1)S(1)}, u32[]{:S(2)}, u32[]{:S(2)}) %collective-permute-start.2) | collective-permute-done | bytes 262176 | tf_op jit(solution)/shard_map/ppermute | solution.py:236
  69.4 4.6 %all-to-all-done.2.tiles = bf16[3,200,256]{2,1,0:T(8,128)(2,1)S(1)} async-done(((bf16[3,200,256]{2,1,0:T(8,128)(2,1)}), bf16[3,200,256]{2,1,0:T(8,128)(2,1)S(1)}, u32[]{:S(2)}, u32[]{:S(2)}) %all-to-all-start.2) | async-done | bytes 307232 | tf_op jit(solution)/shard_map/all_to_all | solution.py:231
  74.1 11.6 %all_to_all.26 = bf16[4,200,256]{2,1,0:T(8,128)(2,1)S(1)} all-to-all(bf16[4,200,256]{2,1,0:T(8,128)(2,1)S(1)} %shard_map.88), channel_id=1, replica_groups=mesh['x'=4,'zh'=3,'zl'=4,'feat'=16] {'zl'}, dimensions={0} | all-to-all | bytes 819200 | tf_op jit(solution)/shard_map/all_to_all | solution.py:231
  85.7 0.0 copy-done
  85.7 6.0 %shard_map.89 = (bf16[800,256]{1,0:T(8,128)(2,1)}, bf16[1024,256]{1,0:T(8,128)(2,1)}) custom-call(bf16[800,256]{1,0:T(8,128)(2,1)S(1)} %bitcast.5, f32[512,1024]{1,0:T(8,128)S(1)} %copy-done, bf16[256,512]{1,0:T(8,128)(2,1)S(1)} %copy-done.2, bf16[256,512]{1,0:T(8,128)(2,1)S(1)} %collective-permute-done.first, ...), custom_call_target="tpu_custom_call" | custom-call | tf_op jit(solution)/shard_map/pallas_call | solution.py:220
  91.7 0.0 copy-start.1
  91.7 0.0 copy-start.3
  91.8 7.5 %all-to-all-start.4 = ((bf16[16,64,256]{2,1,0:T(8,128)(2,1)}), bf16[16,64,256]{2,1,0:T(8,128)(2,1)}, u32[]{:S(2)}, u32[]{:S(2)}) async-start(bf16[16,64,256]{2,1,0:T(8,128)(2,1)} %bitcast.3), calls=%async_computation.4 | async-start | bytes 1048576 | tf_op jit(solution)/shard_map/all_to_all | solution.py:231
  99.2 3.2 %collective-permute-start.5 = (bf16[800,256]{1,0:T(8,128)(2,1)}, bf16[800,256]{1,0:T(8,128)(2,1)S(1)}, u32[]{:S(2)}, u32[]{:S(2)}) collective-permute-start(bf16[800,256]{1,0:T(8,128)(2,1)} %get-tuple-element.27.own), channel_id=1, source_target_pairs={{0,576},{192,0},{384,192},{576,384},{1,577},{193,1},{385,193},{577... | collective-permute-start | bytes 1228808 | tf_op jit(solution)/shard_map/ppermute | solution.py:236
  102.5 4.3 %collective-permute-start.3 = (bf16[800,256]{1,0:T(8,128)(2,1)}, bf16[800,256]{1,0:T(8,128)(2,1)S(1)}, u32[]{:S(2)}, u32[]{:S(2)}) collective-permute-start(bf16[800,256]{1,0:T(8,128)(2,1)} %get-tuple-element.27.own), channel_id=1, source_target_pairs={{0,192},{192,384},{384,576},{576,0},{1,193},{193,385},{385,577},{5... | collective-permute-start | bytes 1228808 | tf_op jit(solution)/shard_map/ppermute | solution.py:236
  106.8 8.0 %collective-permute-done.5.third = bf16[800,256]{1,0:T(8,128)(2,1)S(1)} collective-permute-done((bf16[800,256]{1,0:T(8,128)(2,1)}, bf16[800,256]{1,0:T(8,128)(2,1)S(1)}, u32[]{:S(2)}, u32[]{:S(2)}) %collective-permute-start.5) | collective-permute-done | bytes 409632 | tf_op jit(solution)/shard_map/ppermute | solution.py:236
  114.8 0.7 slice.9
  115.5 1.9 %collective-permute-start.6 = (bf16[400,256]{1,0:T(8,128)(2,1)}, bf16[400,256]{1,0:T(8,128)(2,1)}, u32[]{:S(2)}, u32[]{:S(2)}) collective-permute-start(bf16[400,256]{1,0:T(8,128)(2,1)} %slice.9), channel_id=1, source_target_pairs={{0,576},{192,0},{384,192},{576,384},{1,577},{193,1},{385,193},{577... | collective-permute-start | bytes 614408 | tf_op jit(solution)/shard_map/ppermute | solution.py:236
  117.5 0.0 collective-permute-done.3.first
  117.5 0.7 slice.8
  118.2 5.1 %collective-permute-start.4 = (bf16[400,256]{1,0:T(8,128)(2,1)}, bf16[400,256]{1,0:T(8,128)(2,1)}, u32[]{:S(2)}, u32[]{:S(2)}) collective-permute-start(bf16[400,256]{1,0:T(8,128)(2,1)} %slice.8), channel_id=1, source_target_pairs={{0,192},{192,384},{384,576},{576,0},{1,193},{193,385},{385,577},{5... | collective-permute-start | bytes 614408 | tf_op jit(solution)/shard_map/ppermute | solution.py:236
  123.3 0.0 all-to-all-done.4
  123.3 1.1 reduce_sum.12
  124.4 4.9 %collective-permute-start.7 = (bf16[64,256]{1,0:T(8,128)(2,1)S(1)}, bf16[64,256]{1,0:T(8,128)(2,1)S(1)}, u32[]{:S(2)}, u32[]{:S(2)}) collective-permute-start(bf16[64,256]{1,0:T(8,128)(2,1)S(1)} %reduce_sum.12), channel_id=1, source_target_pairs={{0,0},{1,1},{2,2},{3,3},{4,192},{5,193},{6,194},{7,195},{8,384},{9... | collective-permute-start | bytes 98312 | tf_op jit(solution)/shard_map/ppermute | solution.py:322
  129.3 0.0 collective-permute-done.6.second_low
  129.3 0.0 collective-permute-done.4.second_top
  129.4 0.0 copy-done.1
  129.4 0.0 copy-done.3
  129.4 3.2 %shard_map.90 = (f32[512,1024]{1,0:T(8,128)}, f32[1,1,2,256,256]{4,3,2,1,0:T(8,128)}) custom-call(s32[4,32]{1,0:T(4,128)S(1)} %bitcast.7, bf16[800,256]{1,0:T(8,128)(2,1)} %get-tuple-element.27.own, bf16[800,256]{1,0:T(8,128)(2,1)S(1)} %collective-permute-done.3.first, bf16[400,256]{1,0:T(8,128)(2,1)} %collective-permute-done.4.second_top, ...), custom_call_target="tpu_custom_call" | custom-call | tf_op jit(solution)/shard_map/pallas_call | solution.py:220
  132.6 4.0 %collective-permute-done.7 = bf16[64,256]{1,0:T(8,128)(2,1)S(1)} collective-permute-done((bf16[64,256]{1,0:T(8,128)(2,1)S(1)}, bf16[64,256]{1,0:T(8,128)(2,1)S(1)}, u32[]{:S(2)}, u32[]{:S(2)}) %collective-permute-start.7) | collective-permute-done | bytes 32800 | tf_op jit(solution)/shard_map/ppermute | solution.py:322
  136.6 0.6 copy.10
  (1 shorter events, 0.0 us)
Async XLA Ops:
  28.3 8.4 %copy-start.2 = (bf16[256,512]{1,0:T(8,128)(2,1)S(1)}, bf16[256,512]{1,0:T(8,128)(2,1)}, u32[]{:S(2)}) copy-start(bf16[256,512]{1,0:T(8,128)(2,1)} %own.1) | copy-start | bytes 786436
  29.3 56.4 %copy-start = (f32[512,1024]{1,0:T(8,128)S(1)}, f32[512,1024]{1,0:T(8,128)}, u32[]{:S(2)}) copy-start(f32[512,1024]{1,0:T(8,128)} %weight_in.3) | copy-start | bytes 6291460
  29.3 18.3 %all-to-all-start.1 = ((bf16[4,200,256]{2,1,0:T(8,128)(2,1)}), bf16[4,200,256]{2,1,0:T(8,128)(2,1)S(1)}, u32[]{:S(2)}, u32[]{:S(2)}) async-start(bf16[4,200,256]{2,1,0:T(8,128)(2,1)} %bitcast.1), calls=%async_computation.1 | async-start | bytes 819200 | tf_op jit(solution)/shard_map/all_to_all | solution.py:231
  36.7 9.5 %collective-permute-start.1 = (bf16[256,512]{1,0:T(8,128)(2,1)S(1)}, bf16[256,512]{1,0:T(8,128)(2,1)S(1)}, u32[]{:S(2)}, u32[]{:S(2)}) collective-permute-start(bf16[256,512]{1,0:T(8,128)(2,1)S(1)} %copy-done.2), channel_id=1, source_target_pairs={{0,576},{192,0},{384,192},{576,384},{1,577},{193,1},{385,193},{577... | collective-permute-start | bytes 786440 | tf_op jit(solution)/shard_map/ppermute | solution.py:236
  39.0 8.6 %collective-permute-start = (bf16[256,512]{1,0:T(8,128)(2,1)S(1)}, bf16[256,512]{1,0:T(8,128)(2,1)S(1)}, u32[]{:S(2)}, u32[]{:S(2)}) collective-permute-start(bf16[256,512]{1,0:T(8,128)(2,1)S(1)} %copy-done.2), channel_id=1, source_target_pairs={{0,192},{192,384},{384,576},{576,0},{1,193},{193,385},{385,577},{5... | collective-permute-start | bytes 786440 | tf_op jit(solution)/shard_map/ppermute | solution.py:236
  48.4 25.6 %all-to-all-start.2 = ((bf16[3,200,256]{2,1,0:T(8,128)(2,1)}), bf16[3,200,256]{2,1,0:T(8,128)(2,1)S(1)}, u32[]{:S(2)}, u32[]{:S(2)}) async-start(bf16[3,200,256]{2,1,0:T(8,128)(2,1)} %shard_map.87), calls=%async_computation.2 | async-start | bytes 614400 | tf_op jit(solution)/shard_map/all_to_all | solution.py:231
  59.7 9.8 %collective-permute-start.2 = (bf16[256,512]{1,0:T(8,128)(2,1)S(1)}, bf16[256,512]{1,0:T(8,128)(2,1)S(1)}, u32[]{:S(2)}, u32[]{:S(2)}) collective-permute-start(bf16[256,512]{1,0:T(8,128)(2,1)S(1)} %copy-done.2), channel_id=1, source_target_pairs={{0,384},{192,576},{384,0},{576,192},{1,385},{193,577},{385,1},{577... | collective-permute-start | bytes 786440 | tf_op jit(solution)/shard_map/ppermute | solution.py:236
  91.7 37.6 %copy-start.1 = (f32[1,1,2,256,256]{4,3,2,1,0:T(8,128)S(1)}, f32[1,1,2,256,256]{4,3,2,1,0:T(8,128)}, u32[]{:S(2)}) copy-start(f32[1,1,2,256,256]{4,3,2,1,0:T(8,128)} %stats_in.3) | copy-start | bytes 1572868
  91.7 37.6 %copy-start.3 = (s32[32,4]{0,1:T(4,128)S(1)}, s32[32,4]{0,1:T(4,128)}, u32[]{:S(2)}) copy-start(s32[32,4]{0,1:T(4,128)} %param.10) | copy-start | bytes 1540
  91.8 31.5 %all-to-all-start.4 = ((bf16[16,64,256]{2,1,0:T(8,128)(2,1)}), bf16[16,64,256]{2,1,0:T(8,128)(2,1)}, u32[]{:S(2)}, u32[]{:S(2)}) async-start(bf16[16,64,256]{2,1,0:T(8,128)(2,1)} %bitcast.3), calls=%async_computation.4 | async-start | bytes 1048576 | tf_op jit(solution)/shard_map/all_to_all | solution.py:231
  99.2 15.6 %collective-permute-start.5 = (bf16[800,256]{1,0:T(8,128)(2,1)}, bf16[800,256]{1,0:T(8,128)(2,1)S(1)}, u32[]{:S(2)}, u32[]{:S(2)}) collective-permute-start(bf16[800,256]{1,0:T(8,128)(2,1)} %get-tuple-element.27.own), channel_id=1, source_target_pairs={{0,576},{192,0},{384,192},{576,384},{1,577},{193,1},{385,193},{577... | collective-permute-start | bytes 1228808 | tf_op jit(solution)/shard_map/ppermute | solution.py:236
  102.5 15.0 %collective-permute-start.3 = (bf16[800,256]{1,0:T(8,128)(2,1)}, bf16[800,256]{1,0:T(8,128)(2,1)S(1)}, u32[]{:S(2)}, u32[]{:S(2)}) collective-permute-start(bf16[800,256]{1,0:T(8,128)(2,1)} %get-tuple-element.27.own), channel_id=1, source_target_pairs={{0,192},{192,384},{384,576},{576,0},{1,193},{193,385},{385,577},{5... | collective-permute-start | bytes 1228808 | tf_op jit(solution)/shard_map/ppermute | solution.py:236
  115.5 13.8 %collective-permute-start.6 = (bf16[400,256]{1,0:T(8,128)(2,1)}, bf16[400,256]{1,0:T(8,128)(2,1)}, u32[]{:S(2)}, u32[]{:S(2)}) collective-permute-start(bf16[400,256]{1,0:T(8,128)(2,1)} %slice.9), channel_id=1, source_target_pairs={{0,576},{192,0},{384,192},{576,384},{1,577},{193,1},{385,193},{577... | collective-permute-start | bytes 614408 | tf_op jit(solution)/shard_map/ppermute | solution.py:236
  118.2 11.2 %collective-permute-start.4 = (bf16[400,256]{1,0:T(8,128)(2,1)}, bf16[400,256]{1,0:T(8,128)(2,1)}, u32[]{:S(2)}, u32[]{:S(2)}) collective-permute-start(bf16[400,256]{1,0:T(8,128)(2,1)} %slice.8), channel_id=1, source_target_pairs={{0,192},{192,384},{384,576},{576,0},{1,193},{193,385},{385,577},{5... | collective-permute-start | bytes 614408 | tf_op jit(solution)/shard_map/ppermute | solution.py:236
  124.4 12.1 %collective-permute-start.7 = (bf16[64,256]{1,0:T(8,128)(2,1)S(1)}, bf16[64,256]{1,0:T(8,128)(2,1)S(1)}, u32[]{:S(2)}, u32[]{:S(2)}) collective-permute-start(bf16[64,256]{1,0:T(8,128)(2,1)S(1)} %reduce_sum.12), channel_id=1, source_target_pairs={{0,0},{1,1},{2,2},{3,3},{4,192},{5,193},{6,194},{7,195},{8,384},{9... | collective-permute-start | bytes 98312 | tf_op jit(solution)/shard_map/ppermute | solution.py:322

commit v4 on v3

v4 whole, which is shorter than its diff:
```python
import jax
import jax.numpy as jnp
from jax import lax
from jax.experimental import pallas as pl
from jax.experimental.pallas import tpu as pltpu
from jax.sharding import Mesh
from jax.sharding import PartitionSpec as P

ITERS = 6
DP = ("x", "zh", "zl")
BF = jnp.bfloat16
F32 = jnp.float32
decay_rate = 0.9
step_rate = 0.01

W = 256
H = W // 2
PACK = H + 16
EACH = W + PACK
SENT = 2 * EACH


def room(mib):
    return pltpu.CompilerParams(vmem_limit_bytes=mib * 1024 * 1024)


IN_VMEM = pl.BlockSpec(memory_space=pltpu.VMEM)
IN_HBM = pl.BlockSpec(memory_space=pltpu.HBM)


def dims(rows, cols):
    return (
        lax.broadcasted_iota(jnp.int32, (rows, cols), 0),
        lax.broadcasted_iota(jnp.int32, (rows, cols), 1),
    )


def start_copies(pairs, sems):
    copies = [pltpu.make_async_copy(a, b, sems.at[i]) for i, (a, b) in enumerate(pairs)]
    for copy in copies:
        copy.start()
    return copies


def wide(start):
    return pl.ds(pl.multiple_of(start * W, W), W)


def mine_and_slot(owners, block):
    me = (lax.axis_index("x") * 3 + lax.axis_index("zh")) * 4 + lax.axis_index("zl")
    base = lax.axis_index("feat") * 2
    mine = jnp.int32(0)
    slot = jnp.int32(0)
    for other in range(8):
        held = (owners[other % 4, base + other // 4] == me).astype(jnp.int32)
        slot += jnp.where(other < block, held, 0)
        mine += jnp.where(other == block, held, 0)
    return mine == 1, slot


def pack(old, out, start):
    row, col = dims(H, H)
    upper, lower = old[:H, :H], old[H:, H:]
    out[start : start + H, :H] = old[:H, H:].astype(BF)
    out[start : start + H, H:] = jnp.where(col >= row, upper, lower).astype(BF)
    diagonal = jnp.sum(jnp.where(row == col, lower, 0.0), axis=0, keepdims=True)
    out[start + H : start + PACK, :H] = jnp.broadcast_to(diagonal, (PACK - H, H)).astype(BF)
    out[start + H : start + PACK, H:] = jnp.zeros((PACK - H, H), BF)


def unpack(tile, start):
    row, col = dims(H, H)
    packed = tile[start : start + H, :].astype(F32)
    diagonal = tile[start + H : start + PACK, :H][:1, :].astype(F32)
    flipped = packed.T
    both, both_t = packed[:, H:], flipped[H:, :]
    upper = jnp.where(col >= row, both, both_t)
    lower = jnp.where(col < row, both, jnp.where(col > row, both_t, jnp.broadcast_to(diagonal, (H, H))))
    return jnp.concatenate(
        [
            jnp.concatenate([upper, packed[:, :H]], axis=1),
            jnp.concatenate([flipped[:H, :], lower], axis=1),
        ],
        axis=0,
    )


def grad_kernel(owners_in, acts_in, cot_in, stats_in, sent, owners, acts, cot, stats, turned, out, sems, out_sems):
    copies = start_copies(
        [(acts_in, acts), (owners_in, owners)]
        + [(cot_in.at[:, i * W : (i + 1) * W], cot.at[:, i * W : (i + 1) * W]) for i in range(4)]
        + [(stats_in.at[0, 0, k], stats.at[k]) for k in range(2)],
        sems,
    )
    for r in range(2):
        for i in range(4):
            out[i, r * EACH + W : (r + 1) * EACH, :] = jnp.zeros((PACK, W), BF)
    for at in (1, 6, 7, 0):
        copies[at].wait()
    turned[...] = acts[...].T
    sends = []
    for i in range(4):
        copies[2 + i].wait()
        part = jnp.dot(turned[...], cot[:, i * W : (i + 1) * W], preferred_element_type=F32).astype(BF)
        for r in range(2):
            out[i, r * EACH : r * EACH + W, :] = part[r * W : (r + 1) * W, :]
            mine, slot = mine_and_slot(owners, r * 4 + i)

            @pl.when(mine)
            def _(i=i, r=r, slot=slot):
                pack(stats[jnp.minimum(slot, 1)], out.at[i], r * EACH + W)

        sends.append(pltpu.make_async_copy(out.at[i], sent.at[i], out_sems.at[i]))
        sends[-1].start()
    for send in sends:
        send.wait()


def sum_kernel(tiles, out):
    total = tiles[0].astype(F32)
    for i in range(1, tiles.shape[0]):
        total += tiles[i].astype(F32)
    total = total.astype(BF)
    for i in range(out.shape[0]):
        out[i] = total


def dot(a, b):
    return jnp.dot(a, b, preferred_element_type=F32)


def root_kernel(tile, updates, products):
    big_row, big_col = dims(W, W)
    identity = (big_row == big_col).astype(F32)
    grads, matrices, iterates, norms = [], [], [], []
    for r in range(2):
        grad = tile[r * EACH : r * EACH + W, :]
        old = unpack(tile, r * EACH + W)
        gram = lax.dot_general(grad, grad, (((1,), (1,)), ((), ())), preferred_element_type=F32) / W
        pack(gram, products, r * PACK)
        renewed = decay_rate * old + (1.0 - decay_rate) * gram
        norm = jnp.sqrt(jnp.sum(renewed * renewed, axis=(0, 1), keepdims=True) + 1e-06)
        grads.append(grad)
        matrices.append(renewed / norm)
        norms.append(norm)
        iterates.append(None)
    for step in range(ITERS):
        for r in range(2):
            low = ((5.0 * identity - matrices[r]) / 4.0).astype(BF)
            if step == 0:
                iterates[r] = low.astype(F32)
            else:
                iterates[r] = dot(iterates[r].astype(BF), low)
            if step + 1 < ITERS:
                square = dot(low, low).astype(BF)
                fourth = dot(square, square).astype(BF)
                matrices[r] = dot(fourth, matrices[r].astype(BF))
    for r in range(2):
        root = (iterates[r] * lax.rsqrt(jnp.sqrt(norms[r]))).astype(BF)
        update = dot(root, grads[r]).astype(BF)
        for i in range(updates.shape[0]):
            updates[i, r * W : (r + 1) * W, :] = update


def next_kernel(weight, updates, acts, out, parts, sems):
    sends = []
    for i in range(4):
        new = weight[:, i * W : (i + 1) * W] - step_rate * updates[i].astype(F32)
        parts[i] = lax.dot_general(
            new.astype(BF), acts[...], (((0,), (1,)), ((), ())), preferred_element_type=F32
        ).astype(BF)
        sends.append(pltpu.make_async_copy(parts.at[i], out.at[i], sems.at[i]))
        sends[-1].start()
    for send in sends:
        send.wait()


def weight_kernel(weight, updates, weight_new):
    weight_new[...] = weight[...] - step_rate * updates[0].astype(F32)


def stats_kernel(owners_in, own, first, second, third, stats_in, stats_new, owners, stats, sems):
    x = lax.axis_index("x")
    copies = start_copies(
        [(owners_in, owners)] + [(stats_in.at[0, 0, k], stats.at[k]) for k in range(2)],
        sems,
    )
    stats_new[...] = jnp.zeros(stats_new.shape, F32)
    for copy in copies:
        copy.wait()
    for k, part in enumerate((own, first, second, third)):
        for r in range(2):
            mine, slot = mine_and_slot(owners, r * 4 + (x + (4 - k)) % 4)

            @pl.when(mine)
            def _(r=r, part=part, slot=slot):
                at = jnp.minimum(slot, 1)
                stats_new[0, 0, at] = decay_rate * stats[at] + (1.0 - decay_rate) * unpack(part, r * PACK)


def call(kernel, out, *args, specs=None, out_specs=None, scratch=(), mib=32):
    return pl.pallas_call(
        kernel,
        out_shape=out,
        in_specs=specs or [IN_VMEM] * len(args),
        out_specs=out_specs or jax.tree.map(lambda _: IN_VMEM, out),
        scratch_shapes=list(scratch),
        compiler_params=room(mib),
    )(*args)


def swap(x, axis):
    return lax.all_to_all(x, axis, 0, 0, tiled=True)


def turn(x, axis, by):
    n = lax.axis_size(axis)
    return lax.ppermute(x, axis, [(i, (i + by) % n) for i in range(n)])


def body(activations, cotangent, weight, stats_old, owners, next_acts):
    n_x, n_zh, n_zl, n_feat = (lax.axis_size(a) for a in ("x", "zh", "zl", "feat"))
    rows_dev, columns = weight.shape
    tokens = activations.shape[0]
    owners = owners.T
    shape = jax.ShapeDtypeStruct
    dma = pltpu.SemaphoreType.DMA
    sent = call(
        grad_kernel,
        shape((n_x, SENT, W), BF),
        owners,
        activations,
        cotangent,
        stats_old,
        specs=[IN_HBM] * 4,
        scratch=[
            pltpu.SMEM(owners.shape, jnp.int32),
            pltpu.VMEM((tokens, rows_dev), BF),
            pltpu.VMEM((tokens, columns), BF),
            pltpu.VMEM((2, W, W), F32),
            pltpu.VMEM((rows_dev, tokens), BF),
            pltpu.VMEM((n_x, SENT, W), BF),
            dma((8,)),
            dma((n_x,)),
        ],
        out_specs=IN_HBM,
        mib=60,
    )
    share = SENT // n_zl
    column = call(sum_kernel, shape((1, SENT, W), BF), swap(sent, "x"))
    part = call(sum_kernel, shape((n_zh, share, W), BF), swap(column.reshape(n_zl, share, W), "zl"))
    mine = call(sum_kernel, shape((n_zl, share, W), BF), swap(part, "zh"))
    full = swap(mine, "zl").reshape(SENT, W)
    updates, products = call(root_kernel, [shape((n_x, rows_dev, W), BF), shape((2 * PACK, W), BF)], full)
    updates = swap(updates, "x")
    partial_next = call(
        next_kernel,
        shape((n_x, W, tokens), BF),
        weight,
        updates,
        next_acts,
        out_specs=IN_HBM,
        scratch=[pltpu.VMEM((n_x, W, tokens), BF), dma((n_x,))],
    )
    partial_next, products = lax.optimization_barrier((partial_next, products))
    tiles = swap(partial_next.reshape(n_feat, columns // n_feat, tokens), "feat")
    weight_new = pl.pallas_call(
        weight_kernel,
        grid=(n_x,),
        in_specs=[
            pl.BlockSpec((rows_dev, W), lambda i: (0, i)),
            pl.BlockSpec((1, rows_dev, W), lambda i: (i, 0, 0)),
        ],
        out_specs=pl.BlockSpec((rows_dev, W), lambda i: (0, i)),
        out_shape=shape(weight.shape, F32),
        compiler_params=room(32),
    )(weight, updates)
    stats_new = call(
        stats_kernel,
        shape(stats_old.shape, F32),
        owners,
        products,
        *[turn(products, "x", k) for k in range(1, n_x)],
        stats_old,
        specs=[IN_HBM] + [IN_VMEM] * 4 + [IN_HBM],
        scratch=[pltpu.SMEM(owners.shape, jnp.int32), pltpu.VMEM((2, W, W), F32), dma((3,))],
    )
    next_out = jnp.sum(tiles.astype(F32), axis=0).astype(BF).T
    return (weight_new, stats_new, next_out)


def solution(mesh):
    torus = Mesh(mesh.devices.reshape(4, 3, 4, mesh.shape["feat"]), ("x", "zh", "zl", "feat"))
    return jax.shard_map(
        body,
        mesh=torus,
        in_specs=(
            P(DP, "feat"),
            P(DP, None),
            P("feat", None),
            P("feat", DP, None, None, None),
            P(),
            P(DP, "feat"),
        ),
        out_specs=(P("feat", None), P("feat", DP, None, None, None), P(DP, "feat")),
        check_vma=False,
    )
```

time: 138 us -> 140 us (1.014)
  the two profiles are of different devices: /device:TPU:22 before, /device:TPU:1 now
where the time goes in v4:
time: 140 us
  blocking collectives  98.9 us (71%)
  starting transfers between devices  17.7 us (13%)
  Pallas kernels  13.9 us (10%)
  waiting for transfers between devices  5.78 us (4%)
  other arithmetic  1.74 us (1%)
    all_to_all x5, blocking collectives, swap(): return lax.all_to_all(x, axis, 0, 0, tiled=True)  98.9 us
    pallas_call x7, Pallas kernels, call(): pl.pallas_call(kernel, out_shape=out, in_specs=specs or [IN_VMEM] * len(a...  11.8 us
    all_to_all x1, starting transfers between devices, swap(): return lax.all_to_all(x, axis, 0, 0, tiled=True)  9.75 us
    ppermute x3, starting transfers between devices, turn(): return lax.ppermute(x, axis, [(i, (i + by) % n) for i in range(n)])  7.94 us
    ppermute x3, waiting for transfers between devices, turn(): return lax.ppermute(x, axis, [(i, (i + by) % n) for i in range(n)])  4.64 us
  transfers between devices with their start and end apart: 4, of which 3 were waited for; matrix products, arithmetic and copies ran while one was open for 0% of the time, Pallas kernels for 3%

profile of v4, /device:TPU:1, one launch (start us, length us, event | category | flops | bytes accessed | tf_op | source)
XLA Modules:
  0.0 139.5 jit_solution(953090743656536141)
XLA Ops:
  0.6 3.5 %shard_map.85 = bf16[4,800,256]{2,1,0:T(8,128)(2,1)} custom-call(s32[4,32]{1,0:T(4,128)} %bitcast.8, bf16[256,512]{1,0:T(8,128)(2,1)} %acts_in.1, bf16[256,1024]{1,0:T(8,128)(2,1)} %cot_in.1, f32[1,1,2,256,256]{4,3,2,1,0:T(8,128)} %stats_in.3), custom_call_target="tpu_custom_call" | custom-call | tf_op jit(solution)/shard_map/pallas_call | solution.py:202
  4.1 17.8 %all_to_all.30.tiles = bf16[4,800,256]{2,1,0:T(8,128)(2,1)S(1)} all-to-all(bf16[4,800,256]{2,1,0:T(8,128)(2,1)} %shard_map.85), channel_id=1, replica_groups=mesh['x'=4,'zh'=3,'zl'=4,'feat'=16] {'x'}, dimensions={0} | all-to-all | bytes 3276800 | tf_op jit(solution)/shard_map/all_to_all | solution.py:213
  21.9 0.2 shard_map.86
  22.1 23.8 %all_to_all.31.tiles = bf16[4,200,256]{2,1,0:T(8,128)(2,1)S(1)} all-to-all(bf16[4,200,256]{2,1,0:T(8,128)(2,1)S(1)} %bitcast.7), channel_id=1, replica_groups=mesh['x'=4,'zh'=3,'zl'=4,'feat'=16] {'zl'}, dimensions={0} | all-to-all | bytes 819200 | tf_op jit(solution)/shard_map/all_to_all | solution.py:213
  45.9 0.1 shard_map.87
  45.9 20.4 %all_to_all.32.tiles = bf16[3,200,256]{2,1,0:T(8,128)(2,1)S(1)} all-to-all(bf16[3,200,256]{2,1,0:T(8,128)(2,1)S(1)} %shard_map.87), channel_id=1, replica_groups=mesh['x'=4,'zh'=3,'zl'=4,'feat'=16] {'zh'}, dimensions={0} | all-to-all | bytes 614400 | tf_op jit(solution)/shard_map/all_to_all | solution.py:213
  66.3 0.0 copy-start
  66.3 0.0 copy-start.3
  66.3 21.2 %all_to_all.33 = bf16[4,200,256]{2,1,0:T(8,128)(2,1)S(1)} all-to-all(bf16[4,200,256]{2,1,0:T(8,128)(2,1)S(1)} %shard_map.88), channel_id=1, replica_groups=mesh['x'=4,'zh'=3,'zl'=4,'feat'=16] {'zl'}, dimensions={0} | all-to-all | bytes 819200 | tf_op jit(solution)/shard_map/all_to_all | solution.py:213
  87.5 4.5 %shard_map.89 = (bf16[4,512,256]{2,1,0:T(8,128)(2,1)S(1)}, bf16[288,256]{1,0:T(8,128)(2,1)S(1)}) custom-call(bf16[800,256]{1,0:T(8,128)(2,1)S(1)} %bitcast.6), custom_call_target="tpu_custom_call" | custom-call | tf_op jit(solution)/shard_map/pallas_call | solution.py:202
  92.0 15.8 %all_to_all.34.updates = bf16[4,512,256]{2,1,0:T(8,128)(2,1)S(1)} all-to-all(bf16[4,512,256]{2,1,0:T(8,128)(2,1)S(1)} %get-tuple-element.7), channel_id=1, replica_groups=mesh['x'=4,'zh'=3,'zl'=4,'feat'=16] {'x'}, dimensions={0} | all-to-all | bytes 2097152 | tf_op jit(solution)/shard_map/all_to_all | solution.py:213
  107.8 0.0 copy-done
  107.8 0.0 copy-done.3
  107.8 2.0 %shard_map.91 = bf16[4,256,256]{2,1,0:T(8,128)(2,1)S(1)} custom-call(f32[512,1024]{1,0:T(8,128)S(1)} %copy-done, bf16[4,512,256]{2,1,0:T(8,128)(2,1)S(1)} %all_to_all.34.updates, bf16[256,512]{1,0:T(8,128)(2,1)S(1)} %copy-done.3), custom_call_target="tpu_custom_call" | custom-call | tf_op jit(solution)/shard_map/pallas_call | solution.py:202
  109.8 0.0 copy-start.2
  109.8 0.8 copy-done.2
  110.6 9.8 %all-to-all-start.5 = ((bf16[16,64,256]{2,1,0:T(8,128)(2,1)}), bf16[16,64,256]{2,1,0:T(8,128)(2,1)}, u32[]{:S(2)}, u32[]{:S(2)}) async-start(bf16[16,64,256]{2,1,0:T(8,128)(2,1)} %bitcast.5), calls=%async_computation.5 | async-start | bytes 1048576 | tf_op jit(solution)/shard_map/all_to_all | solution.py:213
  120.3 0.0 copy-start.1
  120.4 0.0 copy-start.4
  120.4 2.9 %collective-permute-start.2 = (bf16[288,256]{1,0:T(8,128)(2,1)S(1)}, bf16[288,256]{1,0:T(8,128)(2,1)S(1)}, u32[]{:S(2)}, u32[]{:S(2)}) collective-permute-start(bf16[288,256]{1,0:T(8,128)(2,1)S(1)} %get-tuple-element.9.own), channel_id=1, source_target_pairs={{0,576},{192,0},{384,192},{576,384},{1,577},{193,1},{385,193},{577... | collective-permute-start | bytes 442376 | tf_op jit(solution)/shard_map/ppermute | solution.py:218
  123.3 3.1 %collective-permute-start.1 = (bf16[288,256]{1,0:T(8,128)(2,1)S(1)}, bf16[288,256]{1,0:T(8,128)(2,1)S(1)}, u32[]{:S(2)}, u32[]{:S(2)}) collective-permute-start(bf16[288,256]{1,0:T(8,128)(2,1)S(1)} %get-tuple-element.9.own), channel_id=1, source_target_pairs={{0,384},{192,576},{384,0},{576,192},{1,385},{193,577},{385,1},{577... | collective-permute-start | bytes 442376 | tf_op jit(solution)/shard_map/ppermute | solution.py:218
  126.4 1.9 %collective-permute-start = (bf16[288,256]{1,0:T(8,128)(2,1)S(1)}, bf16[288,256]{1,0:T(8,128)(2,1)S(1)}, u32[]{:S(2)}, u32[]{:S(2)}) collective-permute-start(bf16[288,256]{1,0:T(8,128)(2,1)S(1)} %get-tuple-element.9.own), channel_id=1, source_target_pairs={{0,192},{192,384},{384,576},{576,0},{1,193},{193,385},{385,577},{5... | collective-permute-start | bytes 442376 | tf_op jit(solution)/shard_map/ppermute | solution.py:218
  128.3 2.0 %shard_map.90 = f32[512,1024]{1,0:T(8,128)} custom-call(f32[512,1024]{1,0:T(8,128)S(1)} %copy-done, bf16[4,512,256]{2,1,0:T(8,128)(2,1)S(1)} %all_to_all.34.updates), custom_call_target="tpu_custom_call" | custom-call | tf_op jit(solution)/shard_map/pallas_call | solution.py:267
  130.3 0.0 collective-permute-done.2.third
  130.3 1.4 %collective-permute-done.1.second = bf16[288,256]{1,0:T(8,128)(2,1)S(1)} collective-permute-done((bf16[288,256]{1,0:T(8,128)(2,1)S(1)}, bf16[288,256]{1,0:T(8,128)(2,1)S(1)}, u32[]{:S(2)}, u32[]{:S(2)}) %collective-permute-start.1) | collective-permute-done | bytes 147488 | tf_op jit(solution)/shard_map/ppermute | solution.py:218
  131.8 3.2 %collective-permute-done.first = bf16[288,256]{1,0:T(8,128)(2,1)S(1)} collective-permute-done((bf16[288,256]{1,0:T(8,128)(2,1)S(1)}, bf16[288,256]{1,0:T(8,128)(2,1)S(1)}, u32[]{:S(2)}, u32[]{:S(2)}) %collective-permute-start) | collective-permute-done | bytes 147488 | tf_op jit(solution)/shard_map/ppermute | solution.py:218
  135.0 0.0 copy-done.1
  135.0 0.0 copy-done.4
  135.0 1.6 %shard_map.92 = f32[1,1,2,256,256]{4,3,2,1,0:T(8,128)} custom-call(s32[4,32]{1,0:T(4,128)S(1)} %bitcast.9, bf16[288,256]{1,0:T(8,128)(2,1)S(1)} %get-tuple-element.9.own, bf16[288,256]{1,0:T(8,128)(2,1)S(1)} %collective-permute-done.first, bf16[288,256]{1,0:T(8,128)(2,1)S(1)} %collective-permute-done.1.second, ...), custom_call_target="tpu_custom_call" | custom-call | tf_op jit(solution)/shard_map/pallas_call | solution.py:202
  136.6 1.1 all-to-all-done.5
  137.8 1.7 %reduce_sum.12 = bf16[64,256]{1,0:T(8,128)(2,1)} reduce(bf16[16,64,256]{2,1,0:T(8,128)(2,1)} %all-to-all-done.5, bf16[]{:T(256)} %constant.2.clone.1), dimensions={0}, to_apply=%region_0.0 | reduce | flops 245760 | bytes 557058 | tf_op jit(solution)/shard_map/reduce_sum | solution.py:288
  (1 shorter events, 0.0 us)
Async XLA Ops:
  66.3 41.5 %copy-start = (f32[512,1024]{1,0:T(8,128)S(1)}, f32[512,1024]{1,0:T(8,128)}, u32[]{:S(2)}) copy-start(f32[512,1024]{1,0:T(8,128)} %weight.3) | copy-start | bytes 6291460
  66.3 41.5 %copy-start.3 = (bf16[256,512]{1,0:T(8,128)(2,1)S(1)}, bf16[256,512]{1,0:T(8,128)(2,1)}, u32[]{:S(2)}) copy-start(bf16[256,512]{1,0:T(8,128)(2,1)} %acts.1) | copy-start | bytes 786436
  109.8 0.8 copy-start.2
  110.6 27.2 %all-to-all-start.5 = ((bf16[16,64,256]{2,1,0:T(8,128)(2,1)}), bf16[16,64,256]{2,1,0:T(8,128)(2,1)}, u32[]{:S(2)}, u32[]{:S(2)}) async-start(bf16[16,64,256]{2,1,0:T(8,128)(2,1)} %bitcast.5), calls=%async_computation.5 | async-start | bytes 1048576 | tf_op jit(solution)/shard_map/all_to_all | solution.py:213
  120.3 14.6 %copy-start.1 = (f32[1,1,2,256,256]{4,3,2,1,0:T(8,128)S(1)}, f32[1,1,2,256,256]{4,3,2,1,0:T(8,128)}, u32[]{:S(2)}) copy-start(f32[1,1,2,256,256]{4,3,2,1,0:T(8,128)} %stats_in.3) | copy-start | bytes 1572868
  120.4 14.6 %copy-start.4 = (s32[32,4]{0,1:T(4,128)S(1)}, s32[32,4]{0,1:T(4,128)}, u32[]{:S(2)}) copy-start(s32[32,4]{0,1:T(4,128)} %param.10) | copy-start | bytes 1540
  120.4 10.0 %collective-permute-start.2 = (bf16[288,256]{1,0:T(8,128)(2,1)S(1)}, bf16[288,256]{1,0:T(8,128)(2,1)S(1)}, u32[]{:S(2)}, u32[]{:S(2)}) collective-permute-start(bf16[288,256]{1,0:T(8,128)(2,1)S(1)} %get-tuple-element.9.own), channel_id=1, source_target_pairs={{0,576},{192,0},{384,192},{576,384},{1,577},{193,1},{385,193},{577... | collective-permute-start | bytes 442376 | tf_op jit(solution)/shard_map/ppermute | solution.py:218
  123.3 8.5 %collective-permute-start.1 = (bf16[288,256]{1,0:T(8,128)(2,1)S(1)}, bf16[288,256]{1,0:T(8,128)(2,1)S(1)}, u32[]{:S(2)}, u32[]{:S(2)}) collective-permute-start(bf16[288,256]{1,0:T(8,128)(2,1)S(1)} %get-tuple-element.9.own), channel_id=1, source_target_pairs={{0,384},{192,576},{384,0},{576,192},{1,385},{193,577},{385,1},{577... | collective-permute-start | bytes 442376 | tf_op jit(solution)/shard_map/ppermute | solution.py:218
  126.4 8.6 %collective-permute-start = (bf16[288,256]{1,0:T(8,128)(2,1)S(1)}, bf16[288,256]{1,0:T(8,128)(2,1)S(1)}, u32[]{:S(2)}, u32[]{:S(2)}) collective-permute-start(bf16[288,256]{1,0:T(8,128)(2,1)S(1)} %get-tuple-element.9.own), channel_id=1, source_target_pairs={{0,192},{192,384},{384,576},{576,0},{1,193},{193,385},{385,577},{5... | collective-permute-start | bytes 442376 | tf_op jit(solution)/shard_map/ppermute | solution.py:218

commit v5 on v3

--- a/solution.py
+++ b/solution.py
@@ -85,7 +85,7 @@
     )
 
 
-def grad_kernel(owners_in, acts_in, cot_in, stats_in, out, owners, acts, cot, stats, turned, sems):
+def grad_kernel(owners_in, acts_in, cot_in, stats_in, sent, owners, acts, cot, stats, turned, out, sems, out_sems):
     copies = start_copies(
         [(acts_in, acts), (owners_in, owners)]
         + [(cot_in.at[:, i * W : (i + 1) * W], cot.at[:, i * W : (i + 1) * W]) for i in range(4)]
@@ -95,22 +95,25 @@
     for r in range(2):
         for i in range(4):
             out[i, r * EACH + W : (r + 1) * EACH, :] = jnp.zeros((PACK, W), BF)
-    copies[0].wait()
+    for at in (1, 6, 7, 0):
+        copies[at].wait()
     turned[...] = acts[...].T
+    sends = []
     for i in range(4):
         copies[2 + i].wait()
         part = jnp.dot(turned[...], cot[:, i * W : (i + 1) * W], preferred_element_type=F32).astype(BF)
         for r in range(2):
             out[i, r * EACH : r * EACH + W, :] = part[r * W : (r + 1) * W, :]
-    for at in (1, 6, 7):
-        copies[at].wait()
-    for r in range(2):
-        for i in range(4):
             mine, slot = mine_and_slot(owners, r * 4 + i)
 
             @pl.when(mine)
             def _(i=i, r=r, slot=slot):
                 pack(stats[jnp.minimum(slot, 1)], out.at[i], r * EACH + W)
+
+        sends.append(pltpu.make_async_copy(out.at[i], sent.at[i], out_sems.at[i]))
+        sends[-1].start()
+    for send in sends:
+        send.wait()
 
 
 def sum_kernel(tiles, out):
@@ -172,57 +175,79 @@
         out[wide((x + (4 - k)) % 4), :] = part
 
 
-def renew(owners, block, packed, start, stats, stats_new):
-    mine, slot = mine_and_slot(owners, block)
-
-    @pl.when(mine)
-    def _():
-        at = jnp.minimum(slot, 1)
-        stats_new[at] = decay_rate * stats[at] + (1.0 - decay_rate) * unpack(packed, start)
-
-
-def finish_kernel(
-    owners_in, own, first, second_top, second_low, third, weight_in, stats_in,
-    weight_out, stats_out, owners, weight, stats, new, stats_new, sems, out_sems
-):
+def finish_kernel(owners_in, own, first, third, weight_in, stats_in, weight_out, stats_out, owners, weight, stats, new, stats_new, sems, out_sems):
     x = lax.axis_index("x")
-    columns = [(x + (4 - k)) % 4 for k in range(4)]
+    columns = [x, (x + 3) % 4, (x + 1) % 4]
     copies = start_copies(
         [(owners_in, owners)]
         + [(stats_in.at[0, 0, k], stats.at[k]) for k in range(2)]
         + [(weight_in.at[:, wide(c)], weight.at[k]) for k, c in enumerate(columns)],
         sems,
     )
-    halves = [[(own, 0), (own, EACH)], [(first, 0), (first, EACH)], [(second_top, 0), (second_low, 0)], [(third, 0), (third, EACH)]]
     sends = []
-    for k in range(4):
+    for k, part in enumerate((own, first, third)):
         copies[3 + k].wait()
-        for r, (part, start) in enumerate(halves[k]):
+        for r in range(2):
             rows = slice(r * W, (r + 1) * W)
-            new[k, rows, :] = weight[k, rows, :] - step_rate * part[start : start + W, :].astype(F32)
-        send = pltpu.make_async_copy(new.at[k], weight_out.at[:, wide(columns[k])], out_sems.at[k])
-        send.start()
-        sends.append(send)
+            new[k, rows, :] = weight[k, rows, :] - step_rate * part[r * EACH : r * EACH + W, :].astype(F32)
+        sends.append(pltpu.make_async_copy(new.at[k], weight_out.at[:, wide(columns[k])], out_sems.at[k]))
+        sends[-1].start()
     for at in range(3):
         copies[at].wait()
     stats_new[...] = jnp.zeros(stats_new.shape, F32)
-    for k in range(4):
-        for r, (part, start) in enumerate(halves[k]):
-            renew(owners, r * 4 + columns[k], part, start + W, stats, stats_new)
-    send = pltpu.make_async_copy(stats_new, stats_out.at[0, 0], out_sems.at[4])
-    send.start()
-    sends.append(send)
+    for k, part in enumerate((own, first, third)):
+        for r in range(2):
+            mine, slot = mine_and_slot(owners, r * 4 + columns[k])
+
+            @pl.when(mine)
+            def _(r=r, part=part, slot=slot):
+                at = jnp.minimum(slot, 1)
+                stats_new[at] = decay_rate * stats[at] + (1.0 - decay_rate) * unpack(part, r * EACH + W)
+
+    sends.append(pltpu.make_async_copy(stats_new, stats_out.at[0, 0], out_sems.at[3]))
+    sends[-1].start()
     for send in sends:
         send.wait()
 
 
-def call(kernel, out, *args, specs=None, out_specs=None, scratch=(), mib=32):
+def last_kernel(owners_in, top, low, weight_in, stats_in, weight_part, stats_part, weight_out, stats_out, owners, weight, stats, new, stats_new, sems, out_sems):
+    column = (lax.axis_index("x") + 2) % 4
+    copies = start_copies(
+        [(owners_in, owners)]
+        + [(stats_in.at[0, 0, k], stats.at[k]) for k in range(2)]
+        + [(weight_in.at[:, wide(column)], weight)],
+        sems,
+    )
+    copies[3].wait()
+    for r, part in enumerate((top, low)):
+        rows = slice(r * W, (r + 1) * W)
+        new[rows, :] = weight[rows, :] - step_rate * part[:W, :].astype(F32)
+    send = pltpu.make_async_copy(new, weight_out.at[:, wide(column)], out_sems.at[0])
+    send.start()
+    for at in range(3):
+        copies[at].wait()
+    for r, part in enumerate((top, low)):
+        mine, slot = mine_and_slot(owners, r * 4 + column)
+
+        @pl.when(mine)
+        def _(r=r, part=part, slot=slot):
+            at = jnp.minimum(slot, 1)
+            stats_new[...] = decay_rate * stats[at] + (1.0 - decay_rate) * unpack(part, W)
+            keep = pltpu.make_async_copy(stats_new, stats_out.at[0, 0, at], out_sems.at[1])
+            keep.start()
+            keep.wait()
+
+    send.wait()
+
+
+def call(kernel, out, *args, specs=None, out_specs=None, scratch=(), mib=32, aliases=None):
     return pl.pallas_call(
         kernel,
         out_shape=out,
         in_specs=specs or [IN_VMEM] * len(args),
         out_specs=out_specs or jax.tree.map(lambda _: IN_VMEM, out),
         scratch_shapes=list(scratch),
+        input_output_aliases=aliases or {},
         compiler_params=room(mib),
     )(*args)
 
@@ -257,22 +282,24 @@
             pltpu.VMEM((tokens, columns), BF),
             pltpu.VMEM((2, W, W), F32),
             pltpu.VMEM((rows_dev, tokens), BF),
+            pltpu.VMEM((n_x, SENT, W), BF),
             dma((8,)),
+            dma((n_x,)),
         ],
+        out_specs=IN_HBM,
         mib=60,
     )
     share = SENT // n_zl
     column = call(sum_kernel, shape((1, SENT, W), BF), swap(sent, "x"))
     column, acts = lax.optimization_barrier((column, next_acts))
-    acts_1, acts_3 = turn(acts, "x", 1), turn(acts, "x", 3)
+    acts_3 = turn(acts, "x", 3)
     tiles = swap(column.reshape(n_zl, share, W), "zl")
-    tiles, acts, acts_1, acts_3 = lax.optimization_barrier((tiles, next_acts, acts_1, acts_3))
-    part = call(sum_kernel, shape((n_zh, share, W), BF), tiles)
-    part, acts = lax.optimization_barrier((part, acts))
+    tiles, acts_3 = lax.optimization_barrier((tiles, acts_3))
+    part, acts = lax.optimization_barrier((call(sum_kernel, shape((n_zh, share, W), BF), tiles), acts))
     acts_2 = turn(acts, "x", 2)
-    tiles = swap(part, "zh")
-    tiles, acts_2 = lax.optimization_barrier((tiles, acts_2))
-    mine = call(sum_kernel, shape((n_zl, share, W), BF), tiles)
+    tiles, acts_2 = lax.optimization_barrier((swap(part, "zh"), acts_2))
+    mine, acts = lax.optimization_barrier((call(sum_kernel, shape((n_zl, share, W), BF), tiles), acts))
+    acts_1 = turn(acts, "x", 1)
     full = swap(mine, "zl").reshape(SENT, W)
     moved, partial_next = call(
         root_kernel,
@@ -289,27 +316,48 @@
     tiles = swap(partial_next.reshape(n_feat, columns // n_feat, tokens), "feat")
     moved_1, moved_3 = turn(moved, "x", 1), turn(moved, "x", 3)
     moved_2 = turn(moved_1[:EACH], "x", 1), turn(moved_3[EACH:], "x", 3)
-    weight_new, stats_new = call(
+    outs = [shape(weight.shape, F32), shape(stats_old.shape, F32)]
+    begun = call(
         finish_kernel,
-        [shape(weight.shape, F32), shape(stats_old.shape, F32)],
+        outs,
         owners,
         moved,
         moved_1,
-        *moved_2,
         moved_3,
         weight,
         stats_old,
-        specs=[IN_HBM] + [IN_VMEM] * 5 + [IN_HBM] * 2,
+        specs=[IN_HBM] + [IN_VMEM] * 3 + [IN_HBM] * 2,
         out_specs=[IN_HBM, IN_HBM],
         scratch=[
             pltpu.SMEM(owners.shape, jnp.int32),
-            pltpu.VMEM((n_x, rows_dev, W), F32),
+            pltpu.VMEM((3, rows_dev, W), F32),
             pltpu.VMEM((2, W, W), F32),
-            pltpu.VMEM((n_x, rows_dev, W), F32),
+            pltpu.VMEM((3, rows_dev, W), F32),
             pltpu.VMEM((2, W, W), F32),
-            dma((7,)),
-            dma((5,)),
+            dma((6,)),
+            dma((4,)),
         ],
+    )
+    weight_new, stats_new = call(
+        last_kernel,
+        outs,
+        owners,
+        *moved_2,
+        weight,
+        stats_old,
+        *begun,
+        specs=[IN_HBM] + [IN_VMEM] * 2 + [IN_HBM] * 4,
+        out_specs=[IN_HBM, IN_HBM],
+        scratch=[
+            pltpu.SMEM(owners.shape, jnp.int32),
+            pltpu.VMEM((rows_dev, W), F32),
+            pltpu.VMEM((2, W, W), F32),
+            pltpu.VMEM((rows_dev, W), F32),
+            pltpu.VMEM((W, W), F32),
+            dma((4,)),
+            dma((2,)),
+        ],
+        aliases={5: 0, 6: 1},
     )
     summed = jnp.sum(tiles.astype(F32), axis=0).astype(BF)
     each = n_feat // n_x

time: 138 us -> 139 us (level)
  blocking collectives: 35.7 us -> 24.1 us
  waiting for transfers between devices: 25.6 us -> 35.1 us
  Pallas kernels: 14.6 us -> 16.8 us
    all_to_all x2 -> x1, blocking collectives: 35.7 us -> 24.1 us  [swap(): return lax.all_to_all(x, axis, 0, 0, tiled=True)]
    ppermute x7, waiting for transfers between devices: 17 us -> 25.7 us  [turn(): return lax.ppermute(x, axis, [(i, (i + by) % n) for i in range(n)])]
    all_to_all x3 -> x4, starting transfers between devices: 26.1 us -> 29.6 us  [swap(): return lax.all_to_all(x, axis, 0, 0, tiled=True)]
    ppermute x7, starting transfers between devices: 26.3 us -> 23.7 us  [turn(): return lax.ppermute(x, axis, [(i, (i + by) % n) for i in range(n)])]
    all_to_all x3 -> x4, waiting for transfers between devices: 4.63 us -> 7.05 us  [swap(): return lax.all_to_all(x, axis, 0, 0, tiled=True)]
    pallas_call x6 -> x7, Pallas kernels: 14.6 us -> 16.8 us  [call(): pl.pallas_call(kernel, out_shape=out, in_specs=specs or [IN_VMEM] * len(a...]
    ppermute x1, waiting for transfers between devices: 4 us -> 2.3 us  [body(): next_out = lax.ppermute(summed, ('x', 'feat'), pairs).T]
  transfers between devices with their start and end apart: 11 -> 12, of which waited for: 6 -> 8; matrix products, arithmetic and copies ran while one was open for 2% -> 2% of each run, Pallas kernels for 2% -> 3%
where the time goes in v5:
time: 139 us; the launch traced here: 138 us
  starting transfers between devices  58.3 us (42%)
  waiting for transfers between devices  35.1 us (25%)
  blocking collectives  24.1 us (17%)
  Pallas kernels  16.8 us (12%)
  local copies, waits for them, and re-layouts  2.03 us (1%)
    all_to_all x4, starting transfers between devices, swap(): return lax.all_to_all(x, axis, 0, 0, tiled=True)  29.6 us
    ppermute x7, waiting for transfers between devices, turn(): return lax.ppermute(x, axis, [(i, (i + by) % n) for i in range(n)])  25.7 us
    all_to_all x1, blocking collectives, swap(): return lax.all_to_all(x, axis, 0, 0, tiled=True)  24.1 us
    ppermute x7, starting transfers between devices, turn(): return lax.ppermute(x, axis, [(i, (i + by) % n) for i in range(n)])  23.7 us
    pallas_call x7, Pallas kernels, call(): pl.pallas_call(kernel, out_shape=out, in_specs=specs or [IN_VMEM] * len(a...  16.8 us
    all_to_all x4, waiting for transfers between devices, swap(): return lax.all_to_all(x, axis, 0, 0, tiled=True)  7.05 us
    ppermute x1, starting transfers between devices, body(): next_out = lax.ppermute(summed, ('x', 'feat'), pairs).T  4.96 us
  transfers between devices with their start and end apart: 12, of which 8 were waited for; matrix products, arithmetic and copies ran while one was open for 2% of the time, Pallas kernels for 3%

profile of v5, /device:TPU:22, one launch (start us, length us, event | category | flops | bytes accessed | tf_op | source)
XLA Modules:
  0.0 138.2 jit_solution(2522228409121125859)
XLA Ops:
  0.6 3.5 %shard_map.85 = bf16[4,800,256]{2,1,0:T(8,128)(2,1)} custom-call(s32[4,32]{1,0:T(4,128)} %bitcast.6, bf16[256,512]{1,0:T(8,128)(2,1)} %acts_in.1, bf16[256,1024]{1,0:T(8,128)(2,1)} %cot_in.1, f32[1,1,2,256,256]{4,3,2,1,0:T(8,128)} %stats_in.5), custom_call_target="tpu_custom_call" | custom-call | tf_op jit(solution)/shard_map/pallas_call | solution.py:244
  4.1 24.1 %all_to_all.25.tiles = bf16[4,800,256]{2,1,0:T(8,128)(2,1)S(1)} all-to-all(bf16[4,800,256]{2,1,0:T(8,128)(2,1)} %shard_map.85), channel_id=1, replica_groups=mesh['x'=4,'zh'=3,'zl'=4,'feat'=16] {'x'}, dimensions={0} | all-to-all | bytes 3276800 | tf_op jit(solution)/shard_map/all_to_all | solution.py:256
  28.3 0.0 copy-start.2
  28.3 1.0 shard_map.86
  29.2 0.0 copy-start
  29.2 7.4 %all-to-all-start.1 = ((bf16[4,200,256]{2,1,0:T(8,128)(2,1)}), bf16[4,200,256]{2,1,0:T(8,128)(2,1)S(1)}, u32[]{:S(2)}, u32[]{:S(2)}) async-start(bf16[4,200,256]{2,1,0:T(8,128)(2,1)} %bitcast.1), calls=%async_computation.1 | async-start | bytes 819200 | tf_op jit(solution)/shard_map/all_to_all | solution.py:256
  36.6 0.0 copy-done.2
  36.6 2.3 %collective-permute-start = (bf16[256,512]{1,0:T(8,128)(2,1)S(1)}, bf16[256,512]{1,0:T(8,128)(2,1)S(1)}, u32[]{:S(2)}, u32[]{:S(2)}) collective-permute-start(bf16[256,512]{1,0:T(8,128)(2,1)S(1)} %copy-done.2), channel_id=1, source_target_pairs={{0,576},{192,0},{384,192},{576,384},{1,577},{193,1},{385,193},{577... | collective-permute-start | bytes 786440 | tf_op jit(solution)/shard_map/ppermute | solution.py:261
  38.9 7.2 %collective-permute-done.third = bf16[256,512]{1,0:T(8,128)(2,1)S(1)} collective-permute-done((bf16[256,512]{1,0:T(8,128)(2,1)S(1)}, bf16[256,512]{1,0:T(8,128)(2,1)S(1)}, u32[]{:S(2)}, u32[]{:S(2)}) %collective-permute-start) | collective-permute-done | bytes 262176 | tf_op jit(solution)/shard_map/ppermute | solution.py:261
  46.1 1.1 all-to-all-done.1.tiles
  47.1 0.8 shard_map.87
  47.9 11.3 %all-to-all-start.2 = ((bf16[3,200,256]{2,1,0:T(8,128)(2,1)}), bf16[3,200,256]{2,1,0:T(8,128)(2,1)S(1)}, u32[]{:S(2)}, u32[]{:S(2)}) async-start(bf16[3,200,256]{2,1,0:T(8,128)(2,1)} %shard_map.87), calls=%async_computation.2 | async-start | bytes 614400 | tf_op jit(solution)/shard_map/all_to_all | solution.py:256
  59.2 4.0 %collective-permute-start.1 = (bf16[256,512]{1,0:T(8,128)(2,1)S(1)}, bf16[256,512]{1,0:T(8,128)(2,1)S(1)}, u32[]{:S(2)}, u32[]{:S(2)}) collective-permute-start(bf16[256,512]{1,0:T(8,128)(2,1)S(1)} %copy-done.2), channel_id=1, source_target_pairs={{0,384},{192,576},{384,0},{576,192},{1,385},{193,577},{385,1},{577... | collective-permute-start | bytes 786440 | tf_op jit(solution)/shard_map/ppermute | solution.py:261
  63.2 5.8 %collective-permute-done.1.second = bf16[256,512]{1,0:T(8,128)(2,1)S(1)} collective-permute-done((bf16[256,512]{1,0:T(8,128)(2,1)S(1)}, bf16[256,512]{1,0:T(8,128)(2,1)S(1)}, u32[]{:S(2)}, u32[]{:S(2)}) %collective-permute-start.1) | collective-permute-done | bytes 262176 | tf_op jit(solution)/shard_map/ppermute | solution.py:261
  69.0 3.6 %all-to-all-done.2.tiles = bf16[3,200,256]{2,1,0:T(8,128)(2,1)S(1)} async-done(((bf16[3,200,256]{2,1,0:T(8,128)(2,1)}), bf16[3,200,256]{2,1,0:T(8,128)(2,1)S(1)}, u32[]{:S(2)}, u32[]{:S(2)}) %all-to-all-start.2) | async-done | bytes 307232 | tf_op jit(solution)/shard_map/all_to_all | solution.py:256
  72.6 0.8 shard_map.88
  73.4 3.5 %all-to-all-start.3 = ((bf16[4,200,256]{2,1,0:T(8,128)(2,1)}), bf16[4,200,256]{2,1,0:T(8,128)(2,1)S(1)}, u32[]{:S(2)}, u32[]{:S(2)}) async-start(bf16[4,200,256]{2,1,0:T(8,128)(2,1)} %shard_map.88), calls=%async_computation.3 | async-start | bytes 819200 | tf_op jit(solution)/shard_map/all_to_all | solution.py:256
  76.9 3.4 %collective-permute-start.2 = (bf16[256,512]{1,0:T(8,128)(2,1)S(1)}, bf16[256,512]{1,0:T(8,128)(2,1)S(1)}, u32[]{:S(2)}, u32[]{:S(2)}) collective-permute-start(bf16[256,512]{1,0:T(8,128)(2,1)S(1)} %copy-done.2), channel_id=1, source_target_pairs={{0,192},{192,384},{384,576},{576,0},{1,193},{193,385},{385,577},{5... | collective-permute-start | bytes 786440 | tf_op jit(solution)/shard_map/ppermute | solution.py:261
  80.2 5.0 %collective-permute-done.2.first = bf16[256,512]{1,0:T(8,128)(2,1)S(1)} collective-permute-done((bf16[256,512]{1,0:T(8,128)(2,1)S(1)}, bf16[256,512]{1,0:T(8,128)(2,1)S(1)}, u32[]{:S(2)}, u32[]{:S(2)}) %collective-permute-start.2) | collective-permute-done | bytes 262176 | tf_op jit(solution)/shard_map/ppermute | solution.py:261
  85.2 2.3 %all-to-all-done.3 = bf16[4,200,256]{2,1,0:T(8,128)(2,1)S(1)} async-done(((bf16[4,200,256]{2,1,0:T(8,128)(2,1)}), bf16[4,200,256]{2,1,0:T(8,128)(2,1)S(1)}, u32[]{:S(2)}, u32[]{:S(2)}) %all-to-all-start.3) | async-done | bytes 409632 | tf_op jit(solution)/shard_map/all_to_all | solution.py:256
  87.5 0.0 copy-done
  87.6 6.0 %shard_map.89 = (bf16[800,256]{1,0:T(8,128)(2,1)}, bf16[1024,256]{1,0:T(8,128)(2,1)}) custom-call(bf16[800,256]{1,0:T(8,128)(2,1)S(1)} %bitcast.5, f32[512,1024]{1,0:T(8,128)S(1)} %copy-done, bf16[256,512]{1,0:T(8,128)(2,1)S(1)} %copy-done.2, bf16[256,512]{1,0:T(8,128)(2,1)S(1)} %collective-permute-done.2.first, ...), custom_call_target="tpu_custom_call" | custom-call | tf_op jit(solution)/shard_map/pallas_call | solution.py:244
  93.6 0.0 copy-start.1
  93.6 0.0 copy-start.3
  93.6 7.5 %all-to-all-start.4 = ((bf16[16,64,256]{2,1,0:T(8,128)(2,1)}), bf16[16,64,256]{2,1,0:T(8,128)(2,1)}, u32[]{:S(2)}, u32[]{:S(2)}) async-start(bf16[16,64,256]{2,1,0:T(8,128)(2,1)} %bitcast.3), calls=%async_computation.4 | async-start | bytes 1048576 | tf_op jit(solution)/shard_map/all_to_all | solution.py:256
  101.1 3.1 %collective-permute-start.5 = (bf16[800,256]{1,0:T(8,128)(2,1)}, bf16[800,256]{1,0:T(8,128)(2,1)S(1)}, u32[]{:S(2)}, u32[]{:S(2)}) collective-permute-start(bf16[800,256]{1,0:T(8,128)(2,1)} %get-tuple-element.29.own), channel_id=1, source_target_pairs={{0,576},{192,0},{384,192},{576,384},{1,577},{193,1},{385,193},{577... | collective-permute-start | bytes 1228808 | tf_op jit(solution)/shard_map/ppermute | solution.py:261
  104.2 4.0 %collective-permute-start.3 = (bf16[800,256]{1,0:T(8,128)(2,1)}, bf16[800,256]{1,0:T(8,128)(2,1)S(1)}, u32[]{:S(2)}, u32[]{:S(2)}) collective-permute-start(bf16[800,256]{1,0:T(8,128)(2,1)} %get-tuple-element.29.own), channel_id=1, source_target_pairs={{0,192},{192,384},{384,576},{576,0},{1,193},{193,385},{385,577},{5... | collective-permute-start | bytes 1228808 | tf_op jit(solution)/shard_map/ppermute | solution.py:261
  108.2 7.8 %collective-permute-done.5.third = bf16[800,256]{1,0:T(8,128)(2,1)S(1)} collective-permute-done((bf16[800,256]{1,0:T(8,128)(2,1)}, bf16[800,256]{1,0:T(8,128)(2,1)S(1)}, u32[]{:S(2)}, u32[]{:S(2)}) %collective-permute-start.5) | collective-permute-done | bytes 409632 | tf_op jit(solution)/shard_map/ppermute | solution.py:261
  115.9 0.7 slice.9
  116.6 1.9 %collective-permute-start.6 = (bf16[400,256]{1,0:T(8,128)(2,1)}, bf16[400,256]{1,0:T(8,128)(2,1)}, u32[]{:S(2)}, u32[]{:S(2)}) collective-permute-start(bf16[400,256]{1,0:T(8,128)(2,1)} %slice.9), channel_id=1, source_target_pairs={{0,576},{192,0},{384,192},{576,384},{1,577},{193,1},{385,193},{577... | collective-permute-start | bytes 614408 | tf_op jit(solution)/shard_map/ppermute | solution.py:261
  118.5 0.0 collective-permute-done.3.first
  118.6 0.7 slice.8
  119.3 5.1 %collective-permute-start.4 = (bf16[400,256]{1,0:T(8,128)(2,1)}, bf16[400,256]{1,0:T(8,128)(2,1)}, u32[]{:S(2)}, u32[]{:S(2)}) collective-permute-start(bf16[400,256]{1,0:T(8,128)(2,1)} %slice.8), channel_id=1, source_target_pairs={{0,192},{192,384},{384,576},{576,0},{1,193},{193,385},{385,577},{5... | collective-permute-start | bytes 614408 | tf_op jit(solution)/shard_map/ppermute | solution.py:261
  124.4 0.0 all-to-all-done.4
  124.4 1.1 reduce_sum.12
  125.5 5.0 %collective-permute-start.7 = (bf16[64,256]{1,0:T(8,128)(2,1)S(1)}, bf16[64,256]{1,0:T(8,128)(2,1)S(1)}, u32[]{:S(2)}, u32[]{:S(2)}) collective-permute-start(bf16[64,256]{1,0:T(8,128)(2,1)S(1)} %reduce_sum.12), channel_id=1, source_target_pairs={{0,0},{1,1},{2,2},{3,3},{4,192},{5,193},{6,194},{7,195},{8,384},{9... | collective-permute-start | bytes 98312 | tf_op jit(solution)/shard_map/ppermute | solution.py:370
  130.5 0.0 copy-done.1
  130.5 0.0 copy-done.3
  130.5 2.7 %shard_map.90 = (f32[512,1024]{1,0:T(8,128)}, f32[1,1,2,256,256]{4,3,2,1,0:T(8,128)}) custom-call(s32[4,32]{1,0:T(4,128)S(1)} %bitcast.7, bf16[800,256]{1,0:T(8,128)(2,1)} %get-tuple-element.29.own, bf16[800,256]{1,0:T(8,128)(2,1)S(1)} %collective-permute-done.3.first, bf16[800,256]{1,0:T(8,128)(2,1)S(1)} %collective-permute-done.5.third, ...), custom_call_target="tpu_custom_call" | custom-call | tf_op jit(solution)/shard_map/pallas_call | solution.py:244
  133.2 0.0 collective-permute-done.6.low
  133.3 0.0 collective-permute-done.4.top
  133.3 2.1 %shard_map.91 = (f32[512,1024]{1,0:T(8,128)}, f32[1,1,2,256,256]{4,3,2,1,0:T(8,128)}) custom-call(s32[4,32]{1,0:T(4,128)S(1)} %bitcast.8, bf16[400,256]{1,0:T(8,128)(2,1)} %collective-permute-done.4.top, bf16[400,256]{1,0:T(8,128)(2,1)} %collective-permute-done.6.low, f32[512,1024]{1,0:T(8,128)S(1)} %copy-done, ...), custom_call_target="tpu_custom_call", output_to_operand_aliasing={{0}: (5, {}), {1}: (6, {})} | custom-call | tf_op jit(solution)/shard_map/pallas_call | solution.py:244
  135.3 2.3 %collective-permute-done.7 = bf16[64,256]{1,0:T(8,128)(2,1)S(1)} collective-permute-done((bf16[64,256]{1,0:T(8,128)(2,1)S(1)}, bf16[64,256]{1,0:T(8,128)(2,1)S(1)}, u32[]{:S(2)}, u32[]{:S(2)}) %collective-permute-start.7) | collective-permute-done | bytes 32800 | tf_op jit(solution)/shard_map/ppermute | solution.py:370
  137.6 0.6 copy.14
Async XLA Ops:
  28.3 8.3 %copy-start.2 = (bf16[256,512]{1,0:T(8,128)(2,1)S(1)}, bf16[256,512]{1,0:T(8,128)(2,1)}, u32[]{:S(2)}) copy-start(bf16[256,512]{1,0:T(8,128)(2,1)} %own.1) | copy-start | bytes 786436
  29.2 58.3 %copy-start = (f32[512,1024]{1,0:T(8,128)S(1)}, f32[512,1024]{1,0:T(8,128)}, u32[]{:S(2)}) copy-start(f32[512,1024]{1,0:T(8,128)} %weight_in.5) | copy-start | bytes 6291460
  29.2 17.9 %all-to-all-start.1 = ((bf16[4,200,256]{2,1,0:T(8,128)(2,1)}), bf16[4,200,256]{2,1,0:T(8,128)(2,1)S(1)}, u32[]{:S(2)}, u32[]{:S(2)}) async-start(bf16[4,200,256]{2,1,0:T(8,128)(2,1)} %bitcast.1), calls=%async_computation.1 | async-start | bytes 819200 | tf_op jit(solution)/shard_map/all_to_all | solution.py:256
  36.6 9.5 %collective-permute-start = (bf16[256,512]{1,0:T(8,128)(2,1)S(1)}, bf16[256,512]{1,0:T(8,128)(2,1)S(1)}, u32[]{:S(2)}, u32[]{:S(2)}) collective-permute-start(bf16[256,512]{1,0:T(8,128)(2,1)S(1)} %copy-done.2), channel_id=1, source_target_pairs={{0,576},{192,0},{384,192},{576,384},{1,577},{193,1},{385,193},{577... | collective-permute-start | bytes 786440 | tf_op jit(solution)/shard_map/ppermute | solution.py:261
  47.9 24.7 %all-to-all-start.2 = ((bf16[3,200,256]{2,1,0:T(8,128)(2,1)}), bf16[3,200,256]{2,1,0:T(8,128)(2,1)S(1)}, u32[]{:S(2)}, u32[]{:S(2)}) async-start(bf16[3,200,256]{2,1,0:T(8,128)(2,1)} %shard_map.87), calls=%async_computation.2 | async-start | bytes 614400 | tf_op jit(solution)/shard_map/all_to_all | solution.py:256
  59.2 9.8 %collective-permute-start.1 = (bf16[256,512]{1,0:T(8,128)(2,1)S(1)}, bf16[256,512]{1,0:T(8,128)(2,1)S(1)}, u32[]{:S(2)}, u32[]{:S(2)}) collective-permute-start(bf16[256,512]{1,0:T(8,128)(2,1)S(1)} %copy-done.2), channel_id=1, source_target_pairs={{0,384},{192,576},{384,0},{576,192},{1,385},{193,577},{385,1},{577... | collective-permute-start | bytes 786440 | tf_op jit(solution)/shard_map/ppermute | solution.py:261
  73.4 14.2 %all-to-all-start.3 = ((bf16[4,200,256]{2,1,0:T(8,128)(2,1)}), bf16[4,200,256]{2,1,0:T(8,128)(2,1)S(1)}, u32[]{:S(2)}, u32[]{:S(2)}) async-start(bf16[4,200,256]{2,1,0:T(8,128)(2,1)} %shard_map.88), calls=%async_computation.3 | async-start | bytes 819200 | tf_op jit(solution)/shard_map/all_to_all | solution.py:256
  76.9 8.3 %collective-permute-start.2 = (bf16[256,512]{1,0:T(8,128)(2,1)S(1)}, bf16[256,512]{1,0:T(8,128)(2,1)S(1)}, u32[]{:S(2)}, u32[]{:S(2)}) collective-permute-start(bf16[256,512]{1,0:T(8,128)(2,1)S(1)} %copy-done.2), channel_id=1, source_target_pairs={{0,192},{192,384},{384,576},{576,0},{1,193},{193,385},{385,577},{5... | collective-permute-start | bytes 786440 | tf_op jit(solution)/shard_map/ppermute | solution.py:261
  93.6 36.9 %copy-start.1 = (f32[1,1,2,256,256]{4,3,2,1,0:T(8,128)S(1)}, f32[1,1,2,256,256]{4,3,2,1,0:T(8,128)}, u32[]{:S(2)}) copy-start(f32[1,1,2,256,256]{4,3,2,1,0:T(8,128)} %stats_in.5) | copy-start | bytes 1572868
  93.6 36.9 %copy-start.3 = (s32[32,4]{0,1:T(4,128)S(1)}, s32[32,4]{0,1:T(4,128)}, u32[]{:S(2)}) copy-start(s32[32,4]{0,1:T(4,128)} %param.10) | copy-start | bytes 1540
  93.6 30.8 %all-to-all-start.4 = ((bf16[16,64,256]{2,1,0:T(8,128)(2,1)}), bf16[16,64,256]{2,1,0:T(8,128)(2,1)}, u32[]{:S(2)}, u32[]{:S(2)}) async-start(bf16[16,64,256]{2,1,0:T(8,128)(2,1)} %bitcast.3), calls=%async_computation.4 | async-start | bytes 1048576 | tf_op jit(solution)/shard_map/all_to_all | solution.py:256
  101.1 14.8 %collective-permute-start.5 = (bf16[800,256]{1,0:T(8,128)(2,1)}, bf16[800,256]{1,0:T(8,128)(2,1)S(1)}, u32[]{:S(2)}, u32[]{:S(2)}) collective-permute-start(bf16[800,256]{1,0:T(8,128)(2,1)} %get-tuple-element.29.own), channel_id=1, source_target_pairs={{0,576},{192,0},{384,192},{576,384},{1,577},{193,1},{385,193},{577... | collective-permute-start | bytes 1228808 | tf_op jit(solution)/shard_map/ppermute | solution.py:261
  104.2 14.4 %collective-permute-start.3 = (bf16[800,256]{1,0:T(8,128)(2,1)}, bf16[800,256]{1,0:T(8,128)(2,1)S(1)}, u32[]{:S(2)}, u32[]{:S(2)}) collective-permute-start(bf16[800,256]{1,0:T(8,128)(2,1)} %get-tuple-element.29.own), channel_id=1, source_target_pairs={{0,192},{192,384},{384,576},{576,0},{1,193},{193,385},{385,577},{5... | collective-permute-start | bytes 1228808 | tf_op jit(solution)/shard_map/ppermute | solution.py:261
  116.6 16.6 %collective-permute-start.6 = (bf16[400,256]{1,0:T(8,128)(2,1)}, bf16[400,256]{1,0:T(8,128)(2,1)}, u32[]{:S(2)}, u32[]{:S(2)}) collective-permute-start(bf16[400,256]{1,0:T(8,128)(2,1)} %slice.9), channel_id=1, source_target_pairs={{0,576},{192,0},{384,192},{576,384},{1,577},{193,1},{385,193},{577... | collective-permute-start | bytes 614408 | tf_op jit(solution)/shard_map/ppermute | solution.py:261
  119.3 14.0 %collective-permute-start.4 = (bf16[400,256]{1,0:T(8,128)(2,1)}, bf16[400,256]{1,0:T(8,128)(2,1)}, u32[]{:S(2)}, u32[]{:S(2)}) collective-permute-start(bf16[400,256]{1,0:T(8,128)(2,1)} %slice.8), channel_id=1, source_target_pairs={{0,192},{192,384},{384,576},{576,0},{1,193},{193,385},{385,577},{5... | collective-permute-start | bytes 614408 | tf_op jit(solution)/shard_map/ppermute | solution.py:261
  125.5 12.1 %collective-permute-start.7 = (bf16[64,256]{1,0:T(8,128)(2,1)S(1)}, bf16[64,256]{1,0:T(8,128)(2,1)S(1)}, u32[]{:S(2)}, u32[]{:S(2)}) collective-permute-start(bf16[64,256]{1,0:T(8,128)(2,1)S(1)} %reduce_sum.12), channel_id=1, source_target_pairs={{0,0},{1,1},{2,2},{3,3},{4,192},{5,193},{6,194},{7,195},{8,384},{9... | collective-permute-start | bytes 98312 | tf_op jit(solution)/shard_map/ppermute | solution.py:370

commit v6 on v5

--- a/solution.py
+++ b/solution.py
@@ -87,20 +87,23 @@
 
 def grad_kernel(owners_in, acts_in, cot_in, stats_in, sent, owners, acts, cot, stats, turned, out, sems, out_sems):
     copies = start_copies(
-        [(acts_in, acts), (owners_in, owners)]
+        [(acts_in.at[:, i * H : (i + 1) * H], acts.at[:, i * H : (i + 1) * H]) for i in range(4)]
         + [(cot_in.at[:, i * W : (i + 1) * W], cot.at[:, i * W : (i + 1) * W]) for i in range(4)]
+        + [(owners_in, owners)]
         + [(stats_in.at[0, 0, k], stats.at[k]) for k in range(2)],
         sems,
     )
     for r in range(2):
         for i in range(4):
             out[i, r * EACH + W : (r + 1) * EACH, :] = jnp.zeros((PACK, W), BF)
-    for at in (1, 6, 7, 0):
+    for i in range(4):
+        copies[i].wait()
+        turned[i * H : (i + 1) * H, :] = acts[:, i * H : (i + 1) * H].T
+    for at in (8, 9, 10):
         copies[at].wait()
-    turned[...] = acts[...].T
     sends = []
     for i in range(4):
-        copies[2 + i].wait()
+        copies[4 + i].wait()
         part = jnp.dot(turned[...], cot[:, i * W : (i + 1) * W], preferred_element_type=F32).astype(BF)
         for r in range(2):
             out[i, r * EACH : r * EACH + W, :] = part[r * W : (r + 1) * W, :]
@@ -110,8 +113,10 @@
             def _(i=i, r=r, slot=slot):
                 pack(stats[jnp.minimum(slot, 1)], out.at[i], r * EACH + W)
 
-        sends.append(pltpu.make_async_copy(out.at[i], sent.at[i], out_sems.at[i]))
-        sends[-1].start()
+        for r in range(2):
+            rows = pl.ds(r * EACH, EACH)
+            sends.append(pltpu.make_async_copy(out.at[i, rows], sent.at[i, rows], out_sems.at[2 * i + r]))
+            sends[-1].start()
     for send in sends:
         send.wait()
 
@@ -172,12 +177,21 @@
     new = jnp.concatenate(news, axis=0)
     for k in range(4):
         part = lax.dot_general(new, acts[k], (((0,), (1,)), ((), ())), preferred_element_type=F32).astype(BF)
-        out[wide((x + (4 - k)) % 4), :] = part
-
-
-def finish_kernel(owners_in, own, first, third, weight_in, stats_in, weight_out, stats_out, owners, weight, stats, new, stats_new, sems, out_sems):
+        out[(x + (4 - k)) % 4] = part
+
+
+def renewed_weight(halves, weight, new, out, sem):
+    for r, (part, start) in enumerate(halves):
+        rows = slice(r * W, (r + 1) * W)
+        new[rows, :] = weight[rows, :] - step_rate * part[start : start + W, :].astype(F32)
+    send = pltpu.make_async_copy(new, out, sem)
+    send.start()
+    return send
+
+
+def finish_kernel(owners_in, own, third, weight_in, stats_in, weight_out, stats_out, owners, weight, stats, new, stats_new, sems, out_sems):
     x = lax.axis_index("x")
-    columns = [x, (x + 3) % 4, (x + 1) % 4]
+    columns = [x, (x + 1) % 4]
     copies = start_copies(
         [(owners_in, owners)]
         + [(stats_in.at[0, 0, k], stats.at[k]) for k in range(2)]
@@ -185,17 +199,14 @@
         sems,
     )
     sends = []
-    for k, part in enumerate((own, first, third)):
+    for k, part in enumerate((own, third)):
         copies[3 + k].wait()
-        for r in range(2):
-            rows = slice(r * W, (r + 1) * W)
-            new[k, rows, :] = weight[k, rows, :] - step_rate * part[r * EACH : r * EACH + W, :].astype(F32)
-        sends.append(pltpu.make_async_copy(new.at[k], weight_out.at[:, wide(columns[k])], out_sems.at[k]))
-        sends[-1].start()
+        halves = (part, 0), (part, EACH)
+        sends.append(renewed_weight(halves, weight.at[k], new.at[k], weight_out.at[:, wide(columns[k])], out_sems.at[k]))
     for at in range(3):
         copies[at].wait()
     stats_new[...] = jnp.zeros(stats_new.shape, F32)
-    for k, part in enumerate((own, first, third)):
+    for k, part in enumerate((own, third)):
         for r in range(2):
             mine, slot = mine_and_slot(owners, r * 4 + columns[k])
 
@@ -204,40 +215,42 @@
                 at = jnp.minimum(slot, 1)
                 stats_new[at] = decay_rate * stats[at] + (1.0 - decay_rate) * unpack(part, r * EACH + W)
 
-    sends.append(pltpu.make_async_copy(stats_new, stats_out.at[0, 0], out_sems.at[3]))
+    sends.append(pltpu.make_async_copy(stats_new, stats_out.at[0, 0], out_sems.at[2]))
     sends[-1].start()
     for send in sends:
         send.wait()
 
 
-def last_kernel(owners_in, top, low, weight_in, stats_in, weight_part, stats_part, weight_out, stats_out, owners, weight, stats, new, stats_new, sems, out_sems):
-    column = (lax.axis_index("x") + 2) % 4
+def last_kernel(owners_in, first, top, low, weight_in, stats_in, weight_part, stats_part, weight_out, stats_out, owners, weight, stats, new, stats_new, sems, out_sems):
+    x = lax.axis_index("x")
+    columns = [(x + 3) % 4, (x + 2) % 4]
     copies = start_copies(
         [(owners_in, owners)]
         + [(stats_in.at[0, 0, k], stats.at[k]) for k in range(2)]
-        + [(weight_in.at[:, wide(column)], weight)],
+        + [(weight_in.at[:, wide(c)], weight.at[k]) for k, c in enumerate(columns)],
         sems,
     )
-    copies[3].wait()
-    for r, part in enumerate((top, low)):
-        rows = slice(r * W, (r + 1) * W)
-        new[rows, :] = weight[rows, :] - step_rate * part[:W, :].astype(F32)
-    send = pltpu.make_async_copy(new, weight_out.at[:, wide(column)], out_sems.at[0])
-    send.start()
+    blocks = [[(first, 0), (first, EACH)], [(top, 0), (low, 0)]]
+    sends = []
+    for k, halves in enumerate(blocks):
+        copies[3 + k].wait()
+        sends.append(renewed_weight(halves, weight.at[k], new.at[k], weight_out.at[:, wide(columns[k])], out_sems.at[k]))
     for at in range(3):
         copies[at].wait()
-    for r, part in enumerate((top, low)):
-        mine, slot = mine_and_slot(owners, r * 4 + column)
-
-        @pl.when(mine)
-        def _(r=r, part=part, slot=slot):
-            at = jnp.minimum(slot, 1)
-            stats_new[...] = decay_rate * stats[at] + (1.0 - decay_rate) * unpack(part, W)
-            keep = pltpu.make_async_copy(stats_new, stats_out.at[0, 0, at], out_sems.at[1])
-            keep.start()
-            keep.wait()
-
-    send.wait()
+    for k, halves in enumerate(blocks):
+        for r, (part, start) in enumerate(halves):
+            mine, slot = mine_and_slot(owners, r * 4 + columns[k])
+
+            @pl.when(mine)
+            def _(part=part, start=start, slot=slot):
+                at = jnp.minimum(slot, 1)
+                stats_new[...] = decay_rate * stats[at] + (1.0 - decay_rate) * unpack(part, start + W)
+                keep = pltpu.make_async_copy(stats_new, stats_out.at[0, 0, at], out_sems.at[2])
+                keep.start()
+                keep.wait()
+
+    for send in sends:
+        send.wait()
 
 
 def call(kernel, out, *args, specs=None, out_specs=None, scratch=(), mib=32, aliases=None):
@@ -283,8 +296,8 @@
             pltpu.VMEM((2, W, W), F32),
             pltpu.VMEM((rows_dev, tokens), BF),
             pltpu.VMEM((n_x, SENT, W), BF),
-            dma((8,)),
-            dma((n_x,)),
+            dma((11,)),
+            dma((2 * n_x,)),
         ],
         out_specs=IN_HBM,
         mib=60,
@@ -303,7 +316,7 @@
     full = swap(mine, "zl").reshape(SENT, W)
     moved, partial_next = call(
         root_kernel,
-        [shape((SENT, W), BF), shape((n_x * W, tokens), BF)],
+        [shape((SENT, W), BF), shape((n_x, W, tokens), BF)],
         full,
         weight,
         next_acts,
@@ -312,52 +325,53 @@
         acts_3,
         specs=[IN_VMEM] + [IN_HBM] * 5,
         scratch=[pltpu.VMEM((rows_dev, W), F32), pltpu.VMEM((n_x, tokens, rows_dev), BF), dma((5,))],
+        mib=60,
     )
     tiles = swap(partial_next.reshape(n_feat, columns // n_feat, tokens), "feat")
-    moved_1, moved_3 = turn(moved, "x", 1), turn(moved, "x", 3)
-    moved_2 = turn(moved_1[:EACH], "x", 1), turn(moved_3[EACH:], "x", 3)
+    moved_3, moved_2, moved_1 = turn(moved, "x", 3), turn(moved[:EACH], "x", 2), turn(moved, "x", 1)
+    moved_2 = moved_2, turn(moved_3[EACH:], "x", 3)
     outs = [shape(weight.shape, F32), shape(stats_old.shape, F32)]
     begun = call(
         finish_kernel,
         outs,
         owners,
         moved,
-        moved_1,
         moved_3,
         weight,
         stats_old,
-        specs=[IN_HBM] + [IN_VMEM] * 3 + [IN_HBM] * 2,
+        specs=[IN_HBM] + [IN_VMEM] * 2 + [IN_HBM] * 2,
         out_specs=[IN_HBM, IN_HBM],
         scratch=[
             pltpu.SMEM(owners.shape, jnp.int32),
-            pltpu.VMEM((3, rows_dev, W), F32),
+            pltpu.VMEM((2, rows_dev, W), F32),
             pltpu.VMEM((2, W, W), F32),
-            pltpu.VMEM((3, rows_dev, W), F32),
+            pltpu.VMEM((2, rows_dev, W), F32),
             pltpu.VMEM((2, W, W), F32),
-            dma((6,)),
-            dma((4,)),
+            dma((5,)),
+            dma((3,)),
         ],
     )
     weight_new, stats_new = call(
         last_kernel,
         outs,
         owners,
+        moved_1,
         *moved_2,
         weight,
         stats_old,
         *begun,
-        specs=[IN_HBM] + [IN_VMEM] * 2 + [IN_HBM] * 4,
+        specs=[IN_HBM] + [IN_VMEM] * 3 + [IN_HBM] * 4,
         out_specs=[IN_HBM, IN_HBM],
         scratch=[
             pltpu.SMEM(owners.shape, jnp.int32),
-            pltpu.VMEM((rows_dev, W), F32),
+            pltpu.VMEM((2, rows_dev, W), F32),
             pltpu.VMEM((2, W, W), F32),
-            pltpu.VMEM((rows_dev, W), F32),
+            pltpu.VMEM((2, rows_dev, W), F32),
             pltpu.VMEM((W, W), F32),
-            dma((4,)),
-            dma((2,)),
+            dma((5,)),
+            dma((3,)),
         ],
-        aliases={5: 0, 6: 1},
+        aliases={6: 0, 7: 1},
     )
     summed = jnp.sum(tiles.astype(F32), axis=0).astype(BF)
     each = n_feat // n_x

time: 139 us -> 138 us (level)
  the two profiles are of different devices: /device:TPU:22 before, /device:TPU:4 now
where the time goes in v6:
time: 138 us; the launch traced here: 137 us
  starting transfers between devices  63.5 us (46%)
  waiting for transfers between devices  25.6 us (19%)
  blocking collectives  24.6 us (18%)
  Pallas kernels  16.8 us (12%)
  local copies, waits for them, and re-layouts  4.7 us (3%)
    all_to_all x4, starting transfers between devices, swap(): return lax.all_to_all(x, axis, 0, 0, tiled=True)  29.1 us
    ppermute x7, starting transfers between devices, turn(): return lax.ppermute(x, axis, [(i, (i + by) % n) for i in range(n)])  24.8 us
    all_to_all x1, blocking collectives, swap(): return lax.all_to_all(x, axis, 0, 0, tiled=True)  24.6 us
    ppermute x7, waiting for transfers between devices, turn(): return lax.ppermute(x, axis, [(i, (i + by) % n) for i in range(n)])  18.3 us
    pallas_call x7, Pallas kernels, call(): pl.pallas_call(kernel, out_shape=out, in_specs=specs or [IN_VMEM] * len(a...  16.8 us
    ppermute x1, starting transfers between devices, body(): next_out = lax.ppermute(summed, ('x', 'feat'), pairs).T  9.66 us
    all_to_all x4, waiting for transfers between devices, swap(): return lax.all_to_all(x, axis, 0, 0, tiled=True)  7.29 us
  transfers between devices with their start and end apart: 12, of which 7 were waited for; matrix products, arithmetic and copies ran while one was open for 3% of the time, Pallas kernels for 3%

profile of v6, /device:TPU:4, one launch (start us, length us, event | category | flops | bytes accessed | tf_op | source)
XLA Modules:
  0.0 137.1 jit_solution(14370143468900420518)
XLA Ops:
  0.6 3.5 %shard_map.85 = bf16[4,800,256]{2,1,0:T(8,128)(2,1)} custom-call(s32[4,32]{1,0:T(4,128)} %bitcast.5, bf16[256,512]{1,0:T(8,128)(2,1)} %acts_in.1, bf16[256,1024]{1,0:T(8,128)(2,1)} %cot_in.1, f32[1,1,2,256,256]{4,3,2,1,0:T(8,128)} %stats_in.5), custom_call_target="tpu_custom_call" | custom-call | tf_op jit(solution)/shard_map/pallas_call | solution.py:257
  4.1 24.6 %all_to_all.25.tiles = bf16[4,800,256]{2,1,0:T(8,128)(2,1)S(1)} all-to-all(bf16[4,800,256]{2,1,0:T(8,128)(2,1)} %shard_map.85), channel_id=1, replica_groups=mesh['x'=4,'zh'=3,'zl'=4,'feat'=16] {'x'}, dimensions={0} | all-to-all | bytes 3276800 | tf_op jit(solution)/shard_map/all_to_all | solution.py:269
  28.7 1.0 shard_map.86
  29.7 6.4 %all-to-all-start.1 = ((bf16[4,200,256]{2,1,0:T(8,128)(2,1)}), bf16[4,200,256]{2,1,0:T(8,128)(2,1)S(1)}, u32[]{:S(2)}, u32[]{:S(2)}) async-start(bf16[4,200,256]{2,1,0:T(8,128)(2,1)} %bitcast.1), calls=%async_computation.1 | async-start | bytes 819200 | tf_op jit(solution)/shard_map/all_to_all | solution.py:269
  36.0 0.0 copy-done.5
  36.0 3.5 %collective-permute-start = (bf16[256,512]{1,0:T(8,128)(2,1)S(1)}, bf16[256,512]{1,0:T(8,128)(2,1)S(1)}, u32[]{:S(2)}, u32[]{:S(2)}) collective-permute-start(bf16[256,512]{1,0:T(8,128)(2,1)S(1)} %copy-done.5), channel_id=1, source_target_pairs={{0,576},{192,0},{384,192},{576,384},{1,577},{193,1},{385,193},{577... | collective-permute-start | bytes 786440 | tf_op jit(solution)/shard_map/ppermute | solution.py:274
  39.6 4.7 %collective-permute-done.third = bf16[256,512]{1,0:T(8,128)(2,1)S(1)} collective-permute-done((bf16[256,512]{1,0:T(8,128)(2,1)S(1)}, bf16[256,512]{1,0:T(8,128)(2,1)S(1)}, u32[]{:S(2)}, u32[]{:S(2)}) %collective-permute-start) | collective-permute-done | bytes 262176 | tf_op jit(solution)/shard_map/ppermute | solution.py:274
  44.3 2.4 %all-to-all-done.1.tiles = bf16[4,200,256]{2,1,0:T(8,128)(2,1)S(1)} async-done(((bf16[4,200,256]{2,1,0:T(8,128)(2,1)}), bf16[4,200,256]{2,1,0:T(8,128)(2,1)S(1)}, u32[]{:S(2)}, u32[]{:S(2)}) %all-to-all-start.1) | async-done | bytes 409632 | tf_op jit(solution)/shard_map/all_to_all | solution.py:269
  46.7 0.8 shard_map.87
  47.4 11.3 %all-to-all-start.2 = ((bf16[3,200,256]{2,1,0:T(8,128)(2,1)}), bf16[3,200,256]{2,1,0:T(8,128)(2,1)S(1)}, u32[]{:S(2)}, u32[]{:S(2)}) async-start(bf16[3,200,256]{2,1,0:T(8,128)(2,1)} %shard_map.87), calls=%async_computation.2 | async-start | bytes 614400 | tf_op jit(solution)/shard_map/all_to_all | solution.py:269
  58.7 4.3 %collective-permute-start.1 = (bf16[256,512]{1,0:T(8,128)(2,1)S(1)}, bf16[256,512]{1,0:T(8,128)(2,1)S(1)}, u32[]{:S(2)}, u32[]{:S(2)}) collective-permute-start(bf16[256,512]{1,0:T(8,128)(2,1)S(1)} %copy-done.5), channel_id=1, source_target_pairs={{0,384},{192,576},{384,0},{576,192},{1,385},{193,577},{385,1},{577... | collective-permute-start | bytes 786440 | tf_op jit(solution)/shard_map/ppermute | solution.py:274
  63.0 5.4 %collective-permute-done.1.second = bf16[256,512]{1,0:T(8,128)(2,1)S(1)} collective-permute-done((bf16[256,512]{1,0:T(8,128)(2,1)S(1)}, bf16[256,512]{1,0:T(8,128)(2,1)S(1)}, u32[]{:S(2)}, u32[]{:S(2)}) %collective-permute-start.1) | collective-permute-done | bytes 262176 | tf_op jit(solution)/shard_map/ppermute | solution.py:274
  68.5 2.5 %all-to-all-done.2.tiles = bf16[3,200,256]{2,1,0:T(8,128)(2,1)S(1)} async-done(((bf16[3,200,256]{2,1,0:T(8,128)(2,1)}), bf16[3,200,256]{2,1,0:T(8,128)(2,1)S(1)}, u32[]{:S(2)}, u32[]{:S(2)}) %all-to-all-start.2) | async-done | bytes 307232 | tf_op jit(solution)/shard_map/all_to_all | solution.py:269
  71.0 0.8 shard_map.88
  71.8 4.0 %all-to-all-start.3 = ((bf16[4,200,256]{2,1,0:T(8,128)(2,1)}), bf16[4,200,256]{2,1,0:T(8,128)(2,1)S(1)}, u32[]{:S(2)}, u32[]{:S(2)}) async-start(bf16[4,200,256]{2,1,0:T(8,128)(2,1)} %shard_map.88), calls=%async_computation.3 | async-start | bytes 819200 | tf_op jit(solution)/shard_map/all_to_all | solution.py:269
  75.8 4.2 %collective-permute-start.2 = (bf16[256,512]{1,0:T(8,128)(2,1)S(1)}, bf16[256,512]{1,0:T(8,128)(2,1)S(1)}, u32[]{:S(2)}, u32[]{:S(2)}) collective-permute-start(bf16[256,512]{1,0:T(8,128)(2,1)S(1)} %copy-done.5), channel_id=1, source_target_pairs={{0,192},{192,384},{384,576},{576,0},{1,193},{193,385},{385,577},{5... | collective-permute-start | bytes 786440 | tf_op jit(solution)/shard_map/ppermute | solution.py:274
  80.0 5.3 %collective-permute-done.2.first = bf16[256,512]{1,0:T(8,128)(2,1)S(1)} collective-permute-done((bf16[256,512]{1,0:T(8,128)(2,1)S(1)}, bf16[256,512]{1,0:T(8,128)(2,1)S(1)}, u32[]{:S(2)}, u32[]{:S(2)}) %collective-permute-start.2) | collective-permute-done | bytes 262176 | tf_op jit(solution)/shard_map/ppermute | solution.py:274
  85.3 2.4 %all-to-all-done.3 = bf16[4,200,256]{2,1,0:T(8,128)(2,1)S(1)} async-done(((bf16[4,200,256]{2,1,0:T(8,128)(2,1)}), bf16[4,200,256]{2,1,0:T(8,128)(2,1)S(1)}, u32[]{:S(2)}, u32[]{:S(2)}) %all-to-all-start.3) | async-done | bytes 409632 | tf_op jit(solution)/shard_map/all_to_all | solution.py:269
  87.6 0.0 copy-done.6
  87.6 0.0 copy-done.7
  87.6 0.0 copy-done.8
  87.6 0.7 copy-done.4
  88.4 7.0 %shard_map.89 = (bf16[800,256]{1,0:T(8,128)(2,1)}, bf16[4,256,256]{2,1,0:T(8,128)(2,1)}) custom-call(bf16[800,256]{1,0:T(8,128)(2,1)} %bitcast.8, f32[512,1024]{1,0:T(8,128)} %weight_in.5, bf16[256,512]{1,0:T(8,128)(2,1)} %own.1, bf16[256,512]{1,0:T(8,128)(2,1)} %copy-done.8, bf16[256,512]{1,0:T(8,128)(2,1)} %copy-done.7, bf16[256,512]{1,0:T(8,128)(2,1)} %copy-done.6), custom_call_target="tpu_custom_call" | custom-call | tf_op jit(solution)/shard_map/pallas_call | solution.py:257
  95.3 0.0 copy-start
  95.4 0.0 copy-start.3
  95.4 7.4 %all-to-all-start.4 = ((bf16[16,64,256]{2,1,0:T(8,128)(2,1)}), bf16[16,64,256]{2,1,0:T(8,128)(2,1)}, u32[]{:S(2)}, u32[]{:S(2)}) async-start(bf16[16,64,256]{2,1,0:T(8,128)(2,1)} %bitcast.9), calls=%async_computation.4 | async-start | bytes 1048576 | tf_op jit(solution)/shard_map/all_to_all | solution.py:269
  102.8 3.1 %collective-permute-start.5 = (bf16[800,256]{1,0:T(8,128)(2,1)}, bf16[800,256]{1,0:T(8,128)(2,1)S(1)}, u32[]{:S(2)}, u32[]{:S(2)}) collective-permute-start(bf16[800,256]{1,0:T(8,128)(2,1)} %get-tuple-element.29.own), channel_id=1, source_target_pairs={{0,576},{192,0},{384,192},{576,384},{1,577},{193,1},{385,193},{577... | collective-permute-start | bytes 1228808 | tf_op jit(solution)/shard_map/ppermute | solution.py:274
  105.9 2.7 %collective-permute-start.3 = (bf16[800,256]{1,0:T(8,128)(2,1)}, bf16[800,256]{1,0:T(8,128)(2,1)S(1)}, u32[]{:S(2)}, u32[]{:S(2)}) collective-permute-start(bf16[800,256]{1,0:T(8,128)(2,1)} %get-tuple-element.29.own), channel_id=1, source_target_pairs={{0,192},{192,384},{384,576},{576,0},{1,193},{193,385},{385,577},{5... | collective-permute-start | bytes 1228808 | tf_op jit(solution)/shard_map/ppermute | solution.py:274
  108.6 1.6 %slice.6 = bf16[400,256]{1,0:T(8,128)(2,1)} slice(bf16[800,256]{1,0:T(8,128)(2,1)} %get-tuple-element.29.own), slice={[0:400], [0:256]} | slice | bytes 409600 | tf_op jit(solution)/shard_map/slice | solution.py:331
  110.3 4.0 %collective-permute-start.4 = (bf16[400,256]{1,0:T(8,128)(2,1)}, bf16[400,256]{1,0:T(8,128)(2,1)}, u32[]{:S(2)}, u32[]{:S(2)}) collective-permute-start(bf16[400,256]{1,0:T(8,128)(2,1)} %slice.6), channel_id=1, source_target_pairs={{0,384},{192,576},{384,0},{576,192},{1,385},{193,577},{385,1},{577... | collective-permute-start | bytes 614408 | tf_op jit(solution)/shard_map/ppermute | solution.py:274
  114.3 2.9 %collective-permute-done.5.third = bf16[800,256]{1,0:T(8,128)(2,1)S(1)} collective-permute-done((bf16[800,256]{1,0:T(8,128)(2,1)}, bf16[800,256]{1,0:T(8,128)(2,1)S(1)}, u32[]{:S(2)}, u32[]{:S(2)}) %collective-permute-start.5) | collective-permute-done | bytes 409632 | tf_op jit(solution)/shard_map/ppermute | solution.py:274
  117.2 0.7 slice.8
  117.8 2.9 %collective-permute-start.6 = (bf16[400,256]{1,0:T(8,128)(2,1)}, bf16[400,256]{1,0:T(8,128)(2,1)}, u32[]{:S(2)}, u32[]{:S(2)}) collective-permute-start(bf16[400,256]{1,0:T(8,128)(2,1)} %slice.8), channel_id=1, source_target_pairs={{0,576},{192,0},{384,192},{576,384},{1,577},{193,1},{385,193},{577... | collective-permute-start | bytes 614408 | tf_op jit(solution)/shard_map/ppermute | solution.py:274
  120.7 0.0 all-to-all-done.4
  120.8 1.1 reduce_sum.12
  121.9 9.7 %collective-permute-start.7 = (bf16[64,256]{1,0:T(8,128)(2,1)S(1)}, bf16[64,256]{1,0:T(8,128)(2,1)S(1)}, u32[]{:S(2)}, u32[]{:S(2)}) collective-permute-start(bf16[64,256]{1,0:T(8,128)(2,1)S(1)} %reduce_sum.12), channel_id=1, source_target_pairs={{0,0},{1,1},{2,2},{3,3},{4,192},{5,193},{6,194},{7,195},{8,384},{9... | collective-permute-start | bytes 98312 | tf_op jit(solution)/shard_map/ppermute | solution.py:384
  131.5 0.0 copy-done.1
  131.5 0.0 copy-done
  131.6 0.0 copy-done.3
  131.6 0.0 copy-start.2
  131.6 1.0 copy-done.2
  132.6 1.6 %shard_map.90 = (f32[512,1024]{1,0:T(8,128)}, f32[1,1,2,256,256]{4,3,2,1,0:T(8,128)}) custom-call(s32[4,32]{1,0:T(4,128)S(1)} %bitcast.6, bf16[800,256]{1,0:T(8,128)(2,1)S(1)} %copy-done.2, bf16[800,256]{1,0:T(8,128)(2,1)S(1)} %collective-permute-done.5.third, f32[512,1024]{1,0:T(8,128)S(1)} %copy-done, f32[1,1,2,256,256]{4,3,2,1,0:T(8,128)S(1)} %copy-done.1), custom_call_target="tpu_custom_call" | custom-call | tf_op jit(solution)/shard_map/pallas_call | solution.py:257
  134.1 0.0 collective-permute-done.4.top
  134.1 0.0 collective-permute-done.3.first
  134.1 0.0 collective-permute-done.6.low
  134.2 2.3 %shard_map.91 = (f32[512,1024]{1,0:T(8,128)}, f32[1,1,2,256,256]{4,3,2,1,0:T(8,128)}) custom-call(s32[4,32]{1,0:T(4,128)S(1)} %bitcast.7, bf16[800,256]{1,0:T(8,128)(2,1)S(1)} %collective-permute-done.3.first, bf16[400,256]{1,0:T(8,128)(2,1)} %collective-permute-done.4.top, ...), custom_call_target="tpu_custom_call", output_to_operand_aliasing={{0}: (6, {}), {1}: (7, {})} | custom-call | tf_op jit(solution)/shard_map/pallas_call | solution.py:257
  136.5 0.0 collective-permute-done.7
  136.5 0.6 copy.14
  (6 shorter events, 0.0 us)
Async XLA Ops:
  28.7 7.3 %copy-start.5 = (bf16[256,512]{1,0:T(8,128)(2,1)S(1)}, bf16[256,512]{1,0:T(8,128)(2,1)}, u32[]{:S(2)}) copy-start(bf16[256,512]{1,0:T(8,128)(2,1)} %own.1) | copy-start | bytes 786436
  29.7 17.0 %all-to-all-start.1 = ((bf16[4,200,256]{2,1,0:T(8,128)(2,1)}), bf16[4,200,256]{2,1,0:T(8,128)(2,1)S(1)}, u32[]{:S(2)}, u32[]{:S(2)}) async-start(bf16[4,200,256]{2,1,0:T(8,128)(2,1)} %bitcast.1), calls=%async_computation.1 | async-start | bytes 819200 | tf_op jit(solution)/shard_map/all_to_all | solution.py:269
  36.0 8.3 %collective-permute-start = (bf16[256,512]{1,0:T(8,128)(2,1)S(1)}, bf16[256,512]{1,0:T(8,128)(2,1)S(1)}, u32[]{:S(2)}, u32[]{:S(2)}) collective-permute-start(bf16[256,512]{1,0:T(8,128)(2,1)S(1)} %copy-done.5), channel_id=1, source_target_pairs={{0,576},{192,0},{384,192},{576,384},{1,577},{193,1},{385,193},{577... | collective-permute-start | bytes 786440 | tf_op jit(solution)/shard_map/ppermute | solution.py:274
  44.3 43.3 %copy-start.6 = (bf16[256,512]{1,0:T(8,128)(2,1)}, bf16[256,512]{1,0:T(8,128)(2,1)S(1)}, u32[]{:S(2)}) copy-start(bf16[256,512]{1,0:T(8,128)(2,1)S(1)} %collective-permute-done.third) | copy-start | bytes 786436
  47.4 23.5 %all-to-all-start.2 = ((bf16[3,200,256]{2,1,0:T(8,128)(2,1)}), bf16[3,200,256]{2,1,0:T(8,128)(2,1)S(1)}, u32[]{:S(2)}, u32[]{:S(2)}) async-start(bf16[3,200,256]{2,1,0:T(8,128)(2,1)} %shard_map.87), calls=%async_computation.2 | async-start | bytes 614400 | tf_op jit(solution)/shard_map/all_to_all | solution.py:269
  58.7 9.8 %collective-permute-start.1 = (bf16[256,512]{1,0:T(8,128)(2,1)S(1)}, bf16[256,512]{1,0:T(8,128)(2,1)S(1)}, u32[]{:S(2)}, u32[]{:S(2)}) collective-permute-start(bf16[256,512]{1,0:T(8,128)(2,1)S(1)} %copy-done.5), channel_id=1, source_target_pairs={{0,384},{192,576},{384,0},{576,192},{1,385},{193,577},{385,1},{577... | collective-permute-start | bytes 786440 | tf_op jit(solution)/shard_map/ppermute | solution.py:274
  68.5 19.2 %copy-start.7 = (bf16[256,512]{1,0:T(8,128)(2,1)}, bf16[256,512]{1,0:T(8,128)(2,1)S(1)}, u32[]{:S(2)}) copy-start(bf16[256,512]{1,0:T(8,128)(2,1)S(1)} %collective-permute-done.1.second) | copy-start | bytes 786436
  71.8 15.9 %all-to-all-start.3 = ((bf16[4,200,256]{2,1,0:T(8,128)(2,1)}), bf16[4,200,256]{2,1,0:T(8,128)(2,1)S(1)}, u32[]{:S(2)}, u32[]{:S(2)}) async-start(bf16[4,200,256]{2,1,0:T(8,128)(2,1)} %shard_map.88), calls=%async_computation.3 | async-start | bytes 819200 | tf_op jit(solution)/shard_map/all_to_all | solution.py:269
  75.8 9.4 %collective-permute-start.2 = (bf16[256,512]{1,0:T(8,128)(2,1)S(1)}, bf16[256,512]{1,0:T(8,128)(2,1)S(1)}, u32[]{:S(2)}, u32[]{:S(2)}) collective-permute-start(bf16[256,512]{1,0:T(8,128)(2,1)S(1)} %copy-done.5), channel_id=1, source_target_pairs={{0,192},{192,384},{384,576},{576,0},{1,193},{193,385},{385,577},{5... | collective-permute-start | bytes 786440 | tf_op jit(solution)/shard_map/ppermute | solution.py:274
  85.2 2.4 %copy-start.8 = (bf16[256,512]{1,0:T(8,128)(2,1)}, bf16[256,512]{1,0:T(8,128)(2,1)S(1)}, u32[]{:S(2)}) copy-start(bf16[256,512]{1,0:T(8,128)(2,1)S(1)} %collective-permute-done.2.first) | copy-start | bytes 786436
  87.6 0.8 copy-start.4
  88.4 43.2 %copy-start.1 = (f32[1,1,2,256,256]{4,3,2,1,0:T(8,128)S(1)}, f32[1,1,2,256,256]{4,3,2,1,0:T(8,128)}, u32[]{:S(2)}) copy-start(f32[1,1,2,256,256]{4,3,2,1,0:T(8,128)} %stats_in.5) | copy-start | bytes 1572868
  95.3 36.2 %copy-start = (f32[512,1024]{1,0:T(8,128)S(1)}, f32[512,1024]{1,0:T(8,128)}, u32[]{:S(2)}) copy-start(f32[512,1024]{1,0:T(8,128)} %weight_in.5) | copy-start | bytes 6291460
  95.4 36.2 %copy-start.3 = (s32[32,4]{0,1:T(4,128)S(1)}, s32[32,4]{0,1:T(4,128)}, u32[]{:S(2)}) copy-start(s32[32,4]{0,1:T(4,128)} %param.10) | copy-start | bytes 1540
  95.4 25.4 %all-to-all-start.4 = ((bf16[16,64,256]{2,1,0:T(8,128)(2,1)}), bf16[16,64,256]{2,1,0:T(8,128)(2,1)}, u32[]{:S(2)}, u32[]{:S(2)}) async-start(bf16[16,64,256]{2,1,0:T(8,128)(2,1)} %bitcast.9), calls=%async_computation.4 | async-start | bytes 1048576 | tf_op jit(solution)/shard_map/all_to_all | solution.py:269
  102.8 14.4 %collective-permute-start.5 = (bf16[800,256]{1,0:T(8,128)(2,1)}, bf16[800,256]{1,0:T(8,128)(2,1)S(1)}, u32[]{:S(2)}, u32[]{:S(2)}) collective-permute-start(bf16[800,256]{1,0:T(8,128)(2,1)} %get-tuple-element.29.own), channel_id=1, source_target_pairs={{0,576},{192,0},{384,192},{576,384},{1,577},{193,1},{385,193},{577... | collective-permute-start | bytes 1228808 | tf_op jit(solution)/shard_map/ppermute | solution.py:274
  105.9 28.2 %collective-permute-start.3 = (bf16[800,256]{1,0:T(8,128)(2,1)}, bf16[800,256]{1,0:T(8,128)(2,1)S(1)}, u32[]{:S(2)}, u32[]{:S(2)}) collective-permute-start(bf16[800,256]{1,0:T(8,128)(2,1)} %get-tuple-element.29.own), channel_id=1, source_target_pairs={{0,192},{192,384},{384,576},{576,0},{1,193},{193,385},{385,577},{5... | collective-permute-start | bytes 1228808 | tf_op jit(solution)/shard_map/ppermute | solution.py:274
  110.3 23.9 %collective-permute-start.4 = (bf16[400,256]{1,0:T(8,128)(2,1)}, bf16[400,256]{1,0:T(8,128)(2,1)}, u32[]{:S(2)}, u32[]{:S(2)}) collective-permute-start(bf16[400,256]{1,0:T(8,128)(2,1)} %slice.6), channel_id=1, source_target_pairs={{0,384},{192,576},{384,0},{576,192},{1,385},{193,577},{385,1},{577... | collective-permute-start | bytes 614408 | tf_op jit(solution)/shard_map/ppermute | solution.py:274
  117.8 16.3 %collective-permute-start.6 = (bf16[400,256]{1,0:T(8,128)(2,1)}, bf16[400,256]{1,0:T(8,128)(2,1)}, u32[]{:S(2)}, u32[]{:S(2)}) collective-permute-start(bf16[400,256]{1,0:T(8,128)(2,1)} %slice.8), channel_id=1, source_target_pairs={{0,576},{192,0},{384,192},{576,384},{1,577},{193,1},{385,193},{577... | collective-permute-start | bytes 614408 | tf_op jit(solution)/shard_map/ppermute | solution.py:274
  121.9 14.6 %collective-permute-start.7 = (bf16[64,256]{1,0:T(8,128)(2,1)S(1)}, bf16[64,256]{1,0:T(8,128)(2,1)S(1)}, u32[]{:S(2)}, u32[]{:S(2)}) collective-permute-start(bf16[64,256]{1,0:T(8,128)(2,1)S(1)} %reduce_sum.12), channel_id=1, source_target_pairs={{0,0},{1,1},{2,2},{3,3},{4,192},{5,193},{6,194},{7,195},{8,384},{9... | collective-permute-start | bytes 98312 | tf_op jit(solution)/shard_map/ppermute | solution.py:384
  131.6 1.0 copy-start.2

commit v7 on v6

--- a/solution.py
+++ b/solution.py
@@ -314,6 +314,7 @@
     mine, acts = lax.optimization_barrier((call(sum_kernel, shape((n_zl, share, W), BF), tiles), acts))
     acts_1 = turn(acts, "x", 1)
     full = swap(mine, "zl").reshape(SENT, W)
+    acts_1, acts_2, acts_3 = (pltpu.with_memory_space_constraint(a, pltpu.HBM) for a in (acts_1, acts_2, acts_3))
     moved, partial_next = call(
         root_kernel,
         [shape((SENT, W), BF), shape((n_x, W, tokens), BF)],
@@ -325,7 +326,6 @@
         acts_3,
         specs=[IN_VMEM] + [IN_HBM] * 5,
         scratch=[pltpu.VMEM((rows_dev, W), F32), pltpu.VMEM((n_x, tokens, rows_dev), BF), dma((5,))],
-        mib=60,
     )
     tiles = swap(partial_next.reshape(n_feat, columns // n_feat, tokens), "feat")
     moved_3, moved_2, moved_1 = turn(moved, "x", 3), turn(moved[:EACH], "x", 2), turn(moved, "x", 1)

time: 138 us -> 136 us (0.986)
  the two profiles are of different devices: /device:TPU:4 before, /device:TPU:32 now
where the time goes in v7:
time: 136 us; the launch traced here: 135 us
  starting transfers between devices  53.3 us (39%)
  waiting for transfers between devices  35.9 us (26%)
  blocking collectives  25.7 us (19%)
  Pallas kernels  16 us (12%)
  local copies, waits for them, and re-layouts  2.02 us (1%)
    all_to_all x4, starting transfers between devices, swap(): return lax.all_to_all(x, axis, 0, 0, tiled=True)  29.9 us
    all_to_all x1, blocking collectives, swap(): return lax.all_to_all(x, axis, 0, 0, tiled=True)  25.7 us
    ppermute x7, waiting for transfers between devices, turn(): return lax.ppermute(x, axis, [(i, (i + by) % n) for i in range(n)])  24.4 us
    ppermute x7, starting transfers between devices, turn(): return lax.ppermute(x, axis, [(i, (i + by) % n) for i in range(n)])  21.1 us
    pallas_call x7, Pallas kernels, call(): pl.pallas_call(kernel, out_shape=out, in_specs=specs or [IN_VMEM] * len(a...  16 us
    all_to_all x4, waiting for transfers between devices, swap(): return lax.all_to_all(x, axis, 0, 0, tiled=True)  5.75 us
    ppermute x1, waiting for transfers between devices, body(): next_out = lax.ppermute(summed, ('x', 'feat'), pairs).T  5.74 us
  transfers between devices with their start and end apart: 12, of which 8 were waited for; matrix products, arithmetic and copies ran while one was open for 2% of the time, Pallas kernels for 3%

profile of v7, /device:TPU:32, one launch (start us, length us, event | category | flops | bytes accessed | tf_op | source)
XLA Modules:
  0.0 134.9 jit_solution(15427365569441374682)
XLA Ops:
  0.6 3.5 %shard_map.85 = bf16[4,800,256]{2,1,0:T(8,128)(2,1)} custom-call(s32[4,32]{1,0:T(4,128)} %bitcast.6, bf16[256,512]{1,0:T(8,128)(2,1)} %acts_in.1, bf16[256,1024]{1,0:T(8,128)(2,1)} %cot_in.1, f32[1,1,2,256,256]{4,3,2,1,0:T(8,128)} %stats_in.5), custom_call_target="tpu_custom_call" | custom-call | tf_op jit(solution)/shard_map/pallas_call | solution.py:257
  4.1 25.7 %all_to_all.25.tiles = bf16[4,800,256]{2,1,0:T(8,128)(2,1)S(1)} all-to-all(bf16[4,800,256]{2,1,0:T(8,128)(2,1)} %shard_map.85), channel_id=1, replica_groups=mesh['x'=4,'zh'=3,'zl'=4,'feat'=16] {'x'}, dimensions={0} | all-to-all | bytes 3276800 | tf_op jit(solution)/shard_map/all_to_all | solution.py:269
  29.9 0.0 copy-start.2
  29.9 1.0 shard_map.86
  30.8 0.0 copy-start
  30.8 7.4 %all-to-all-start.1 = ((bf16[4,200,256]{2,1,0:T(8,128)(2,1)}), bf16[4,200,256]{2,1,0:T(8,128)(2,1)S(1)}, u32[]{:S(2)}, u32[]{:S(2)}) async-start(bf16[4,200,256]{2,1,0:T(8,128)(2,1)} %bitcast.1), calls=%async_computation.1 | async-start | bytes 819200 | tf_op jit(solution)/shard_map/all_to_all | solution.py:269
  38.2 0.0 copy-done.2
  38.2 3.1 %collective-permute-start = (bf16[256,512]{1,0:T(8,128)(2,1)S(1)}, bf16[256,512]{1,0:T(8,128)(2,1)}, u32[]{:S(2)}, u32[]{:S(2)}) collective-permute-start(bf16[256,512]{1,0:T(8,128)(2,1)S(1)} %copy-done.2), channel_id=1, source_target_pairs={{0,576},{192,0},{384,192},{576,384},{1,577},{193,1},{385,193},{577... | collective-permute-start | bytes 786440 | tf_op jit(solution)/shard_map/ppermute | solution.py:274
  41.3 5.3 %collective-permute-done.third = bf16[256,512]{1,0:T(8,128)(2,1)} collective-permute-done((bf16[256,512]{1,0:T(8,128)(2,1)S(1)}, bf16[256,512]{1,0:T(8,128)(2,1)}, u32[]{:S(2)}, u32[]{:S(2)}) %collective-permute-start) | collective-permute-done | bytes 262176 | tf_op jit(solution)/shard_map/ppermute | solution.py:274
  46.6 2.2 %all-to-all-done.1.tiles = bf16[4,200,256]{2,1,0:T(8,128)(2,1)S(1)} async-done(((bf16[4,200,256]{2,1,0:T(8,128)(2,1)}), bf16[4,200,256]{2,1,0:T(8,128)(2,1)S(1)}, u32[]{:S(2)}, u32[]{:S(2)}) %all-to-all-start.1) | async-done | bytes 409632 | tf_op jit(solution)/shard_map/all_to_all | solution.py:269
  48.8 0.8 shard_map.87
  49.6 11.2 %all-to-all-start.2 = ((bf16[3,200,256]{2,1,0:T(8,128)(2,1)}), bf16[3,200,256]{2,1,0:T(8,128)(2,1)S(1)}, u32[]{:S(2)}, u32[]{:S(2)}) async-start(bf16[3,200,256]{2,1,0:T(8,128)(2,1)} %shard_map.87), calls=%async_computation.2 | async-start | bytes 614400 | tf_op jit(solution)/shard_map/all_to_all | solution.py:269
  60.7 3.0 %collective-permute-start.1 = (bf16[256,512]{1,0:T(8,128)(2,1)S(1)}, bf16[256,512]{1,0:T(8,128)(2,1)}, u32[]{:S(2)}, u32[]{:S(2)}) collective-permute-start(bf16[256,512]{1,0:T(8,128)(2,1)S(1)} %copy-done.2), channel_id=1, source_target_pairs={{0,384},{192,576},{384,0},{576,192},{1,385},{193,577},{385,1},{577... | collective-permute-start | bytes 786440 | tf_op jit(solution)/shard_map/ppermute | solution.py:274
  63.8 6.8 %collective-permute-done.1.second = bf16[256,512]{1,0:T(8,128)(2,1)} collective-permute-done((bf16[256,512]{1,0:T(8,128)(2,1)S(1)}, bf16[256,512]{1,0:T(8,128)(2,1)}, u32[]{:S(2)}, u32[]{:S(2)}) %collective-permute-start.1) | collective-permute-done | bytes 262176 | tf_op jit(solution)/shard_map/ppermute | solution.py:274
  70.6 2.4 %all-to-all-done.2.tiles = bf16[3,200,256]{2,1,0:T(8,128)(2,1)S(1)} async-done(((bf16[3,200,256]{2,1,0:T(8,128)(2,1)}), bf16[3,200,256]{2,1,0:T(8,128)(2,1)S(1)}, u32[]{:S(2)}, u32[]{:S(2)}) %all-to-all-start.2) | async-done | bytes 307232 | tf_op jit(solution)/shard_map/all_to_all | solution.py:269
  73.0 0.8 shard_map.88
  73.8 4.0 %all-to-all-start.3 = ((bf16[4,200,256]{2,1,0:T(8,128)(2,1)}), bf16[4,200,256]{2,1,0:T(8,128)(2,1)S(1)}, u32[]{:S(2)}, u32[]{:S(2)}) async-start(bf16[4,200,256]{2,1,0:T(8,128)(2,1)} %shard_map.88), calls=%async_computation.3 | async-start | bytes 819200 | tf_op jit(solution)/shard_map/all_to_all | solution.py:269
  77.7 2.5 %collective-permute-start.2 = (bf16[256,512]{1,0:T(8,128)(2,1)S(1)}, bf16[256,512]{1,0:T(8,128)(2,1)S(1)}, u32[]{:S(2)}, u32[]{:S(2)}) collective-permute-start(bf16[256,512]{1,0:T(8,128)(2,1)S(1)} %copy-done.2), channel_id=1, source_target_pairs={{0,192},{192,384},{384,576},{576,0},{1,193},{193,385},{385,577},{5... | collective-permute-start | bytes 786440 | tf_op jit(solution)/shard_map/ppermute | solution.py:274
  80.2 7.9 %collective-permute-done.2.first = bf16[256,512]{1,0:T(8,128)(2,1)S(1)} collective-permute-done((bf16[256,512]{1,0:T(8,128)(2,1)S(1)}, bf16[256,512]{1,0:T(8,128)(2,1)S(1)}, u32[]{:S(2)}, u32[]{:S(2)}) %collective-permute-start.2) | collective-permute-done | bytes 262176 | tf_op jit(solution)/shard_map/ppermute | solution.py:274
  88.1 0.0 copy-start.4
  88.1 1.2 all-to-all-done.3
  89.3 0.0 copy-done.4
  89.3 0.0 copy-done
  89.3 6.0 %shard_map.89 = (bf16[800,256]{1,0:T(8,128)(2,1)S(1)}, bf16[4,256,256]{2,1,0:T(8,128)(2,1)}) custom-call(bf16[800,256]{1,0:T(8,128)(2,1)S(1)} %bitcast.5, f32[512,1024]{1,0:T(8,128)S(1)} %copy-done, bf16[256,512]{1,0:T(8,128)(2,1)S(1)} %copy-done.2, bf16[256,512]{1,0:T(8,128)(2,1)} %copy-done.4, bf16[256,512]{1,0:T(8,128)(2,1)} %collective-permute-done.1.second, ...), custom_call_target="tpu_custom_call" | custom-call | tf_op jit(solution)/shard_map/pallas_call | solution.py:257
  95.3 0.0 copy-start.1
  95.3 0.0 copy-start.3
  95.3 7.4 %all-to-all-start.4 = ((bf16[16,64,256]{2,1,0:T(8,128)(2,1)}), bf16[16,64,256]{2,1,0:T(8,128)(2,1)}, u32[]{:S(2)}, u32[]{:S(2)}) async-start(bf16[16,64,256]{2,1,0:T(8,128)(2,1)} %bitcast.3), calls=%async_computation.4 | async-start | bytes 1048576 | tf_op jit(solution)/shard_map/all_to_all | solution.py:269
  102.7 2.8 %collective-permute-start.5 = (bf16[800,256]{1,0:T(8,128)(2,1)S(1)}, bf16[800,256]{1,0:T(8,128)(2,1)S(1)}, u32[]{:S(2)}, u32[]{:S(2)}) collective-permute-start(bf16[800,256]{1,0:T(8,128)(2,1)S(1)} %get-tuple-element.29.own), channel_id=1, source_target_pairs={{0,576},{192,0},{384,192},{576,384},{1,577},{193,1},{385,193},{577... | collective-permute-start | bytes 1228808 | tf_op jit(solution)/shard_map/ppermute | solution.py:274
  105.5 3.0 %collective-permute-start.3 = (bf16[800,256]{1,0:T(8,128)(2,1)S(1)}, bf16[800,256]{1,0:T(8,128)(2,1)}, u32[]{:S(2)}, u32[]{:S(2)}) collective-permute-start(bf16[800,256]{1,0:T(8,128)(2,1)S(1)} %get-tuple-element.29.own), channel_id=1, source_target_pairs={{0,192},{192,384},{384,576},{576,0},{1,193},{193,385},{385,577},{5... | collective-permute-start | bytes 1228808 | tf_op jit(solution)/shard_map/ppermute | solution.py:274
  108.5 0.7 slice.6
  109.2 3.3 %collective-permute-start.4 = (bf16[400,256]{1,0:T(8,128)(2,1)}, bf16[400,256]{1,0:T(8,128)(2,1)}, u32[]{:S(2)}, u32[]{:S(2)}) collective-permute-start(bf16[400,256]{1,0:T(8,128)(2,1)} %slice.6), channel_id=1, source_target_pairs={{0,384},{192,576},{384,0},{576,192},{1,385},{193,577},{385,1},{577... | collective-permute-start | bytes 614408 | tf_op jit(solution)/shard_map/ppermute | solution.py:274
  112.5 4.4 %collective-permute-done.5.third = bf16[800,256]{1,0:T(8,128)(2,1)S(1)} collective-permute-done((bf16[800,256]{1,0:T(8,128)(2,1)S(1)}, bf16[800,256]{1,0:T(8,128)(2,1)S(1)}, u32[]{:S(2)}, u32[]{:S(2)}) %collective-permute-start.5) | collective-permute-done | bytes 409632 | tf_op jit(solution)/shard_map/ppermute | solution.py:274
  116.9 0.7 slice.8
  117.6 3.5 %collective-permute-start.6 = (bf16[400,256]{1,0:T(8,128)(2,1)}, bf16[400,256]{1,0:T(8,128)(2,1)}, u32[]{:S(2)}, u32[]{:S(2)}) collective-permute-start(bf16[400,256]{1,0:T(8,128)(2,1)} %slice.8), channel_id=1, source_target_pairs={{0,576},{192,0},{384,192},{576,384},{1,577},{193,1},{385,193},{577... | collective-permute-start | bytes 614408 | tf_op jit(solution)/shard_map/ppermute | solution.py:274
  121.0 0.0 all-to-all-done.4
  121.0 1.1 reduce_sum.12
  122.2 2.3 %collective-permute-start.7 = (bf16[64,256]{1,0:T(8,128)(2,1)S(1)}, bf16[64,256]{1,0:T(8,128)(2,1)S(1)}, u32[]{:S(2)}, u32[]{:S(2)}) collective-permute-start(bf16[64,256]{1,0:T(8,128)(2,1)S(1)} %reduce_sum.12), channel_id=1, source_target_pairs={{0,0},{1,1},{2,2},{3,3},{4,192},{5,193},{6,194},{7,195},{8,384},{9... | collective-permute-start | bytes 98312 | tf_op jit(solution)/shard_map/ppermute | solution.py:384
  124.5 0.0 copy-done.1
  124.5 0.0 copy-done.3
  124.5 1.6 %shard_map.90 = (f32[512,1024]{1,0:T(8,128)}, f32[1,1,2,256,256]{4,3,2,1,0:T(8,128)}) custom-call(s32[4,32]{1,0:T(4,128)S(1)} %bitcast.7, bf16[800,256]{1,0:T(8,128)(2,1)S(1)} %get-tuple-element.29.own, bf16[800,256]{1,0:T(8,128)(2,1)S(1)} %collective-permute-done.5.third, f32[512,1024]{1,0:T(8,128)S(1)} %copy-done, f32[1,1,2,256,256]{4,3,2,1,0:T(8,128)S(1)} %copy-done.1), custom_call_target="tpu_custom_call" | custom-call | tf_op jit(solution)/shard_map/pallas_call | solution.py:257
  126.0 0.0 collective-permute-done.4.top
  126.1 0.0 collective-permute-done.3.first
  126.1 0.0 collective-permute-done.6.low
  126.1 2.5 %shard_map.91 = (f32[512,1024]{1,0:T(8,128)}, f32[1,1,2,256,256]{4,3,2,1,0:T(8,128)}) custom-call(s32[4,32]{1,0:T(4,128)S(1)} %bitcast.8, bf16[800,256]{1,0:T(8,128)(2,1)} %collective-permute-done.3.first, bf16[400,256]{1,0:T(8,128)(2,1)} %collective-permute-done.4.top, ...), custom_call_target="tpu_custom_call", output_to_operand_aliasing={{0}: (6, {}), {1}: (7, {})} | custom-call | tf_op jit(solution)/shard_map/pallas_call | solution.py:257
  128.5 5.7 %collective-permute-done.7 = bf16[64,256]{1,0:T(8,128)(2,1)S(1)} collective-permute-done((bf16[64,256]{1,0:T(8,128)(2,1)S(1)}, bf16[64,256]{1,0:T(8,128)(2,1)S(1)}, u32[]{:S(2)}, u32[]{:S(2)}) %collective-permute-start.7) | collective-permute-done | bytes 32800 | tf_op jit(solution)/shard_map/ppermute | solution.py:384
  134.3 0.6 copy.14
Async XLA Ops:
  29.9 8.4 %copy-start.2 = (bf16[256,512]{1,0:T(8,128)(2,1)S(1)}, bf16[256,512]{1,0:T(8,128)(2,1)}, u32[]{:S(2)}) copy-start(bf16[256,512]{1,0:T(8,128)(2,1)} %own.1) | copy-start | bytes 786436
  30.8 58.5 %copy-start = (f32[512,1024]{1,0:T(8,128)S(1)}, f32[512,1024]{1,0:T(8,128)}, u32[]{:S(2)}) copy-start(f32[512,1024]{1,0:T(8,128)} %weight_in.5) | copy-start | bytes 6291460
  30.8 18.0 %all-to-all-start.1 = ((bf16[4,200,256]{2,1,0:T(8,128)(2,1)}), bf16[4,200,256]{2,1,0:T(8,128)(2,1)S(1)}, u32[]{:S(2)}, u32[]{:S(2)}) async-start(bf16[4,200,256]{2,1,0:T(8,128)(2,1)} %bitcast.1), calls=%async_computation.1 | async-start | bytes 819200 | tf_op jit(solution)/shard_map/all_to_all | solution.py:269
  38.2 8.4 %collective-permute-start = (bf16[256,512]{1,0:T(8,128)(2,1)S(1)}, bf16[256,512]{1,0:T(8,128)(2,1)}, u32[]{:S(2)}, u32[]{:S(2)}) collective-permute-start(bf16[256,512]{1,0:T(8,128)(2,1)S(1)} %copy-done.2), channel_id=1, source_target_pairs={{0,576},{192,0},{384,192},{576,384},{1,577},{193,1},{385,193},{577... | collective-permute-start | bytes 786440 | tf_op jit(solution)/shard_map/ppermute | solution.py:274
  49.6 23.4 %all-to-all-start.2 = ((bf16[3,200,256]{2,1,0:T(8,128)(2,1)}), bf16[3,200,256]{2,1,0:T(8,128)(2,1)S(1)}, u32[]{:S(2)}, u32[]{:S(2)}) async-start(bf16[3,200,256]{2,1,0:T(8,128)(2,1)} %shard_map.87), calls=%async_computation.2 | async-start | bytes 614400 | tf_op jit(solution)/shard_map/all_to_all | solution.py:269
  60.7 9.9 %collective-permute-start.1 = (bf16[256,512]{1,0:T(8,128)(2,1)S(1)}, bf16[256,512]{1,0:T(8,128)(2,1)}, u32[]{:S(2)}, u32[]{:S(2)}) collective-permute-start(bf16[256,512]{1,0:T(8,128)(2,1)S(1)} %copy-done.2), channel_id=1, source_target_pairs={{0,384},{192,576},{384,0},{576,192},{1,385},{193,577},{385,1},{577... | collective-permute-start | bytes 786440 | tf_op jit(solution)/shard_map/ppermute | solution.py:274
  73.8 15.5 %all-to-all-start.3 = ((bf16[4,200,256]{2,1,0:T(8,128)(2,1)}), bf16[4,200,256]{2,1,0:T(8,128)(2,1)S(1)}, u32[]{:S(2)}, u32[]{:S(2)}) async-start(bf16[4,200,256]{2,1,0:T(8,128)(2,1)} %shard_map.88), calls=%async_computation.3 | async-start | bytes 819200 | tf_op jit(solution)/shard_map/all_to_all | solution.py:269
  77.7 10.4 %collective-permute-start.2 = (bf16[256,512]{1,0:T(8,128)(2,1)S(1)}, bf16[256,512]{1,0:T(8,128)(2,1)S(1)}, u32[]{:S(2)}, u32[]{:S(2)}) collective-permute-start(bf16[256,512]{1,0:T(8,128)(2,1)S(1)} %copy-done.2), channel_id=1, source_target_pairs={{0,192},{192,384},{384,576},{576,0},{1,193},{193,385},{385,577},{5... | collective-permute-start | bytes 786440 | tf_op jit(solution)/shard_map/ppermute | solution.py:274
  88.1 1.2 copy-start.4
  95.3 29.2 %copy-start.1 = (f32[1,1,2,256,256]{4,3,2,1,0:T(8,128)S(1)}, f32[1,1,2,256,256]{4,3,2,1,0:T(8,128)}, u32[]{:S(2)}) copy-start(f32[1,1,2,256,256]{4,3,2,1,0:T(8,128)} %stats_in.5) | copy-start | bytes 1572868
  95.3 29.2 %copy-start.3 = (s32[32,4]{0,1:T(4,128)S(1)}, s32[32,4]{0,1:T(4,128)}, u32[]{:S(2)}) copy-start(s32[32,4]{0,1:T(4,128)} %param.10) | copy-start | bytes 1540
  95.3 25.7 %all-to-all-start.4 = ((bf16[16,64,256]{2,1,0:T(8,128)(2,1)}), bf16[16,64,256]{2,1,0:T(8,128)(2,1)}, u32[]{:S(2)}, u32[]{:S(2)}) async-start(bf16[16,64,256]{2,1,0:T(8,128)(2,1)} %bitcast.3), calls=%async_computation.4 | async-start | bytes 1048576 | tf_op jit(solution)/shard_map/all_to_all | solution.py:269
  102.7 14.2 %collective-permute-start.5 = (bf16[800,256]{1,0:T(8,128)(2,1)S(1)}, bf16[800,256]{1,0:T(8,128)(2,1)S(1)}, u32[]{:S(2)}, u32[]{:S(2)}) collective-permute-start(bf16[800,256]{1,0:T(8,128)(2,1)S(1)} %get-tuple-element.29.own), channel_id=1, source_target_pairs={{0,576},{192,0},{384,192},{576,384},{1,577},{193,1},{385,193},{577... | collective-permute-start | bytes 1228808 | tf_op jit(solution)/shard_map/ppermute | solution.py:274
  105.5 20.6 %collective-permute-start.3 = (bf16[800,256]{1,0:T(8,128)(2,1)S(1)}, bf16[800,256]{1,0:T(8,128)(2,1)}, u32[]{:S(2)}, u32[]{:S(2)}) collective-permute-start(bf16[800,256]{1,0:T(8,128)(2,1)S(1)} %get-tuple-element.29.own), channel_id=1, source_target_pairs={{0,192},{192,384},{384,576},{576,0},{1,193},{193,385},{385,577},{5... | collective-permute-start | bytes 1228808 | tf_op jit(solution)/shard_map/ppermute | solution.py:274
  109.2 16.8 %collective-permute-start.4 = (bf16[400,256]{1,0:T(8,128)(2,1)}, bf16[400,256]{1,0:T(8,128)(2,1)}, u32[]{:S(2)}, u32[]{:S(2)}) collective-permute-start(bf16[400,256]{1,0:T(8,128)(2,1)} %slice.6), channel_id=1, source_target_pairs={{0,384},{192,576},{384,0},{576,192},{1,385},{193,577},{385,1},{577... | collective-permute-start | bytes 614408 | tf_op jit(solution)/shard_map/ppermute | solution.py:274
  117.6 8.5 %collective-permute-start.6 = (bf16[400,256]{1,0:T(8,128)(2,1)}, bf16[400,256]{1,0:T(8,128)(2,1)}, u32[]{:S(2)}, u32[]{:S(2)}) collective-permute-start(bf16[400,256]{1,0:T(8,128)(2,1)} %slice.8), channel_id=1, source_target_pairs={{0,576},{192,0},{384,192},{576,384},{1,577},{193,1},{385,193},{577... | collective-permute-start | bytes 614408 | tf_op jit(solution)/shard_map/ppermute | solution.py:274
  122.2 12.1 %collective-permute-start.7 = (bf16[64,256]{1,0:T(8,128)(2,1)S(1)}, bf16[64,256]{1,0:T(8,128)(2,1)S(1)}, u32[]{:S(2)}, u32[]{:S(2)}) collective-permute-start(bf16[64,256]{1,0:T(8,128)(2,1)S(1)} %reduce_sum.12), channel_id=1, source_target_pairs={{0,0},{1,1},{2,2},{3,3},{4,192},{5,193},{6,194},{7,195},{8,384},{9... | collective-permute-start | bytes 98312 | tf_op jit(solution)/shard_map/ppermute | solution.py:384

commit v8 on v7

--- a/solution.py
+++ b/solution.py
@@ -85,7 +85,7 @@
     )
 
 
-def grad_kernel(owners_in, acts_in, cot_in, stats_in, sent, owners, acts, cot, stats, turned, out, sems, out_sems):
+def grad_kernel(owners_in, acts_in, cot_in, stats_in, out, owners, acts, cot, stats, turned, sems):
     copies = start_copies(
         [(acts_in.at[:, i * H : (i + 1) * H], acts.at[:, i * H : (i + 1) * H]) for i in range(4)]
         + [(cot_in.at[:, i * W : (i + 1) * W], cot.at[:, i * W : (i + 1) * W]) for i in range(4)]
@@ -101,7 +101,6 @@
         turned[i * H : (i + 1) * H, :] = acts[:, i * H : (i + 1) * H].T
     for at in (8, 9, 10):
         copies[at].wait()
-    sends = []
     for i in range(4):
         copies[4 + i].wait()
         part = jnp.dot(turned[...], cot[:, i * W : (i + 1) * W], preferred_element_type=F32).astype(BF)
@@ -112,13 +111,6 @@
             @pl.when(mine)
             def _(i=i, r=r, slot=slot):
                 pack(stats[jnp.minimum(slot, 1)], out.at[i], r * EACH + W)
-
-        for r in range(2):
-            rows = pl.ds(r * EACH, EACH)
-            sends.append(pltpu.make_async_copy(out.at[i, rows], sent.at[i, rows], out_sems.at[2 * i + r]))
-            sends[-1].start()
-    for send in sends:
-        send.wait()
 
 
 def sum_kernel(tiles, out):
@@ -189,48 +181,43 @@
     return send
 
 
-def finish_kernel(owners_in, own, third, weight_in, stats_in, weight_out, stats_out, owners, weight, stats, new, stats_new, sems, out_sems):
+def finish_kernel(owners_in, own, weight_in, stats_in, weight_out, stats_out, owners, weight, stats, new, stats_new, sems, out_sems):
     x = lax.axis_index("x")
-    columns = [x, (x + 1) % 4]
+    copies = start_copies(
+        [(owners_in, owners)]
+        + [(stats_in.at[0, 0, k], stats.at[k]) for k in range(2)]
+        + [(weight_in.at[:, wide(x)], weight)],
+        sems,
+    )
+    copies[3].wait()
+    sends = [renewed_weight([(own, 0), (own, EACH)], weight, new, weight_out.at[:, wide(x)], out_sems.at[0])]
+    for at in range(3):
+        copies[at].wait()
+    stats_new[...] = jnp.zeros(stats_new.shape, F32)
+    for r in range(2):
+        mine, slot = mine_and_slot(owners, r * 4 + x)
+
+        @pl.when(mine)
+        def _(r=r, slot=slot):
+            at = jnp.minimum(slot, 1)
+            stats_new[at] = decay_rate * stats[at] + (1.0 - decay_rate) * unpack(own, r * EACH + W)
+
+    sends.append(pltpu.make_async_copy(stats_new, stats_out.at[0, 0], out_sems.at[1]))
+    sends[-1].start()
+    for send in sends:
+        send.wait()
+
+
+def last_kernel(owners_in, third, first, top, low, weight_in, stats_in, weight_part, stats_part, weight_out, stats_out, owners, weight, stats, new, stats_new, sems, out_sems):
+    x = lax.axis_index("x")
+    columns = [(x + 1) % 4, (x + 3) % 4, (x + 2) % 4]
     copies = start_copies(
         [(owners_in, owners)]
         + [(stats_in.at[0, 0, k], stats.at[k]) for k in range(2)]
         + [(weight_in.at[:, wide(c)], weight.at[k]) for k, c in enumerate(columns)],
         sems,
     )
-    sends = []
-    for k, part in enumerate((own, third)):
-        copies[3 + k].wait()
-        halves = (part, 0), (part, EACH)
-        sends.append(renewed_weight(halves, weight.at[k], new.at[k], weight_out.at[:, wide(columns[k])], out_sems.at[k]))
-    for at in range(3):
-        copies[at].wait()
-    stats_new[...] = jnp.zeros(stats_new.shape, F32)
-    for k, part in enumerate((own, third)):
-        for r in range(2):
-            mine, slot = mine_and_slot(owners, r * 4 + columns[k])
-
-            @pl.when(mine)
-            def _(r=r, part=part, slot=slot):
-                at = jnp.minimum(slot, 1)
-                stats_new[at] = decay_rate * stats[at] + (1.0 - decay_rate) * unpack(part, r * EACH + W)
-
-    sends.append(pltpu.make_async_copy(stats_new, stats_out.at[0, 0], out_sems.at[2]))
-    sends[-1].start()
-    for send in sends:
-        send.wait()
-
-
-def last_kernel(owners_in, first, top, low, weight_in, stats_in, weight_part, stats_part, weight_out, stats_out, owners, weight, stats, new, stats_new, sems, out_sems):
-    x = lax.axis_index("x")
-    columns = [(x + 3) % 4, (x + 2) % 4]
-    copies = start_copies(
-        [(owners_in, owners)]
-        + [(stats_in.at[0, 0, k], stats.at[k]) for k in range(2)]
-        + [(weight_in.at[:, wide(c)], weight.at[k]) for k, c in enumerate(columns)],
-        sems,
-    )
-    blocks = [[(first, 0), (first, EACH)], [(top, 0), (low, 0)]]
+    blocks = [[(third, 0), (third, EACH)], [(first, 0), (first, EACH)], [(top, 0), (low, 0)]]
     sends = []
     for k, halves in enumerate(blocks):
         copies[3 + k].wait()
@@ -245,7 +232,7 @@
             def _(part=part, start=start, slot=slot):
                 at = jnp.minimum(slot, 1)
                 stats_new[...] = decay_rate * stats[at] + (1.0 - decay_rate) * unpack(part, start + W)
-                keep = pltpu.make_async_copy(stats_new, stats_out.at[0, 0, at], out_sems.at[2])
+                keep = pltpu.make_async_copy(stats_new, stats_out.at[0, 0, at], out_sems.at[3])
                 keep.start()
                 keep.wait()
 
@@ -284,10 +271,7 @@
     sent = call(
         grad_kernel,
         shape((n_x, SENT, W), BF),
-        owners,
-        activations,
-        cotangent,
-        stats_old,
+        *[pltpu.with_memory_space_constraint(a, pltpu.HBM) for a in (owners, activations, cotangent, stats_old)],
         specs=[IN_HBM] * 4,
         scratch=[
             pltpu.SMEM(owners.shape, jnp.int32),
@@ -295,12 +279,8 @@
             pltpu.VMEM((tokens, columns), BF),
             pltpu.VMEM((2, W, W), F32),
             pltpu.VMEM((rows_dev, tokens), BF),
-            pltpu.VMEM((n_x, SENT, W), BF),
             dma((11,)),
-            dma((2 * n_x,)),
         ],
-        out_specs=IN_HBM,
-        mib=60,
     )
     share = SENT // n_zl
     column = call(sum_kernel, shape((1, SENT, W), BF), swap(sent, "x"))
@@ -320,58 +300,60 @@
         [shape((SENT, W), BF), shape((n_x, W, tokens), BF)],
         full,
         weight,
-        next_acts,
+        pltpu.with_memory_space_constraint(next_acts, pltpu.HBM),
         acts_1,
         acts_2,
         acts_3,
         specs=[IN_VMEM] + [IN_HBM] * 5,
         scratch=[pltpu.VMEM((rows_dev, W), F32), pltpu.VMEM((n_x, tokens, rows_dev), BF), dma((5,))],
+        mib=32,
     )
     tiles = swap(partial_next.reshape(n_feat, columns // n_feat, tokens), "feat")
     moved_3, moved_2, moved_1 = turn(moved, "x", 3), turn(moved[:EACH], "x", 2), turn(moved, "x", 1)
-    moved_2 = moved_2, turn(moved_3[EACH:], "x", 3)
     outs = [shape(weight.shape, F32), shape(stats_old.shape, F32)]
-    begun = call(
+    begun = list(call(
         finish_kernel,
         outs,
         owners,
         moved,
-        moved_3,
         weight,
         stats_old,
-        specs=[IN_HBM] + [IN_VMEM] * 2 + [IN_HBM] * 2,
+        specs=[IN_HBM, IN_VMEM, IN_HBM, IN_HBM],
         out_specs=[IN_HBM, IN_HBM],
         scratch=[
             pltpu.SMEM(owners.shape, jnp.int32),
-            pltpu.VMEM((2, rows_dev, W), F32),
+            pltpu.VMEM((rows_dev, W), F32),
             pltpu.VMEM((2, W, W), F32),
-            pltpu.VMEM((2, rows_dev, W), F32),
+            pltpu.VMEM((rows_dev, W), F32),
             pltpu.VMEM((2, W, W), F32),
-            dma((5,)),
-            dma((3,)),
+            dma((4,)),
+            dma((2,)),
         ],
-    )
+    ))
+    begun[0], begun[1], handed = lax.optimization_barrier((*begun, moved_3))
+    moved_2 = moved_2, turn(handed[EACH:], "x", 3)
     weight_new, stats_new = call(
         last_kernel,
         outs,
         owners,
+        moved_3,
         moved_1,
         *moved_2,
         weight,
         stats_old,
         *begun,
-        specs=[IN_HBM] + [IN_VMEM] * 3 + [IN_HBM] * 4,
+        specs=[IN_HBM] + [IN_VMEM] * 4 + [IN_HBM] * 4,
         out_specs=[IN_HBM, IN_HBM],
         scratch=[
             pltpu.SMEM(owners.shape, jnp.int32),
-            pltpu.VMEM((2, rows_dev, W), F32),
+            pltpu.VMEM((3, rows_dev, W), F32),
             pltpu.VMEM((2, W, W), F32),
-            pltpu.VMEM((2, rows_dev, W), F32),
+            pltpu.VMEM((3, rows_dev, W), F32),
             pltpu.VMEM((W, W), F32),
-            dma((5,)),
-            dma((3,)),
+            dma((6,)),
+            dma((4,)),
         ],
-        aliases={6: 0, 7: 1},
+        aliases={7: 0, 8: 1},
     )
     summed = jnp.sum(tiles.astype(F32), axis=0).astype(BF)
     each = n_feat // n_x

time: 136 us -> 134 us (0.985)
  Pallas kernels: 16 us -> 14.6 us
    pallas_call x7, Pallas kernels: 16 us -> 14.6 us  [call(): pl.pallas_call(kernel, out_shape=out, in_specs=specs or [IN_VMEM] * len(a...]
  transfers between devices with their start and end apart: 12 -> 12, of which waited for: 8 -> 10; matrix products, arithmetic and copies ran while one was open for 2% -> 2% of each run, Pallas kernels for 3% -> 3%
where the time goes in v8:
time: 134 us
  starting transfers between devices  53.7 us (40%)
  waiting for transfers between devices  35.1 us (26%)
  blocking collectives  25.5 us (19%)
  Pallas kernels  14.6 us (11%)
  local copies, waits for them, and re-layouts  2.8 us (2%)
    all_to_all x4, starting transfers between devices, swap(): return lax.all_to_all(x, axis, 0, 0, tiled=True)  29.8 us
    all_to_all x1, blocking collectives, swap(): return lax.all_to_all(x, axis, 0, 0, tiled=True)  25.5 us
    ppermute x7, waiting for transfers between devices, turn(): return lax.ppermute(x, axis, [(i, (i + by) % n) for i in range(n)])  23.4 us
    ppermute x7, starting transfers between devices, turn(): return lax.ppermute(x, axis, [(i, (i + by) % n) for i in range(n)])  21.6 us
    pallas_call x7, Pallas kernels, call(): pl.pallas_call(kernel, out_shape=out, in_specs=specs or [IN_VMEM] * len(a...  14.6 us
    ppermute x1, waiting for transfers between devices, body(): next_out = lax.ppermute(summed, ('x', 'feat'), pairs).T  5.94 us
    all_to_all x4, waiting for transfers between devices, swap(): return lax.all_to_all(x, axis, 0, 0, tiled=True)  5.72 us
  transfers between devices with their start and end apart: 12, of which 10 were waited for; matrix products, arithmetic and copies ran while one was open for 2% of the time, Pallas kernels for 3%

profile of v8, /device:TPU:32, one launch (start us, length us, event | category | flops | bytes accessed | tf_op | source)
XLA Modules:
  0.0 133.5 jit_solution(6057777940192276332)
XLA Ops:
  0.6 2.7 %shard_map.85 = bf16[4,800,256]{2,1,0:T(8,128)(2,1)S(1)} custom-call(s32[4,32]{1,0:T(4,128)} %bitcast.7, bf16[256,512]{1,0:T(8,128)(2,1)} %acts_in.1, bf16[256,1024]{1,0:T(8,128)(2,1)} %cot_in.1, f32[1,1,2,256,256]{4,3,2,1,0:T(8,128)} %stats_in.5), custom_call_target="tpu_custom_call" | custom-call | tf_op jit(solution)/shard_map/pallas_call | solution.py:244
  3.3 25.5 %all_to_all.25.tiles = bf16[4,800,256]{2,1,0:T(8,128)(2,1)S(1)} all-to-all(bf16[4,800,256]{2,1,0:T(8,128)(2,1)S(1)} %shard_map.85), channel_id=1, replica_groups=mesh['x'=4,'zh'=3,'zl'=4,'feat'=16] {'x'}, dimensions={0} | all-to-all | bytes 3276800 | tf_op jit(solution)/shard_map/all_to_all | solution.py:256
  28.9 0.0 copy-start.4
  28.9 1.0 shard_map.86
  29.8 0.0 copy-start
  29.8 7.4 %all-to-all-start.1 = ((bf16[4,200,256]{2,1,0:T(8,128)(2,1)}), bf16[4,200,256]{2,1,0:T(8,128)(2,1)S(1)}, u32[]{:S(2)}, u32[]{:S(2)}) async-start(bf16[4,200,256]{2,1,0:T(8,128)(2,1)} %bitcast.1), calls=%async_computation.1 | async-start | bytes 819200 | tf_op jit(solution)/shard_map/all_to_all | solution.py:256
  37.2 0.0 copy-done.4
  37.2 3.1 %collective-permute-start = (bf16[256,512]{1,0:T(8,128)(2,1)S(1)}, bf16[256,512]{1,0:T(8,128)(2,1)}, u32[]{:S(2)}, u32[]{:S(2)}) collective-permute-start(bf16[256,512]{1,0:T(8,128)(2,1)S(1)} %copy-done.4), channel_id=1, source_target_pairs={{0,576},{192,0},{384,192},{576,384},{1,577},{193,1},{385,193},{577... | collective-permute-start | bytes 786440 | tf_op jit(solution)/shard_map/ppermute | solution.py:261
  40.3 5.3 %collective-permute-done.third = bf16[256,512]{1,0:T(8,128)(2,1)} collective-permute-done((bf16[256,512]{1,0:T(8,128)(2,1)S(1)}, bf16[256,512]{1,0:T(8,128)(2,1)}, u32[]{:S(2)}, u32[]{:S(2)}) %collective-permute-start) | collective-permute-done | bytes 262176 | tf_op jit(solution)/shard_map/ppermute | solution.py:261
  45.6 2.2 %all-to-all-done.1.tiles = bf16[4,200,256]{2,1,0:T(8,128)(2,1)S(1)} async-done(((bf16[4,200,256]{2,1,0:T(8,128)(2,1)}), bf16[4,200,256]{2,1,0:T(8,128)(2,1)S(1)}, u32[]{:S(2)}, u32[]{:S(2)}) %all-to-all-start.1) | async-done | bytes 409632 | tf_op jit(solution)/shard_map/all_to_all | solution.py:256
  47.8 0.8 shard_map.87
  48.5 11.2 %all-to-all-start.2 = ((bf16[3,200,256]{2,1,0:T(8,128)(2,1)}), bf16[3,200,256]{2,1,0:T(8,128)(2,1)S(1)}, u32[]{:S(2)}, u32[]{:S(2)}) async-start(bf16[3,200,256]{2,1,0:T(8,128)(2,1)} %shard_map.87), calls=%async_computation.2 | async-start | bytes 614400 | tf_op jit(solution)/shard_map/all_to_all | solution.py:256
  59.7 3.0 %collective-permute-start.1 = (bf16[256,512]{1,0:T(8,128)(2,1)S(1)}, bf16[256,512]{1,0:T(8,128)(2,1)}, u32[]{:S(2)}, u32[]{:S(2)}) collective-permute-start(bf16[256,512]{1,0:T(8,128)(2,1)S(1)} %copy-done.4), channel_id=1, source_target_pairs={{0,384},{192,576},{384,0},{576,192},{1,385},{193,577},{385,1},{577... | collective-permute-start | bytes 786440 | tf_op jit(solution)/shard_map/ppermute | solution.py:261
  62.8 6.8 %collective-permute-done.1.second = bf16[256,512]{1,0:T(8,128)(2,1)} collective-permute-done((bf16[256,512]{1,0:T(8,128)(2,1)S(1)}, bf16[256,512]{1,0:T(8,128)(2,1)}, u32[]{:S(2)}, u32[]{:S(2)}) %collective-permute-start.1) | collective-permute-done | bytes 262176 | tf_op jit(solution)/shard_map/ppermute | solution.py:261
  69.6 2.4 %all-to-all-done.2.tiles = bf16[3,200,256]{2,1,0:T(8,128)(2,1)S(1)} async-done(((bf16[3,200,256]{2,1,0:T(8,128)(2,1)}), bf16[3,200,256]{2,1,0:T(8,128)(2,1)S(1)}, u32[]{:S(2)}, u32[]{:S(2)}) %all-to-all-start.2) | async-done | bytes 307232 | tf_op jit(solution)/shard_map/all_to_all | solution.py:256
  72.0 0.8 shard_map.88
  72.8 4.0 %all-to-all-start.3 = ((bf16[4,200,256]{2,1,0:T(8,128)(2,1)}), bf16[4,200,256]{2,1,0:T(8,128)(2,1)S(1)}, u32[]{:S(2)}, u32[]{:S(2)}) async-start(bf16[4,200,256]{2,1,0:T(8,128)(2,1)} %shard_map.88), calls=%async_computation.3 | async-start | bytes 819200 | tf_op jit(solution)/shard_map/all_to_all | solution.py:256
  76.8 2.5 %collective-permute-start.2 = (bf16[256,512]{1,0:T(8,128)(2,1)S(1)}, bf16[256,512]{1,0:T(8,128)(2,1)S(1)}, u32[]{:S(2)}, u32[]{:S(2)}) collective-permute-start(bf16[256,512]{1,0:T(8,128)(2,1)S(1)} %copy-done.4), channel_id=1, source_target_pairs={{0,192},{192,384},{384,576},{576,0},{1,193},{193,385},{385,577},{5... | collective-permute-start | bytes 786440 | tf_op jit(solution)/shard_map/ppermute | solution.py:261
  79.2 7.9 %collective-permute-done.2.first = bf16[256,512]{1,0:T(8,128)(2,1)S(1)} collective-permute-done((bf16[256,512]{1,0:T(8,128)(2,1)S(1)}, bf16[256,512]{1,0:T(8,128)(2,1)S(1)}, u32[]{:S(2)}, u32[]{:S(2)}) %collective-permute-start.2) | collective-permute-done | bytes 262176 | tf_op jit(solution)/shard_map/ppermute | solution.py:261
  87.1 0.0 copy-start.5
  87.1 1.2 all-to-all-done.3
  88.3 0.0 copy-done.5
  88.3 0.0 copy-done
  88.3 0.0 copy-start.1
  88.3 0.0 copy-start.3
  88.3 5.2 %shard_map.89 = (bf16[800,256]{1,0:T(8,128)(2,1)S(1)}, bf16[4,256,256]{2,1,0:T(8,128)(2,1)S(1)}) custom-call(bf16[800,256]{1,0:T(8,128)(2,1)S(1)} %bitcast.5, f32[512,1024]{1,0:T(8,128)S(1)} %copy-done, bf16[256,512]{1,0:T(8,128)(2,1)} %own.1, bf16[256,512]{1,0:T(8,128)(2,1)} %copy-done.5, bf16[256,512]{1,0:T(8,128)(2,1)} %collective-permute-done.1.second, ...), custom_call_target="tpu_custom_call" | custom-call | tf_op jit(solution)/shard_map/pallas_call | solution.py:244
  93.5 0.0 copy-start.2
  93.5 0.8 copy-done.2
  94.3 7.2 %all-to-all-start.4 = ((bf16[16,64,256]{2,1,0:T(8,128)(2,1)}), bf16[16,64,256]{2,1,0:T(8,128)(2,1)}, u32[]{:S(2)}, u32[]{:S(2)}) async-start(bf16[16,64,256]{2,1,0:T(8,128)(2,1)} %bitcast.6), calls=%async_computation.4 | async-start | bytes 1048576 | tf_op jit(solution)/shard_map/all_to_all | solution.py:256
  101.5 2.8 %collective-permute-start.3 = (bf16[800,256]{1,0:T(8,128)(2,1)S(1)}, bf16[800,256]{1,0:T(8,128)(2,1)S(1)}, u32[]{:S(2)}, u32[]{:S(2)}) collective-permute-start(bf16[800,256]{1,0:T(8,128)(2,1)S(1)} %get-tuple-element.32.own), channel_id=1, source_target_pairs={{0,576},{192,0},{384,192},{576,384},{1,577},{193,1},{385,193},{577... | collective-permute-start | bytes 1228808 | tf_op jit(solution)/shard_map/ppermute | solution.py:261
  104.4 3.0 %collective-permute-start.4 = (bf16[800,256]{1,0:T(8,128)(2,1)S(1)}, bf16[800,256]{1,0:T(8,128)(2,1)}, u32[]{:S(2)}, u32[]{:S(2)}) collective-permute-start(bf16[800,256]{1,0:T(8,128)(2,1)S(1)} %get-tuple-element.32.own), channel_id=1, source_target_pairs={{0,192},{192,384},{384,576},{576,0},{1,193},{193,385},{385,577},{5... | collective-permute-start | bytes 1228808 | tf_op jit(solution)/shard_map/ppermute | solution.py:261
  107.4 0.7 slice.6
  108.1 0.0 copy-done.1
  108.1 0.0 copy-done.3
  108.1 1.5 %shard_map.90 = (f32[512,1024]{1,0:T(8,128)}, f32[1,1,2,256,256]{4,3,2,1,0:T(8,128)}) custom-call(s32[4,32]{1,0:T(4,128)S(1)} %bitcast.8, bf16[800,256]{1,0:T(8,128)(2,1)S(1)} %get-tuple-element.32.own, f32[512,1024]{1,0:T(8,128)S(1)} %copy-done, f32[1,1,2,256,256]{4,3,2,1,0:T(8,128)S(1)} %copy-done.1), custom_call_target="tpu_custom_call" | custom-call | tf_op jit(solution)/shard_map/pallas_call | solution.py:244
  109.6 3.3 %collective-permute-start.5 = (bf16[400,256]{1,0:T(8,128)(2,1)}, bf16[400,256]{1,0:T(8,128)(2,1)}, u32[]{:S(2)}, u32[]{:S(2)}) collective-permute-start(bf16[400,256]{1,0:T(8,128)(2,1)} %slice.6), channel_id=1, source_target_pairs={{0,384},{192,576},{384,0},{576,192},{1,385},{193,577},{385,1},{577... | collective-permute-start | bytes 614408 | tf_op jit(solution)/shard_map/ppermute | solution.py:261
  112.9 2.1 %collective-permute-done.3.third = bf16[800,256]{1,0:T(8,128)(2,1)S(1)} collective-permute-done((bf16[800,256]{1,0:T(8,128)(2,1)S(1)}, bf16[800,256]{1,0:T(8,128)(2,1)S(1)}, u32[]{:S(2)}, u32[]{:S(2)}) %collective-permute-start.3) | collective-permute-done | bytes 409632 | tf_op jit(solution)/shard_map/ppermute | solution.py:261
  115.0 0.7 slice.7
  115.7 3.9 %collective-permute-start.6 = (bf16[400,256]{1,0:T(8,128)(2,1)}, bf16[400,256]{1,0:T(8,128)(2,1)}, u32[]{:S(2)}, u32[]{:S(2)}) collective-permute-start(bf16[400,256]{1,0:T(8,128)(2,1)} %slice.7), channel_id=1, source_target_pairs={{0,576},{192,0},{384,192},{576,384},{1,577},{193,1},{385,193},{577... | collective-permute-start | bytes 614408 | tf_op jit(solution)/shard_map/ppermute | solution.py:261
  119.7 0.0 all-to-all-done.4
  119.7 1.1 reduce_sum.12
  120.8 2.2 %collective-permute-start.7 = (bf16[64,256]{1,0:T(8,128)(2,1)S(1)}, bf16[64,256]{1,0:T(8,128)(2,1)S(1)}, u32[]{:S(2)}, u32[]{:S(2)}) collective-permute-start(bf16[64,256]{1,0:T(8,128)(2,1)S(1)} %reduce_sum.12), channel_id=1, source_target_pairs={{0,0},{1,1},{2,2},{3,3},{4,192},{5,193},{6,194},{7,195},{8,384},{9... | collective-permute-start | bytes 98312 | tf_op jit(solution)/shard_map/ppermute | solution.py:366
  123.0 0.0 collective-permute-done.5.top
  123.0 0.2 collective-permute-done.4.first
  123.2 1.0 collective-permute-done.6.low
  124.2 2.7 %shard_map.91 = (f32[512,1024]{1,0:T(8,128)}, f32[1,1,2,256,256]{4,3,2,1,0:T(8,128)}) custom-call(s32[4,32]{1,0:T(4,128)S(1)} %bitcast.9, bf16[800,256]{1,0:T(8,128)(2,1)S(1)} %collective-permute-done.3.third, bf16[800,256]{1,0:T(8,128)(2,1)} %collective-permute-done.4.first, ...), custom_call_target="tpu_custom_call", output_to_operand_aliasing={{0}: (7, {}), {1}: (8, {})} | custom-call | tf_op jit(solution)/shard_map/pallas_call | solution.py:244
  127.0 5.9 %collective-permute-done.7 = bf16[64,256]{1,0:T(8,128)(2,1)S(1)} collective-permute-done((bf16[64,256]{1,0:T(8,128)(2,1)S(1)}, bf16[64,256]{1,0:T(8,128)(2,1)S(1)}, u32[]{:S(2)}, u32[]{:S(2)}) %collective-permute-start.7) | collective-permute-done | bytes 32800 | tf_op jit(solution)/shard_map/ppermute | solution.py:366
  132.9 0.6 copy.14
Async XLA Ops:
  28.9 8.4 %copy-start.4 = (bf16[256,512]{1,0:T(8,128)(2,1)S(1)}, bf16[256,512]{1,0:T(8,128)(2,1)}, u32[]{:S(2)}) copy-start(bf16[256,512]{1,0:T(8,128)(2,1)} %own.1) | copy-start | bytes 786436
  29.8 58.5 %copy-start = (f32[512,1024]{1,0:T(8,128)S(1)}, f32[512,1024]{1,0:T(8,128)}, u32[]{:S(2)}) copy-start(f32[512,1024]{1,0:T(8,128)} %weight_in.5) | copy-start | bytes 6291460
  29.8 17.9 %all-to-all-start.1 = ((bf16[4,200,256]{2,1,0:T(8,128)(2,1)}), bf16[4,200,256]{2,1,0:T(8,128)(2,1)S(1)}, u32[]{:S(2)}, u32[]{:S(2)}) async-start(bf16[4,200,256]{2,1,0:T(8,128)(2,1)} %bitcast.1), calls=%async_computation.1 | async-start | bytes 819200 | tf_op jit(solution)/shard_map/all_to_all | solution.py:256
  37.2 8.4 %collective-permute-start = (bf16[256,512]{1,0:T(8,128)(2,1)S(1)}, bf16[256,512]{1,0:T(8,128)(2,1)}, u32[]{:S(2)}, u32[]{:S(2)}) collective-permute-start(bf16[256,512]{1,0:T(8,128)(2,1)S(1)} %copy-done.4), channel_id=1, source_target_pairs={{0,576},{192,0},{384,192},{576,384},{1,577},{193,1},{385,193},{577... | collective-permute-start | bytes 786440 | tf_op jit(solution)/shard_map/ppermute | solution.py:261
  48.5 23.4 %all-to-all-start.2 = ((bf16[3,200,256]{2,1,0:T(8,128)(2,1)}), bf16[3,200,256]{2,1,0:T(8,128)(2,1)S(1)}, u32[]{:S(2)}, u32[]{:S(2)}) async-start(bf16[3,200,256]{2,1,0:T(8,128)(2,1)} %shard_map.87), calls=%async_computation.2 | async-start | bytes 614400 | tf_op jit(solution)/shard_map/all_to_all | solution.py:256
  59.7 9.9 %collective-permute-start.1 = (bf16[256,512]{1,0:T(8,128)(2,1)S(1)}, bf16[256,512]{1,0:T(8,128)(2,1)}, u32[]{:S(2)}, u32[]{:S(2)}) collective-permute-start(bf16[256,512]{1,0:T(8,128)(2,1)S(1)} %copy-done.4), channel_id=1, source_target_pairs={{0,384},{192,576},{384,0},{576,192},{1,385},{193,577},{385,1},{577... | collective-permute-start | bytes 786440 | tf_op jit(solution)/shard_map/ppermute | solution.py:261
  72.8 15.5 %all-to-all-start.3 = ((bf16[4,200,256]{2,1,0:T(8,128)(2,1)}), bf16[4,200,256]{2,1,0:T(8,128)(2,1)S(1)}, u32[]{:S(2)}, u32[]{:S(2)}) async-start(bf16[4,200,256]{2,1,0:T(8,128)(2,1)} %shard_map.88), calls=%async_computation.3 | async-start | bytes 819200 | tf_op jit(solution)/shard_map/all_to_all | solution.py:256
  76.8 10.4 %collective-permute-start.2 = (bf16[256,512]{1,0:T(8,128)(2,1)S(1)}, bf16[256,512]{1,0:T(8,128)(2,1)S(1)}, u32[]{:S(2)}, u32[]{:S(2)}) collective-permute-start(bf16[256,512]{1,0:T(8,128)(2,1)S(1)} %copy-done.4), channel_id=1, source_target_pairs={{0,192},{192,384},{384,576},{576,0},{1,193},{193,385},{385,577},{5... | collective-permute-start | bytes 786440 | tf_op jit(solution)/shard_map/ppermute | solution.py:261
  87.1 1.2 copy-start.5
  88.3 19.8 %copy-start.1 = (f32[1,1,2,256,256]{4,3,2,1,0:T(8,128)S(1)}, f32[1,1,2,256,256]{4,3,2,1,0:T(8,128)}, u32[]{:S(2)}) copy-start(f32[1,1,2,256,256]{4,3,2,1,0:T(8,128)} %stats_in.5) | copy-start | bytes 1572868
  88.3 19.8 %copy-start.3 = (s32[32,4]{0,1:T(4,128)S(1)}, s32[32,4]{0,1:T(4,128)}, u32[]{:S(2)}) copy-start(s32[32,4]{0,1:T(4,128)} %param.10) | copy-start | bytes 1540
  93.5 0.8 copy-start.2
  94.3 25.3 %all-to-all-start.4 = ((bf16[16,64,256]{2,1,0:T(8,128)(2,1)}), bf16[16,64,256]{2,1,0:T(8,128)(2,1)}, u32[]{:S(2)}, u32[]{:S(2)}) async-start(bf16[16,64,256]{2,1,0:T(8,128)(2,1)} %bitcast.6), calls=%async_computation.4 | async-start | bytes 1048576 | tf_op jit(solution)/shard_map/all_to_all | solution.py:256
  101.5 13.5 %collective-permute-start.3 = (bf16[800,256]{1,0:T(8,128)(2,1)S(1)}, bf16[800,256]{1,0:T(8,128)(2,1)S(1)}, u32[]{:S(2)}, u32[]{:S(2)}) collective-permute-start(bf16[800,256]{1,0:T(8,128)(2,1)S(1)} %get-tuple-element.32.own), channel_id=1, source_target_pairs={{0,576},{192,0},{384,192},{576,384},{1,577},{193,1},{385,193},{577... | collective-permute-start | bytes 1228808 | tf_op jit(solution)/shard_map/ppermute | solution.py:261
  104.4 18.8 %collective-permute-start.4 = (bf16[800,256]{1,0:T(8,128)(2,1)S(1)}, bf16[800,256]{1,0:T(8,128)(2,1)}, u32[]{:S(2)}, u32[]{:S(2)}) collective-permute-start(bf16[800,256]{1,0:T(8,128)(2,1)S(1)} %get-tuple-element.32.own), channel_id=1, source_target_pairs={{0,192},{192,384},{384,576},{576,0},{1,193},{193,385},{385,577},{5... | collective-permute-start | bytes 1228808 | tf_op jit(solution)/shard_map/ppermute | solution.py:261
  109.6 13.4 %collective-permute-start.5 = (bf16[400,256]{1,0:T(8,128)(2,1)}, bf16[400,256]{1,0:T(8,128)(2,1)}, u32[]{:S(2)}, u32[]{:S(2)}) collective-permute-start(bf16[400,256]{1,0:T(8,128)(2,1)} %slice.6), channel_id=1, source_target_pairs={{0,384},{192,576},{384,0},{576,192},{1,385},{193,577},{385,1},{577... | collective-permute-start | bytes 614408 | tf_op jit(solution)/shard_map/ppermute | solution.py:261
  115.7 8.5 %collective-permute-start.6 = (bf16[400,256]{1,0:T(8,128)(2,1)}, bf16[400,256]{1,0:T(8,128)(2,1)}, u32[]{:S(2)}, u32[]{:S(2)}) collective-permute-start(bf16[400,256]{1,0:T(8,128)(2,1)} %slice.7), channel_id=1, source_target_pairs={{0,576},{192,0},{384,192},{576,384},{1,577},{193,1},{385,193},{577... | collective-permute-start | bytes 614408 | tf_op jit(solution)/shard_map/ppermute | solution.py:261
  120.8 12.1 %collective-permute-start.7 = (bf16[64,256]{1,0:T(8,128)(2,1)S(1)}, bf16[64,256]{1,0:T(8,128)(2,1)S(1)}, u32[]{:S(2)}, u32[]{:S(2)}) collective-permute-start(bf16[64,256]{1,0:T(8,128)(2,1)S(1)} %reduce_sum.12), channel_id=1, source_target_pairs={{0,0},{1,1},{2,2},{3,3},{4,192},{5,193},{6,194},{7,195},{8,384},{9... | collective-permute-start | bytes 98312 | tf_op jit(solution)/shard_map/ppermute | solution.py:366

commit v9 on v8

--- a/solution.py
+++ b/solution.py
@@ -113,13 +113,41 @@
                 pack(stats[jnp.minimum(slot, 1)], out.at[i], r * EACH + W)
 
 
-def sum_kernel(tiles, out):
-    total = tiles[0].astype(F32)
+def sum_rows_kernel(tiles, out, total, sems):
+    sends = []
+    step = tiles.shape[1] // sems.shape[0]
+    for piece in range(sems.shape[0]):
+        rows = slice(piece * step, (piece + 1) * step)
+        part = tiles[0, rows, :].astype(F32)
+        for i in range(1, tiles.shape[0]):
+            part += tiles[i, rows, :].astype(F32)
+        total[rows, :] = part.astype(BF)
+        sends.append(pltpu.make_async_copy(total.at[rows], out.at[rows], sems.at[piece]))
+        sends[-1].start()
+    for send in sends:
+        send.wait()
+
+
+def sum_kernel(tiles, out, total, sems):
+    part = tiles[0].astype(F32)
     for i in range(1, tiles.shape[0]):
+        part += tiles[i].astype(F32)
+    total[...] = part.astype(BF)
+    sends = start_copies([(total, out.at[i]) for i in range(out.shape[0])], sems)
+    for send in sends:
+        send.wait()
+
+
+def gather_sum_kernel(tiles_in, out, tiles, sems):
+    step = tiles.shape[0] // sems.shape[0]
+    pieces = [pl.ds(i * step, step) for i in range(sems.shape[0])]
+    copies = start_copies([(tiles_in.at[piece], tiles.at[piece]) for piece in pieces], sems)
+    total = jnp.zeros(tiles.shape[1:], F32)
+    for i in range(tiles.shape[0]):
+        if i % step == 0:
+            copies[i // step].wait()
         total += tiles[i].astype(F32)
-    total = total.astype(BF)
-    for i in range(out.shape[0]):
-        out[i] = total
+    out[...] = total.astype(BF)
 
 
 def dot(a, b):
@@ -283,15 +311,31 @@
         ],
     )
     share = SENT // n_zl
-    column = call(sum_kernel, shape((1, SENT, W), BF), swap(sent, "x"))
+
+    def copies_of_sum(count, tiles):
+        return call(
+            sum_kernel,
+            shape((count, share, W), BF),
+            tiles,
+            out_specs=IN_HBM,
+            scratch=[pltpu.VMEM((share, W), BF), dma((count,))],
+        )
+
+    column = call(
+        sum_rows_kernel,
+        shape((SENT, W), BF),
+        swap(sent, "x"),
+        out_specs=IN_HBM,
+        scratch=[pltpu.VMEM((SENT, W), BF), dma((5,))],
+    )
     column, acts = lax.optimization_barrier((column, next_acts))
     acts_3 = turn(acts, "x", 3)
     tiles = swap(column.reshape(n_zl, share, W), "zl")
     tiles, acts_3 = lax.optimization_barrier((tiles, acts_3))
-    part, acts = lax.optimization_barrier((call(sum_kernel, shape((n_zh, share, W), BF), tiles), acts))
+    part, acts = lax.optimization_barrier((copies_of_sum(n_zh, tiles), acts))
     acts_2 = turn(acts, "x", 2)
     tiles, acts_2 = lax.optimization_barrier((swap(part, "zh"), acts_2))
-    mine, acts = lax.optimization_barrier((call(sum_kernel, shape((n_zl, share, W), BF), tiles), acts))
+    mine, acts = lax.optimization_barrier((copies_of_sum(n_zl, tiles), acts))
     acts_1 = turn(acts, "x", 1)
     full = swap(mine, "zl").reshape(SENT, W)
     acts_1, acts_2, acts_3 = (pltpu.with_memory_space_constraint(a, pltpu.HBM) for a in (acts_1, acts_2, acts_3))
@@ -355,7 +399,13 @@
         ],
         aliases={7: 0, 8: 1},
     )
-    summed = jnp.sum(tiles.astype(F32), axis=0).astype(BF)
+    summed = call(
+        gather_sum_kernel,
+        shape(tiles.shape[1:], BF),
+        pltpu.with_memory_space_constraint(tiles, pltpu.HBM),
+        specs=[IN_HBM],
+        scratch=[pltpu.VMEM(tiles.shape, BF), dma((8,))],
+    )
     each = n_feat // n_x
     pairs = [
         (x * n_feat + to * each + j, to * n_feat + x * each + j)

time: 134 us -> 134 us (level)
    pallas_call x7 -> x8, Pallas kernels: 14.6 us -> 15.7 us  [call(): pl.pallas_call(kernel, out_shape=out, in_specs=specs or [IN_VMEM] * len(a...]
  transfers between devices with their start and end apart: 12 -> 12, of which waited for: 10 -> 10; matrix products, arithmetic and copies ran while one was open for 2% -> 1% of each run, Pallas kernels for 3% -> 4%
where the time goes in v9:
time: 134 us
  starting transfers between devices  53.7 us (40%)
  waiting for transfers between devices  35 us (26%)
  blocking collectives  25.5 us (19%)
  Pallas kernels  15.7 us (12%)
  local copies, waits for them, and re-layouts  2.84 us (2%)
    all_to_all x4, starting transfers between devices, swap(): return lax.all_to_all(x, axis, 0, 0, tiled=True)  29.9 us
    all_to_all x1, blocking collectives, swap(): return lax.all_to_all(x, axis, 0, 0, tiled=True)  25.5 us
    ppermute x7, waiting for transfers between devices, turn(): return lax.ppermute(x, axis, [(i, (i + by) % n) for i in range(n)])  23.3 us
    ppermute x7, starting transfers between devices, turn(): return lax.ppermute(x, axis, [(i, (i + by) % n) for i in range(n)])  21.6 us
    pallas_call x8, Pallas kernels, call(): pl.pallas_call(kernel, out_shape=out, in_specs=specs or [IN_VMEM] * len(a...  15.7 us
    ppermute x1, waiting for transfers between devices, body(): next_out = lax.ppermute(summed, ('x', 'feat'), pairs).T  5.97 us
    all_to_all x4, waiting for transfers between devices, swap(): return lax.all_to_all(x, axis, 0, 0, tiled=True)  5.69 us
  transfers between devices with their start and end apart: 12, of which 10 were waited for; matrix products, arithmetic and copies ran while one was open for 1% of the time, Pallas kernels for 4%

profile of v9, /device:TPU:32, one launch (start us, length us, event | category | flops | bytes accessed | tf_op | source)
XLA Modules:
  0.0 133.6 jit_solution(844947614733968952)
XLA Ops:
  0.6 2.7 %shard_map.85 = bf16[4,800,256]{2,1,0:T(8,128)(2,1)S(1)} custom-call(s32[4,32]{1,0:T(4,128)} %bitcast.7, bf16[256,512]{1,0:T(8,128)(2,1)} %acts_in.1, bf16[256,1024]{1,0:T(8,128)(2,1)} %cot_in.1, f32[1,1,2,256,256]{4,3,2,1,0:T(8,128)} %stats_in.5), custom_call_target="tpu_custom_call" | custom-call | tf_op jit(solution)/shard_map/pallas_call | solution.py:272
  3.3 25.5 %all_to_all.25.tiles = bf16[4,800,256]{2,1,0:T(8,128)(2,1)S(1)} all-to-all(bf16[4,800,256]{2,1,0:T(8,128)(2,1)S(1)} %shard_map.85), channel_id=1, replica_groups=mesh['x'=4,'zh'=3,'zl'=4,'feat'=16] {'x'}, dimensions={0} | all-to-all | bytes 3276800 | tf_op jit(solution)/shard_map/all_to_all | solution.py:284
  28.9 0.0 copy-start.4
  28.9 0.9 shard_map.86
  29.7 0.0 copy-start
  29.8 7.4 %all-to-all-start.1 = ((bf16[4,200,256]{2,1,0:T(8,128)(2,1)}), bf16[4,200,256]{2,1,0:T(8,128)(2,1)S(1)}, u32[]{:S(2)}, u32[]{:S(2)}) async-start(bf16[4,200,256]{2,1,0:T(8,128)(2,1)} %bitcast.1), calls=%async_computation.1 | async-start | bytes 819200 | tf_op jit(solution)/shard_map/all_to_all | solution.py:284
  37.2 0.0 copy-done.4
  37.2 3.1 %collective-permute-start = (bf16[256,512]{1,0:T(8,128)(2,1)S(1)}, bf16[256,512]{1,0:T(8,128)(2,1)}, u32[]{:S(2)}, u32[]{:S(2)}) collective-permute-start(bf16[256,512]{1,0:T(8,128)(2,1)S(1)} %copy-done.4), channel_id=1, source_target_pairs={{0,576},{192,0},{384,192},{576,384},{1,577},{193,1},{385,193},{577... | collective-permute-start | bytes 786440 | tf_op jit(solution)/shard_map/ppermute | solution.py:289
  40.2 5.3 %collective-permute-done.third = bf16[256,512]{1,0:T(8,128)(2,1)} collective-permute-done((bf16[256,512]{1,0:T(8,128)(2,1)S(1)}, bf16[256,512]{1,0:T(8,128)(2,1)}, u32[]{:S(2)}, u32[]{:S(2)}) %collective-permute-start) | collective-permute-done | bytes 262176 | tf_op jit(solution)/shard_map/ppermute | solution.py:289
  45.5 2.1 %all-to-all-done.1.tiles = bf16[4,200,256]{2,1,0:T(8,128)(2,1)S(1)} async-done(((bf16[4,200,256]{2,1,0:T(8,128)(2,1)}), bf16[4,200,256]{2,1,0:T(8,128)(2,1)S(1)}, u32[]{:S(2)}, u32[]{:S(2)}) %all-to-all-start.1) | async-done | bytes 409632 | tf_op jit(solution)/shard_map/all_to_all | solution.py:284
  47.7 0.8 shard_map.87
  48.5 11.3 %all-to-all-start.2 = ((bf16[3,200,256]{2,1,0:T(8,128)(2,1)}), bf16[3,200,256]{2,1,0:T(8,128)(2,1)S(1)}, u32[]{:S(2)}, u32[]{:S(2)}) async-start(bf16[3,200,256]{2,1,0:T(8,128)(2,1)} %shard_map.87), calls=%async_computation.2 | async-start | bytes 614400 | tf_op jit(solution)/shard_map/all_to_all | solution.py:284
  59.7 3.0 %collective-permute-start.1 = (bf16[256,512]{1,0:T(8,128)(2,1)S(1)}, bf16[256,512]{1,0:T(8,128)(2,1)}, u32[]{:S(2)}, u32[]{:S(2)}) collective-permute-start(bf16[256,512]{1,0:T(8,128)(2,1)S(1)} %copy-done.4), channel_id=1, source_target_pairs={{0,384},{192,576},{384,0},{576,192},{1,385},{193,577},{385,1},{577... | collective-permute-start | bytes 786440 | tf_op jit(solution)/shard_map/ppermute | solution.py:289
  62.8 6.8 %collective-permute-done.1.second = bf16[256,512]{1,0:T(8,128)(2,1)} collective-permute-done((bf16[256,512]{1,0:T(8,128)(2,1)S(1)}, bf16[256,512]{1,0:T(8,128)(2,1)}, u32[]{:S(2)}, u32[]{:S(2)}) %collective-permute-start.1) | collective-permute-done | bytes 262176 | tf_op jit(solution)/shard_map/ppermute | solution.py:289
  69.6 2.4 %all-to-all-done.2.tiles = bf16[3,200,256]{2,1,0:T(8,128)(2,1)S(1)} async-done(((bf16[3,200,256]{2,1,0:T(8,128)(2,1)}), bf16[3,200,256]{2,1,0:T(8,128)(2,1)S(1)}, u32[]{:S(2)}, u32[]{:S(2)}) %all-to-all-start.2) | async-done | bytes 307232 | tf_op jit(solution)/shard_map/all_to_all | solution.py:284
  72.0 0.8 shard_map.88
  72.8 4.0 %all-to-all-start.3 = ((bf16[4,200,256]{2,1,0:T(8,128)(2,1)}), bf16[4,200,256]{2,1,0:T(8,128)(2,1)S(1)}, u32[]{:S(2)}, u32[]{:S(2)}) async-start(bf16[4,200,256]{2,1,0:T(8,128)(2,1)} %shard_map.88), calls=%async_computation.3 | async-start | bytes 819200 | tf_op jit(solution)/shard_map/all_to_all | solution.py:284
  76.8 2.5 %collective-permute-start.2 = (bf16[256,512]{1,0:T(8,128)(2,1)S(1)}, bf16[256,512]{1,0:T(8,128)(2,1)S(1)}, u32[]{:S(2)}, u32[]{:S(2)}) collective-permute-start(bf16[256,512]{1,0:T(8,128)(2,1)S(1)} %copy-done.4), channel_id=1, source_target_pairs={{0,192},{192,384},{384,576},{576,0},{1,193},{193,385},{385,577},{5... | collective-permute-start | bytes 786440 | tf_op jit(solution)/shard_map/ppermute | solution.py:289
  79.3 7.9 %collective-permute-done.2.first = bf16[256,512]{1,0:T(8,128)(2,1)S(1)} collective-permute-done((bf16[256,512]{1,0:T(8,128)(2,1)S(1)}, bf16[256,512]{1,0:T(8,128)(2,1)S(1)}, u32[]{:S(2)}, u32[]{:S(2)}) %collective-permute-start.2) | collective-permute-done | bytes 262176 | tf_op jit(solution)/shard_map/ppermute | solution.py:289
  87.2 0.0 copy-start.5
  87.2 1.2 all-to-all-done.3
  88.3 0.0 copy-done.5
  88.3 0.0 copy-done
  88.4 0.0 copy-start.1
  88.4 0.0 copy-start.3
  88.4 5.2 %shard_map.89 = (bf16[800,256]{1,0:T(8,128)(2,1)S(1)}, bf16[4,256,256]{2,1,0:T(8,128)(2,1)S(1)}) custom-call(bf16[800,256]{1,0:T(8,128)(2,1)S(1)} %bitcast.5, f32[512,1024]{1,0:T(8,128)S(1)} %copy-done, bf16[256,512]{1,0:T(8,128)(2,1)} %own.1, bf16[256,512]{1,0:T(8,128)(2,1)} %copy-done.5, bf16[256,512]{1,0:T(8,128)(2,1)} %collective-permute-done.1.second, ...), custom_call_target="tpu_custom_call" | custom-call | tf_op jit(solution)/shard_map/pallas_call | solution.py:272
  93.6 0.0 copy-start.2
  93.6 0.8 copy-done.2
  94.4 7.2 %all-to-all-start.4 = ((bf16[16,64,256]{2,1,0:T(8,128)(2,1)}), bf16[16,64,256]{2,1,0:T(8,128)(2,1)}, u32[]{:S(2)}, u32[]{:S(2)}) async-start(bf16[16,64,256]{2,1,0:T(8,128)(2,1)} %bitcast.6), calls=%async_computation.4 | async-start | bytes 1048576 | tf_op jit(solution)/shard_map/all_to_all | solution.py:284
  101.6 2.8 %collective-permute-start.3 = (bf16[800,256]{1,0:T(8,128)(2,1)S(1)}, bf16[800,256]{1,0:T(8,128)(2,1)S(1)}, u32[]{:S(2)}, u32[]{:S(2)}) collective-permute-start(bf16[800,256]{1,0:T(8,128)(2,1)S(1)} %get-tuple-element.32.own), channel_id=1, source_target_pairs={{0,576},{192,0},{384,192},{576,384},{1,577},{193,1},{385,193},{577... | collective-permute-start | bytes 1228808 | tf_op jit(solution)/shard_map/ppermute | solution.py:289
  104.4 3.0 %collective-permute-start.4 = (bf16[800,256]{1,0:T(8,128)(2,1)S(1)}, bf16[800,256]{1,0:T(8,128)(2,1)}, u32[]{:S(2)}, u32[]{:S(2)}) collective-permute-start(bf16[800,256]{1,0:T(8,128)(2,1)S(1)} %get-tuple-element.32.own), channel_id=1, source_target_pairs={{0,192},{192,384},{384,576},{576,0},{1,193},{193,385},{385,577},{5... | collective-permute-start | bytes 1228808 | tf_op jit(solution)/shard_map/ppermute | solution.py:289
  107.4 0.7 slice.6
  108.2 0.0 copy-done.1
  108.2 0.0 copy-done.3
  108.2 1.5 %shard_map.90 = (f32[512,1024]{1,0:T(8,128)}, f32[1,1,2,256,256]{4,3,2,1,0:T(8,128)}) custom-call(s32[4,32]{1,0:T(4,128)S(1)} %bitcast.8, bf16[800,256]{1,0:T(8,128)(2,1)S(1)} %get-tuple-element.32.own, f32[512,1024]{1,0:T(8,128)S(1)} %copy-done, f32[1,1,2,256,256]{4,3,2,1,0:T(8,128)S(1)} %copy-done.1), custom_call_target="tpu_custom_call" | custom-call | tf_op jit(solution)/shard_map/pallas_call | solution.py:272
  109.6 3.3 %collective-permute-start.5 = (bf16[400,256]{1,0:T(8,128)(2,1)}, bf16[400,256]{1,0:T(8,128)(2,1)}, u32[]{:S(2)}, u32[]{:S(2)}) collective-permute-start(bf16[400,256]{1,0:T(8,128)(2,1)} %slice.6), channel_id=1, source_target_pairs={{0,384},{192,576},{384,0},{576,192},{1,385},{193,577},{385,1},{577... | collective-permute-start | bytes 614408 | tf_op jit(solution)/shard_map/ppermute | solution.py:289
  112.9 2.1 %collective-permute-done.3.third = bf16[800,256]{1,0:T(8,128)(2,1)S(1)} collective-permute-done((bf16[800,256]{1,0:T(8,128)(2,1)S(1)}, bf16[800,256]{1,0:T(8,128)(2,1)S(1)}, u32[]{:S(2)}, u32[]{:S(2)}) %collective-permute-start.3) | collective-permute-done | bytes 409632 | tf_op jit(solution)/shard_map/ppermute | solution.py:289
  115.1 0.7 slice.7
  115.8 4.0 %collective-permute-start.6 = (bf16[400,256]{1,0:T(8,128)(2,1)}, bf16[400,256]{1,0:T(8,128)(2,1)}, u32[]{:S(2)}, u32[]{:S(2)}) collective-permute-start(bf16[400,256]{1,0:T(8,128)(2,1)} %slice.7), channel_id=1, source_target_pairs={{0,576},{192,0},{384,192},{576,384},{1,577},{193,1},{385,193},{577... | collective-permute-start | bytes 614408 | tf_op jit(solution)/shard_map/ppermute | solution.py:289
  119.7 0.0 all-to-all-done.4.tiles_in
  119.7 1.1 shard_map.92
  120.9 2.2 %collective-permute-start.7 = (bf16[64,256]{1,0:T(8,128)(2,1)S(1)}, bf16[64,256]{1,0:T(8,128)(2,1)S(1)}, u32[]{:S(2)}, u32[]{:S(2)}) collective-permute-start(bf16[64,256]{1,0:T(8,128)(2,1)S(1)} %shard_map.92), channel_id=1, source_target_pairs={{0,0},{1,1},{2,2},{3,3},{4,192},{5,193},{6,194},{7,195},{8,384},{9... | collective-permute-start | bytes 98312 | tf_op jit(solution)/shard_map/ppermute | solution.py:416
  123.1 0.0 collective-permute-done.5.top
  123.1 0.1 collective-permute-done.4.first
  123.3 1.1 collective-permute-done.6.low
  124.3 2.7 %shard_map.91 = (f32[512,1024]{1,0:T(8,128)}, f32[1,1,2,256,256]{4,3,2,1,0:T(8,128)}) custom-call(s32[4,32]{1,0:T(4,128)S(1)} %bitcast.9, bf16[800,256]{1,0:T(8,128)(2,1)S(1)} %collective-permute-done.3.third, bf16[800,256]{1,0:T(8,128)(2,1)} %collective-permute-done.4.first, ...), custom_call_target="tpu_custom_call", output_to_operand_aliasing={{0}: (7, {}), {1}: (8, {})} | custom-call | tf_op jit(solution)/shard_map/pallas_call | solution.py:272
  127.0 6.0 %collective-permute-done.7 = bf16[64,256]{1,0:T(8,128)(2,1)S(1)} collective-permute-done((bf16[64,256]{1,0:T(8,128)(2,1)S(1)}, bf16[64,256]{1,0:T(8,128)(2,1)S(1)}, u32[]{:S(2)}, u32[]{:S(2)}) %collective-permute-start.7) | collective-permute-done | bytes 32800 | tf_op jit(solution)/shard_map/ppermute | solution.py:416
  133.0 0.6 copy.14
Async XLA Ops:
  28.9 8.3 %copy-start.4 = (bf16[256,512]{1,0:T(8,128)(2,1)S(1)}, bf16[256,512]{1,0:T(8,128)(2,1)}, u32[]{:S(2)}) copy-start(bf16[256,512]{1,0:T(8,128)(2,1)} %own.1) | copy-start | bytes 786436
  29.7 58.6 %copy-start = (f32[512,1024]{1,0:T(8,128)S(1)}, f32[512,1024]{1,0:T(8,128)}, u32[]{:S(2)}) copy-start(f32[512,1024]{1,0:T(8,128)} %weight_in.5) | copy-start | bytes 6291460
  29.8 17.9 %all-to-all-start.1 = ((bf16[4,200,256]{2,1,0:T(8,128)(2,1)}), bf16[4,200,256]{2,1,0:T(8,128)(2,1)S(1)}, u32[]{:S(2)}, u32[]{:S(2)}) async-start(bf16[4,200,256]{2,1,0:T(8,128)(2,1)} %bitcast.1), calls=%async_computation.1 | async-start | bytes 819200 | tf_op jit(solution)/shard_map/all_to_all | solution.py:284
  37.2 8.4 %collective-permute-start = (bf16[256,512]{1,0:T(8,128)(2,1)S(1)}, bf16[256,512]{1,0:T(8,128)(2,1)}, u32[]{:S(2)}, u32[]{:S(2)}) collective-permute-start(bf16[256,512]{1,0:T(8,128)(2,1)S(1)} %copy-done.4), channel_id=1, source_target_pairs={{0,576},{192,0},{384,192},{576,384},{1,577},{193,1},{385,193},{577... | collective-permute-start | bytes 786440 | tf_op jit(solution)/shard_map/ppermute | solution.py:289
  48.5 23.5 %all-to-all-start.2 = ((bf16[3,200,256]{2,1,0:T(8,128)(2,1)}), bf16[3,200,256]{2,1,0:T(8,128)(2,1)S(1)}, u32[]{:S(2)}, u32[]{:S(2)}) async-start(bf16[3,200,256]{2,1,0:T(8,128)(2,1)} %shard_map.87), calls=%async_computation.2 | async-start | bytes 614400 | tf_op jit(solution)/shard_map/all_to_all | solution.py:284
  59.7 9.9 %collective-permute-start.1 = (bf16[256,512]{1,0:T(8,128)(2,1)S(1)}, bf16[256,512]{1,0:T(8,128)(2,1)}, u32[]{:S(2)}, u32[]{:S(2)}) collective-permute-start(bf16[256,512]{1,0:T(8,128)(2,1)S(1)} %copy-done.4), channel_id=1, source_target_pairs={{0,384},{192,576},{384,0},{576,192},{1,385},{193,577},{385,1},{577... | collective-permute-start | bytes 786440 | tf_op jit(solution)/shard_map/ppermute | solution.py:289
  72.8 15.6 %all-to-all-start.3 = ((bf16[4,200,256]{2,1,0:T(8,128)(2,1)}), bf16[4,200,256]{2,1,0:T(8,128)(2,1)S(1)}, u32[]{:S(2)}, u32[]{:S(2)}) async-start(bf16[4,200,256]{2,1,0:T(8,128)(2,1)} %shard_map.88), calls=%async_computation.3 | async-start | bytes 819200 | tf_op jit(solution)/shard_map/all_to_all | solution.py:284
  76.8 10.4 %collective-permute-start.2 = (bf16[256,512]{1,0:T(8,128)(2,1)S(1)}, bf16[256,512]{1,0:T(8,128)(2,1)S(1)}, u32[]{:S(2)}, u32[]{:S(2)}) collective-permute-start(bf16[256,512]{1,0:T(8,128)(2,1)S(1)} %copy-done.4), channel_id=1, source_target_pairs={{0,192},{192,384},{384,576},{576,0},{1,193},{193,385},{385,577},{5... | collective-permute-start | bytes 786440 | tf_op jit(solution)/shard_map/ppermute | solution.py:289
  87.2 1.2 copy-start.5
  88.4 19.8 %copy-start.1 = (f32[1,1,2,256,256]{4,3,2,1,0:T(8,128)S(1)}, f32[1,1,2,256,256]{4,3,2,1,0:T(8,128)}, u32[]{:S(2)}) copy-start(f32[1,1,2,256,256]{4,3,2,1,0:T(8,128)} %stats_in.5) | copy-start | bytes 1572868
  88.4 19.8 %copy-start.3 = (s32[32,4]{0,1:T(4,128)S(1)}, s32[32,4]{0,1:T(4,128)}, u32[]{:S(2)}) copy-start(s32[32,4]{0,1:T(4,128)} %param.10) | copy-start | bytes 1540
  93.6 0.8 copy-start.2
  94.4 25.4 %all-to-all-start.4 = ((bf16[16,64,256]{2,1,0:T(8,128)(2,1)}), bf16[16,64,256]{2,1,0:T(8,128)(2,1)}, u32[]{:S(2)}, u32[]{:S(2)}) async-start(bf16[16,64,256]{2,1,0:T(8,128)(2,1)} %bitcast.6), calls=%async_computation.4 | async-start | bytes 1048576 | tf_op jit(solution)/shard_map/all_to_all | solution.py:284
  101.6 13.5 %collective-permute-start.3 = (bf16[800,256]{1,0:T(8,128)(2,1)S(1)}, bf16[800,256]{1,0:T(8,128)(2,1)S(1)}, u32[]{:S(2)}, u32[]{:S(2)}) collective-permute-start(bf16[800,256]{1,0:T(8,128)(2,1)S(1)} %get-tuple-element.32.own), channel_id=1, source_target_pairs={{0,576},{192,0},{384,192},{576,384},{1,577},{193,1},{385,193},{577... | collective-permute-start | bytes 1228808 | tf_op jit(solution)/shard_map/ppermute | solution.py:289
  104.4 18.8 %collective-permute-start.4 = (bf16[800,256]{1,0:T(8,128)(2,1)S(1)}, bf16[800,256]{1,0:T(8,128)(2,1)}, u32[]{:S(2)}, u32[]{:S(2)}) collective-permute-start(bf16[800,256]{1,0:T(8,128)(2,1)S(1)} %get-tuple-element.32.own), channel_id=1, source_target_pairs={{0,192},{192,384},{384,576},{576,0},{1,193},{193,385},{385,577},{5... | collective-permute-start | bytes 1228808 | tf_op jit(solution)/shard_map/ppermute | solution.py:289
  109.6 13.5 %collective-permute-start.5 = (bf16[400,256]{1,0:T(8,128)(2,1)}, bf16[400,256]{1,0:T(8,128)(2,1)}, u32[]{:S(2)}, u32[]{:S(2)}) collective-permute-start(bf16[400,256]{1,0:T(8,128)(2,1)} %slice.6), channel_id=1, source_target_pairs={{0,384},{192,576},{384,0},{576,192},{1,385},{193,577},{385,1},{577... | collective-permute-start | bytes 614408 | tf_op jit(solution)/shard_map/ppermute | solution.py:289
  115.8 8.6 %collective-permute-start.6 = (bf16[400,256]{1,0:T(8,128)(2,1)}, bf16[400,256]{1,0:T(8,128)(2,1)}, u32[]{:S(2)}, u32[]{:S(2)}) collective-permute-start(bf16[400,256]{1,0:T(8,128)(2,1)} %slice.7), channel_id=1, source_target_pairs={{0,576},{192,0},{384,192},{576,384},{1,577},{193,1},{385,193},{577... | collective-permute-start | bytes 614408 | tf_op jit(solution)/shard_map/ppermute | solution.py:289
  120.9 12.1 %collective-permute-start.7 = (bf16[64,256]{1,0:T(8,128)(2,1)S(1)}, bf16[64,256]{1,0:T(8,128)(2,1)S(1)}, u32[]{:S(2)}, u32[]{:S(2)}) collective-permute-start(bf16[64,256]{1,0:T(8,128)(2,1)S(1)} %shard_map.92), channel_id=1, source_target_pairs={{0,0},{1,1},{2,2},{3,3},{4,192},{5,193},{6,194},{7,195},{8,384},{9... | collective-permute-start | bytes 98312 | tf_op jit(solution)/shard_map/ppermute | solution.py:416

commit v10 on v8

--- a/solution.py
+++ b/solution.py
@@ -148,16 +148,16 @@
         norms.append(norm)
         iterates.append(None)
     for step in range(ITERS):
-        for r in range(2):
-            low = ((5.0 * identity - matrices[r]) / 4.0).astype(BF)
-            if step == 0:
-                iterates[r] = low.astype(F32)
-            else:
-                iterates[r] = dot(iterates[r].astype(BF), low)
-            if step + 1 < ITERS:
-                square = dot(low, low).astype(BF)
-                fourth = dot(square, square).astype(BF)
-                matrices[r] = dot(fourth, matrices[r].astype(BF))
+        lows = [((5.0 * identity - matrix) / 4.0).astype(BF) for matrix in matrices]
+        if step + 1 < ITERS:
+            squares = [dot(low, low).astype(BF) for low in lows]
+        if step == 0:
+            iterates = [low.astype(F32) for low in lows]
+        else:
+            iterates = [dot(iterate.astype(BF), low) for iterate, low in zip(iterates, lows)]
+        if step + 1 < ITERS:
+            fourths = [dot(square, square).astype(BF) for square in squares]
+            matrices = [dot(fourth, matrix.astype(BF)) for fourth, matrix in zip(fourths, matrices)]
     for copy in copies:
         copy.wait()
     news = []

time: 134 us -> 133 us (level)
  no operation moved by 1% of the time
where the time goes in v10:
time: 133 us
  starting transfers between devices  53.6 us (40%)
  waiting for transfers between devices  35 us (26%)
  blocking collectives  25.5 us (19%)
  Pallas kernels  13.7 us (10%)
  local copies, waits for them, and re-layouts  2.8 us (2%)
    all_to_all x4, starting transfers between devices, swap(): return lax.all_to_all(x, axis, 0, 0, tiled=True)  29.7 us
    all_to_all x1, blocking collectives, swap(): return lax.all_to_all(x, axis, 0, 0, tiled=True)  25.5 us
    ppermute x7, waiting for transfers between devices, turn(): return lax.ppermute(x, axis, [(i, (i + by) % n) for i in range(n)])  23.3 us
    ppermute x7, starting transfers between devices, turn(): return lax.ppermute(x, axis, [(i, (i + by) % n) for i in range(n)])  21.8 us
    pallas_call x7, Pallas kernels, call(): pl.pallas_call(kernel, out_shape=out, in_specs=specs or [IN_VMEM] * len(a...  13.7 us
    ppermute x1, waiting for transfers between devices, body(): next_out = lax.ppermute(summed, ('x', 'feat'), pairs).T  6.03 us
    all_to_all x4, waiting for transfers between devices, swap(): return lax.all_to_all(x, axis, 0, 0, tiled=True)  5.72 us
  transfers between devices with their start and end apart: 12, of which 10 were waited for; matrix products, arithmetic and copies ran while one was open for 2% of the time, Pallas kernels for 3%

profile of v10, /device:TPU:32, one launch (start us, length us, event | category | flops | bytes accessed | tf_op | source)
XLA Modules:
  0.0 132.6 jit_solution(560051170744706820)
XLA Ops:
  0.6 2.7 %shard_map.85 = bf16[4,800,256]{2,1,0:T(8,128)(2,1)S(1)} custom-call(s32[4,32]{1,0:T(4,128)} %bitcast.7, bf16[256,512]{1,0:T(8,128)(2,1)} %acts_in.1, bf16[256,1024]{1,0:T(8,128)(2,1)} %cot_in.1, f32[1,1,2,256,256]{4,3,2,1,0:T(8,128)} %stats_in.5), custom_call_target="tpu_custom_call" | custom-call | tf_op jit(solution)/shard_map/pallas_call | solution.py:244
  3.3 25.5 %all_to_all.25.tiles = bf16[4,800,256]{2,1,0:T(8,128)(2,1)S(1)} all-to-all(bf16[4,800,256]{2,1,0:T(8,128)(2,1)S(1)} %shard_map.85), channel_id=1, replica_groups=mesh['x'=4,'zh'=3,'zl'=4,'feat'=16] {'x'}, dimensions={0} | all-to-all | bytes 3276800 | tf_op jit(solution)/shard_map/all_to_all | solution.py:256
  28.9 0.0 copy-start.4
  28.9 1.0 shard_map.86
  29.8 0.0 copy-start
  29.8 7.4 %all-to-all-start.1 = ((bf16[4,200,256]{2,1,0:T(8,128)(2,1)}), bf16[4,200,256]{2,1,0:T(8,128)(2,1)S(1)}, u32[]{:S(2)}, u32[]{:S(2)}) async-start(bf16[4,200,256]{2,1,0:T(8,128)(2,1)} %bitcast.1), calls=%async_computation.1 | async-start | bytes 819200 | tf_op jit(solution)/shard_map/all_to_all | solution.py:256
  37.2 0.0 copy-done.4
  37.2 3.1 %collective-permute-start = (bf16[256,512]{1,0:T(8,128)(2,1)S(1)}, bf16[256,512]{1,0:T(8,128)(2,1)}, u32[]{:S(2)}, u32[]{:S(2)}) collective-permute-start(bf16[256,512]{1,0:T(8,128)(2,1)S(1)} %copy-done.4), channel_id=1, source_target_pairs={{0,576},{192,0},{384,192},{576,384},{1,577},{193,1},{385,193},{577... | collective-permute-start | bytes 786440 | tf_op jit(solution)/shard_map/ppermute | solution.py:261
  40.3 5.3 %collective-permute-done.third = bf16[256,512]{1,0:T(8,128)(2,1)} collective-permute-done((bf16[256,512]{1,0:T(8,128)(2,1)S(1)}, bf16[256,512]{1,0:T(8,128)(2,1)}, u32[]{:S(2)}, u32[]{:S(2)}) %collective-permute-start) | collective-permute-done | bytes 262176 | tf_op jit(solution)/shard_map/ppermute | solution.py:261
  45.6 2.2 %all-to-all-done.1.tiles = bf16[4,200,256]{2,1,0:T(8,128)(2,1)S(1)} async-done(((bf16[4,200,256]{2,1,0:T(8,128)(2,1)}), bf16[4,200,256]{2,1,0:T(8,128)(2,1)S(1)}, u32[]{:S(2)}, u32[]{:S(2)}) %all-to-all-start.1) | async-done | bytes 409632 | tf_op jit(solution)/shard_map/all_to_all | solution.py:256
  47.8 0.8 shard_map.87
  48.5 11.2 %all-to-all-start.2 = ((bf16[3,200,256]{2,1,0:T(8,128)(2,1)}), bf16[3,200,256]{2,1,0:T(8,128)(2,1)S(1)}, u32[]{:S(2)}, u32[]{:S(2)}) async-start(bf16[3,200,256]{2,1,0:T(8,128)(2,1)} %shard_map.87), calls=%async_computation.2 | async-start | bytes 614400 | tf_op jit(solution)/shard_map/all_to_all | solution.py:256
  59.7 3.0 %collective-permute-start.1 = (bf16[256,512]{1,0:T(8,128)(2,1)S(1)}, bf16[256,512]{1,0:T(8,128)(2,1)}, u32[]{:S(2)}, u32[]{:S(2)}) collective-permute-start(bf16[256,512]{1,0:T(8,128)(2,1)S(1)} %copy-done.4), channel_id=1, source_target_pairs={{0,384},{192,576},{384,0},{576,192},{1,385},{193,577},{385,1},{577... | collective-permute-start | bytes 786440 | tf_op jit(solution)/shard_map/ppermute | solution.py:261
  62.7 6.8 %collective-permute-done.1.second = bf16[256,512]{1,0:T(8,128)(2,1)} collective-permute-done((bf16[256,512]{1,0:T(8,128)(2,1)S(1)}, bf16[256,512]{1,0:T(8,128)(2,1)}, u32[]{:S(2)}, u32[]{:S(2)}) %collective-permute-start.1) | collective-permute-done | bytes 262176 | tf_op jit(solution)/shard_map/ppermute | solution.py:261
  69.6 2.4 %all-to-all-done.2.tiles = bf16[3,200,256]{2,1,0:T(8,128)(2,1)S(1)} async-done(((bf16[3,200,256]{2,1,0:T(8,128)(2,1)}), bf16[3,200,256]{2,1,0:T(8,128)(2,1)S(1)}, u32[]{:S(2)}, u32[]{:S(2)}) %all-to-all-start.2) | async-done | bytes 307232 | tf_op jit(solution)/shard_map/all_to_all | solution.py:256
  71.9 0.8 shard_map.88
  72.7 4.0 %all-to-all-start.3 = ((bf16[4,200,256]{2,1,0:T(8,128)(2,1)}), bf16[4,200,256]{2,1,0:T(8,128)(2,1)S(1)}, u32[]{:S(2)}, u32[]{:S(2)}) async-start(bf16[4,200,256]{2,1,0:T(8,128)(2,1)} %shard_map.88), calls=%async_computation.3 | async-start | bytes 819200 | tf_op jit(solution)/shard_map/all_to_all | solution.py:256
  76.7 2.5 %collective-permute-start.2 = (bf16[256,512]{1,0:T(8,128)(2,1)S(1)}, bf16[256,512]{1,0:T(8,128)(2,1)S(1)}, u32[]{:S(2)}, u32[]{:S(2)}) collective-permute-start(bf16[256,512]{1,0:T(8,128)(2,1)S(1)} %copy-done.4), channel_id=1, source_target_pairs={{0,192},{192,384},{384,576},{576,0},{1,193},{193,385},{385,577},{5... | collective-permute-start | bytes 786440 | tf_op jit(solution)/shard_map/ppermute | solution.py:261
  79.1 7.9 %collective-permute-done.2.first = bf16[256,512]{1,0:T(8,128)(2,1)S(1)} collective-permute-done((bf16[256,512]{1,0:T(8,128)(2,1)S(1)}, bf16[256,512]{1,0:T(8,128)(2,1)S(1)}, u32[]{:S(2)}, u32[]{:S(2)}) %collective-permute-start.2) | collective-permute-done | bytes 262176 | tf_op jit(solution)/shard_map/ppermute | solution.py:261
  87.0 0.0 copy-start.5
  87.0 1.2 all-to-all-done.3
  88.2 0.0 copy-done.5
  88.2 0.0 copy-done
  88.2 0.0 copy-start.1
  88.2 0.0 copy-start.3
  88.2 4.3 %shard_map.89 = (bf16[800,256]{1,0:T(8,128)(2,1)S(1)}, bf16[4,256,256]{2,1,0:T(8,128)(2,1)S(1)}) custom-call(bf16[800,256]{1,0:T(8,128)(2,1)S(1)} %bitcast.5, f32[512,1024]{1,0:T(8,128)S(1)} %copy-done, bf16[256,512]{1,0:T(8,128)(2,1)} %own.1, bf16[256,512]{1,0:T(8,128)(2,1)} %copy-done.5, bf16[256,512]{1,0:T(8,128)(2,1)} %collective-permute-done.1.second, ...), custom_call_target="tpu_custom_call" | custom-call | tf_op jit(solution)/shard_map/pallas_call | solution.py:244
  92.5 0.0 copy-start.2
  92.5 0.8 copy-done.2
  93.3 7.2 %all-to-all-start.4 = ((bf16[16,64,256]{2,1,0:T(8,128)(2,1)}), bf16[16,64,256]{2,1,0:T(8,128)(2,1)}, u32[]{:S(2)}, u32[]{:S(2)}) async-start(bf16[16,64,256]{2,1,0:T(8,128)(2,1)} %bitcast.6), calls=%async_computation.4 | async-start | bytes 1048576 | tf_op jit(solution)/shard_map/all_to_all | solution.py:256
  100.5 2.9 %collective-permute-start.3 = (bf16[800,256]{1,0:T(8,128)(2,1)S(1)}, bf16[800,256]{1,0:T(8,128)(2,1)S(1)}, u32[]{:S(2)}, u32[]{:S(2)}) collective-permute-start(bf16[800,256]{1,0:T(8,128)(2,1)S(1)} %get-tuple-element.32.own), channel_id=1, source_target_pairs={{0,576},{192,0},{384,192},{576,384},{1,577},{193,1},{385,193},{577... | collective-permute-start | bytes 1228808 | tf_op jit(solution)/shard_map/ppermute | solution.py:261
  103.4 2.9 %collective-permute-start.4 = (bf16[800,256]{1,0:T(8,128)(2,1)S(1)}, bf16[800,256]{1,0:T(8,128)(2,1)}, u32[]{:S(2)}, u32[]{:S(2)}) collective-permute-start(bf16[800,256]{1,0:T(8,128)(2,1)S(1)} %get-tuple-element.32.own), channel_id=1, source_target_pairs={{0,192},{192,384},{384,576},{576,0},{1,193},{193,385},{385,577},{5... | collective-permute-start | bytes 1228808 | tf_op jit(solution)/shard_map/ppermute | solution.py:261
  106.4 0.7 slice.6
  107.0 0.0 copy-done.1
  107.0 0.0 copy-done.3
  107.1 1.5 %shard_map.90 = (f32[512,1024]{1,0:T(8,128)}, f32[1,1,2,256,256]{4,3,2,1,0:T(8,128)}) custom-call(s32[4,32]{1,0:T(4,128)S(1)} %bitcast.8, bf16[800,256]{1,0:T(8,128)(2,1)S(1)} %get-tuple-element.32.own, f32[512,1024]{1,0:T(8,128)S(1)} %copy-done, f32[1,1,2,256,256]{4,3,2,1,0:T(8,128)S(1)} %copy-done.1), custom_call_target="tpu_custom_call" | custom-call | tf_op jit(solution)/shard_map/pallas_call | solution.py:244
  108.5 3.3 %collective-permute-start.5 = (bf16[400,256]{1,0:T(8,128)(2,1)}, bf16[400,256]{1,0:T(8,128)(2,1)}, u32[]{:S(2)}, u32[]{:S(2)}) collective-permute-start(bf16[400,256]{1,0:T(8,128)(2,1)} %slice.6), channel_id=1, source_target_pairs={{0,384},{192,576},{384,0},{576,192},{1,385},{193,577},{385,1},{577... | collective-permute-start | bytes 614408 | tf_op jit(solution)/shard_map/ppermute | solution.py:261
  111.8 2.1 %collective-permute-done.3.third = bf16[800,256]{1,0:T(8,128)(2,1)S(1)} collective-permute-done((bf16[800,256]{1,0:T(8,128)(2,1)S(1)}, bf16[800,256]{1,0:T(8,128)(2,1)S(1)}, u32[]{:S(2)}, u32[]{:S(2)}) %collective-permute-start.3) | collective-permute-done | bytes 409632 | tf_op jit(solution)/shard_map/ppermute | solution.py:261
  113.9 0.7 slice.7
  114.6 4.1 %collective-permute-start.6 = (bf16[400,256]{1,0:T(8,128)(2,1)}, bf16[400,256]{1,0:T(8,128)(2,1)}, u32[]{:S(2)}, u32[]{:S(2)}) collective-permute-start(bf16[400,256]{1,0:T(8,128)(2,1)} %slice.7), channel_id=1, source_target_pairs={{0,576},{192,0},{384,192},{576,384},{1,577},{193,1},{385,193},{577... | collective-permute-start | bytes 614408 | tf_op jit(solution)/shard_map/ppermute | solution.py:261
  118.7 0.0 all-to-all-done.4
  118.7 1.1 reduce_sum.12
  119.8 2.1 %collective-permute-start.7 = (bf16[64,256]{1,0:T(8,128)(2,1)S(1)}, bf16[64,256]{1,0:T(8,128)(2,1)S(1)}, u32[]{:S(2)}, u32[]{:S(2)}) collective-permute-start(bf16[64,256]{1,0:T(8,128)(2,1)S(1)} %reduce_sum.12), channel_id=1, source_target_pairs={{0,0},{1,1},{2,2},{3,3},{4,192},{5,193},{6,194},{7,195},{8,384},{9... | collective-permute-start | bytes 98312 | tf_op jit(solution)/shard_map/ppermute | solution.py:366
  122.0 0.0 collective-permute-done.5.top
  122.0 0.3 collective-permute-done.4.first
  122.2 1.0 collective-permute-done.6.low
  123.2 2.7 %shard_map.91 = (f32[512,1024]{1,0:T(8,128)}, f32[1,1,2,256,256]{4,3,2,1,0:T(8,128)}) custom-call(s32[4,32]{1,0:T(4,128)S(1)} %bitcast.9, bf16[800,256]{1,0:T(8,128)(2,1)S(1)} %collective-permute-done.3.third, bf16[800,256]{1,0:T(8,128)(2,1)} %collective-permute-done.4.first, ...), custom_call_target="tpu_custom_call", output_to_operand_aliasing={{0}: (7, {}), {1}: (8, {})} | custom-call | tf_op jit(solution)/shard_map/pallas_call | solution.py:244
  125.9 6.0 %collective-permute-done.7 = bf16[64,256]{1,0:T(8,128)(2,1)S(1)} collective-permute-done((bf16[64,256]{1,0:T(8,128)(2,1)S(1)}, bf16[64,256]{1,0:T(8,128)(2,1)S(1)}, u32[]{:S(2)}, u32[]{:S(2)}) %collective-permute-start.7) | collective-permute-done | bytes 32800 | tf_op jit(solution)/shard_map/ppermute | solution.py:366
  132.0 0.6 copy.14
Async XLA Ops:
  28.9 8.3 %copy-start.4 = (bf16[256,512]{1,0:T(8,128)(2,1)S(1)}, bf16[256,512]{1,0:T(8,128)(2,1)}, u32[]{:S(2)}) copy-start(bf16[256,512]{1,0:T(8,128)(2,1)} %own.1) | copy-start | bytes 786436
  29.8 58.3 %copy-start = (f32[512,1024]{1,0:T(8,128)S(1)}, f32[512,1024]{1,0:T(8,128)}, u32[]{:S(2)}) copy-start(f32[512,1024]{1,0:T(8,128)} %weight_in.5) | copy-start | bytes 6291460
  29.8 17.9 %all-to-all-start.1 = ((bf16[4,200,256]{2,1,0:T(8,128)(2,1)}), bf16[4,200,256]{2,1,0:T(8,128)(2,1)S(1)}, u32[]{:S(2)}, u32[]{:S(2)}) async-start(bf16[4,200,256]{2,1,0:T(8,128)(2,1)} %bitcast.1), calls=%async_computation.1 | async-start | bytes 819200 | tf_op jit(solution)/shard_map/all_to_all | solution.py:256
  37.2 8.4 %collective-permute-start = (bf16[256,512]{1,0:T(8,128)(2,1)S(1)}, bf16[256,512]{1,0:T(8,128)(2,1)}, u32[]{:S(2)}, u32[]{:S(2)}) collective-permute-start(bf16[256,512]{1,0:T(8,128)(2,1)S(1)} %copy-done.4), channel_id=1, source_target_pairs={{0,576},{192,0},{384,192},{576,384},{1,577},{193,1},{385,193},{577... | collective-permute-start | bytes 786440 | tf_op jit(solution)/shard_map/ppermute | solution.py:261
  48.5 23.4 %all-to-all-start.2 = ((bf16[3,200,256]{2,1,0:T(8,128)(2,1)}), bf16[3,200,256]{2,1,0:T(8,128)(2,1)S(1)}, u32[]{:S(2)}, u32[]{:S(2)}) async-start(bf16[3,200,256]{2,1,0:T(8,128)(2,1)} %shard_map.87), calls=%async_computation.2 | async-start | bytes 614400 | tf_op jit(solution)/shard_map/all_to_all | solution.py:256
  59.7 9.9 %collective-permute-start.1 = (bf16[256,512]{1,0:T(8,128)(2,1)S(1)}, bf16[256,512]{1,0:T(8,128)(2,1)}, u32[]{:S(2)}, u32[]{:S(2)}) collective-permute-start(bf16[256,512]{1,0:T(8,128)(2,1)S(1)} %copy-done.4), channel_id=1, source_target_pairs={{0,384},{192,576},{384,0},{576,192},{1,385},{193,577},{385,1},{577... | collective-permute-start | bytes 786440 | tf_op jit(solution)/shard_map/ppermute | solution.py:261
  72.7 15.4 %all-to-all-start.3 = ((bf16[4,200,256]{2,1,0:T(8,128)(2,1)}), bf16[4,200,256]{2,1,0:T(8,128)(2,1)S(1)}, u32[]{:S(2)}, u32[]{:S(2)}) async-start(bf16[4,200,256]{2,1,0:T(8,128)(2,1)} %shard_map.88), calls=%async_computation.3 | async-start | bytes 819200 | tf_op jit(solution)/shard_map/all_to_all | solution.py:256
  76.7 10.3 %collective-permute-start.2 = (bf16[256,512]{1,0:T(8,128)(2,1)S(1)}, bf16[256,512]{1,0:T(8,128)(2,1)S(1)}, u32[]{:S(2)}, u32[]{:S(2)}) collective-permute-start(bf16[256,512]{1,0:T(8,128)(2,1)S(1)} %copy-done.4), channel_id=1, source_target_pairs={{0,192},{192,384},{384,576},{576,0},{1,193},{193,385},{385,577},{5... | collective-permute-start | bytes 786440 | tf_op jit(solution)/shard_map/ppermute | solution.py:261
  87.0 1.2 copy-start.5
  88.2 18.9 %copy-start.1 = (f32[1,1,2,256,256]{4,3,2,1,0:T(8,128)S(1)}, f32[1,1,2,256,256]{4,3,2,1,0:T(8,128)}, u32[]{:S(2)}) copy-start(f32[1,1,2,256,256]{4,3,2,1,0:T(8,128)} %stats_in.5) | copy-start | bytes 1572868
  88.2 18.9 %copy-start.3 = (s32[32,4]{0,1:T(4,128)S(1)}, s32[32,4]{0,1:T(4,128)}, u32[]{:S(2)}) copy-start(s32[32,4]{0,1:T(4,128)} %param.10) | copy-start | bytes 1540
  92.5 0.8 copy-start.2
  93.3 25.4 %all-to-all-start.4 = ((bf16[16,64,256]{2,1,0:T(8,128)(2,1)}), bf16[16,64,256]{2,1,0:T(8,128)(2,1)}, u32[]{:S(2)}, u32[]{:S(2)}) async-start(bf16[16,64,256]{2,1,0:T(8,128)(2,1)} %bitcast.6), calls=%async_computation.4 | async-start | bytes 1048576 | tf_op jit(solution)/shard_map/all_to_all | solution.py:256
  100.5 13.4 %collective-permute-start.3 = (bf16[800,256]{1,0:T(8,128)(2,1)S(1)}, bf16[800,256]{1,0:T(8,128)(2,1)S(1)}, u32[]{:S(2)}, u32[]{:S(2)}) collective-permute-start(bf16[800,256]{1,0:T(8,128)(2,1)S(1)} %get-tuple-element.32.own), channel_id=1, source_target_pairs={{0,576},{192,0},{384,192},{576,384},{1,577},{193,1},{385,193},{577... | collective-permute-start | bytes 1228808 | tf_op jit(solution)/shard_map/ppermute | solution.py:261
  103.4 18.8 %collective-permute-start.4 = (bf16[800,256]{1,0:T(8,128)(2,1)S(1)}, bf16[800,256]{1,0:T(8,128)(2,1)}, u32[]{:S(2)}, u32[]{:S(2)}) collective-permute-start(bf16[800,256]{1,0:T(8,128)(2,1)S(1)} %get-tuple-element.32.own), channel_id=1, source_target_pairs={{0,192},{192,384},{384,576},{576,0},{1,193},{193,385},{385,577},{5... | collective-permute-start | bytes 1228808 | tf_op jit(solution)/shard_map/ppermute | solution.py:261
  108.5 13.4 %collective-permute-start.5 = (bf16[400,256]{1,0:T(8,128)(2,1)}, bf16[400,256]{1,0:T(8,128)(2,1)}, u32[]{:S(2)}, u32[]{:S(2)}) collective-permute-start(bf16[400,256]{1,0:T(8,128)(2,1)} %slice.6), channel_id=1, source_target_pairs={{0,384},{192,576},{384,0},{576,192},{1,385},{193,577},{385,1},{577... | collective-permute-start | bytes 614408 | tf_op jit(solution)/shard_map/ppermute | solution.py:261
  114.6 8.6 %collective-permute-start.6 = (bf16[400,256]{1,0:T(8,128)(2,1)}, bf16[400,256]{1,0:T(8,128)(2,1)}, u32[]{:S(2)}, u32[]{:S(2)}) collective-permute-start(bf16[400,256]{1,0:T(8,128)(2,1)} %slice.7), channel_id=1, source_target_pairs={{0,576},{192,0},{384,192},{576,384},{1,577},{193,1},{385,193},{577... | collective-permute-start | bytes 614408 | tf_op jit(solution)/shard_map/ppermute | solution.py:261
  119.8 12.1 %collective-permute-start.7 = (bf16[64,256]{1,0:T(8,128)(2,1)S(1)}, bf16[64,256]{1,0:T(8,128)(2,1)S(1)}, u32[]{:S(2)}, u32[]{:S(2)}) collective-permute-start(bf16[64,256]{1,0:T(8,128)(2,1)S(1)} %reduce_sum.12), channel_id=1, source_target_pairs={{0,0},{1,1},{2,2},{3,3},{4,192},{5,193},{6,194},{7,195},{8,384},{9... | collective-permute-start | bytes 98312 | tf_op jit(solution)/shard_map/ppermute | solution.py:366
